TPU v7x, 32 devices: a whole 2x2x4 slice. The times are simulated.
32 devices in a mesh: replica: 4 (over x, core), fsdp: 8 (over z, y).
Axes of the slice: x: 2, y: 2, z: 4, core: 2. Of those that a mesh axis runs over, the one named last changes fastest.
Arguments:
- tokens: bfloat16 [8192, 2048], P(('replica', 'fsdp')), may hold values from -6 to 6
- seq_lengths: int32 [32, 2], P(('replica', 'fsdp')), may hold values from 0 to 256, as said below
- attn_gain: bfloat16 [2048], P('fsdp'), may hold values from 0.099609375 to 1.8984375
- w_query: bfloat16 [2048, 2048], P('fsdp'), may hold values from -0.125 to 0.125
- w_key: bfloat16 [2048, 2048], P('fsdp'), may hold values from -0.125 to 0.125
- w_value: bfloat16 [2048, 2048], P('fsdp'), may hold values from -0.125 to 0.125
- w_outgate: bfloat16 [2048, 2048], P('fsdp'), may hold values from -0.125 to 0.125
- w_alpha: bfloat16 [2048, 16], P('fsdp'), may hold values from -0.125 to 0.125
- w_beta: bfloat16 [2048, 16], P('fsdp'), may hold values from -0.125 to 0.125
- conv_weight: bfloat16 [4, 6144], P(None, 'fsdp'), may hold values from -3 to 3
- decay_log: float32 [16], replicated, may hold values from -1.5 to 1.5
- decay_bias: float32 [16], replicated, may hold values from -7 to -2
- head_gain: float32 [128], replicated, may hold values from 0.1 to 1.9
- w_output: bfloat16 [2048, 2048], P('fsdp'), may hold values from -0.125 to 0.125
- mlp_gain: bfloat16 [2048], P('fsdp'), may hold values from 0.099609375 to 1.8984375
- w_gate: bfloat16 [2048, 5632], P('fsdp'), may hold values from -0.125 to 0.125
- w_up: bfloat16 [2048, 5632], P('fsdp'), may hold values from -0.125 to 0.125
- w_down: bfloat16 [5632, 2048], P('fsdp'), may hold values from -0.078125 to 0.078125
- cotangent: bfloat16 [8192, 2048], P(('replica', 'fsdp')), may hold values from -6 to 6
Outputs:
- output: bfloat16 [8192, 2048], P(('replica', 'fsdp'))
- grad_tokens: bfloat16 [8192, 2048], P(('replica', 'fsdp'))
- grad_attn_gain: float32 [2048], P('fsdp')
- grad_query: float32 [2048, 2048], P('fsdp')
- grad_key: float32 [2048, 2048], P('fsdp')
- grad_value: float32 [2048, 2048], P('fsdp')
- grad_outgate: float32 [2048, 2048], P('fsdp')
- grad_alpha: float32 [2048, 16], P('fsdp')
- grad_beta: float32 [2048, 16], P('fsdp')
- grad_conv: float32 [4, 6144], P(None, 'fsdp')
- grad_decay_log: float32 [16], replicated
- grad_decay_bias: float32 [16], replicated
- grad_head_gain: float32 [128], replicated
- grad_output_proj: float32 [2048, 2048], P('fsdp')
- grad_mlp_gain: float32 [2048], P('fsdp')
- grad_gate: float32 [2048, 5632], P('fsdp')
- grad_up: float32 [2048, 5632], P('fsdp')
- grad_down: float32 [5632, 2048], P('fsdp')
Inputs may be any that keep to these rules, and one draw needn't show every extreme that they name: `seq_lengths`: row r describes buffer r: its sequences are packed in order from row 0 of the buffer, the first of length 64 or more; every length is a multiple of 64 and a row sums to at most 256; rows after that sum are padding. In every draw some buffer holds one sequence of 256 rows and some other buffer is filled to 256.
All inputs are finite; a program needn't handle non-finite values.
Results may differ from a plain program's by a relative error of at most 0.019.
Values may be sent and summed in bfloat16 or wider, within the bound.
No kernel may reach another device: no remote copies, remote signals or barrier semaphores. Data moves between devices by JAX's collectives and lax.ppermute only.
A program may use at most 512 MiB of HBM per device.

v0:
```python
from functools import partial

import jax
import jax.numpy as jnp
from jax import lax
from jax.sharding import PartitionSpec as P

BLOCK = 64


EPS = 1e-06


def rms_scale(values, gain):
    return values * lax.rsqrt(jnp.mean(values * values, axis=-1, keepdims=True) + EPS) * gain


def rounded(values):
    return lax.optimization_barrier(values.astype(jnp.bfloat16)).astype(jnp.float32)


def rows_product(left, right):
    return lax.dot_general(
        left, right, (((0,), (0,)), ((), ())), preferred_element_type=jnp.float32
    )


def cols_product(left, right):
    return lax.dot_general(
        left, right, (((1,), (1,)), ((), ())), preferred_element_type=jnp.float32
    )


def plain_product(left, right):
    return jnp.dot(left, right, preferred_element_type=jnp.float32)


def segment_layout(lengths, cap_rows, block_rows):
    bounds = jnp.cumsum(lengths)
    places = jnp.arange(cap_rows, dtype=jnp.int32)
    below = bounds[None, :] <= places[:, None]
    seg_start = jnp.max(jnp.where(below, bounds[None, :], 0), axis=1)
    offset = places - seg_start
    live_rows = (places < bounds[-1]).astype(jnp.float32)
    firsts = jnp.arange(cap_rows // block_rows, dtype=jnp.int32) * block_rows
    begins = jnp.any(firsts[:, None] == bounds[None, :], axis=1) | (firsts == 0)
    return (offset, begins.astype(jnp.float32), live_rows)


def short_conv(pre_rows, taps, offset):
    summed = pre_rows * taps[0]
    for shift_by in range(1, taps.shape[0]):
        moved = jnp.concatenate(
            [jnp.zeros((shift_by, pre_rows.shape[1]), pre_rows.dtype), pre_rows[:-shift_by]], axis=0
        )
        summed = summed + jnp.where((offset >= shift_by)[:, None], moved, 0.0) * taps[shift_by]
    return jax.nn.silu(summed)


def unit_heads(values, head_count):
    pieces = values.reshape(values.shape[0], head_count, -1)
    return pieces * lax.rsqrt(jnp.sum(pieces * pieces, axis=-1, keepdims=True) + EPS)


def block_step(carried_state, inputs):
    query_rows_in, key_rows, value_rows, decay, beta, begins = inputs
    accurate_product = lax.Precision.HIGHEST
    carried_state = carried_state * (1.0 - begins)
    size = decay.shape[-1]
    running = jnp.cumsum(decay, axis=-1)
    places = jnp.arange(size)
    strict = places[:, None] > places[None, :]
    within = places[:, None] >= places[None, :]
    spread = running[:, :, None] - running[:, None, :]
    fall_strict = jnp.where(strict, jnp.exp(jnp.where(strict, spread, 0.0)), 0.0)
    fall_within = jnp.where(within, jnp.exp(jnp.where(within, spread, 0.0)), 0.0)
    keys_keys = jnp.einsum("hik,hjk->hij", key_rows, key_rows, precision=accurate_product)
    lower = beta[:, :, None] * fall_strict * keys_keys
    inverse = jnp.eye(size, dtype=lower.dtype) - lower
    power = lower
    reach = 2
    while reach < size:
        power = jnp.einsum("hij,hjk->hik", power, power, precision=accurate_product)
        inverse = inverse + jnp.einsum("hij,hjk->hik", inverse, power, precision=accurate_product)
        reach = reach * 2
    boost_factor = jnp.exp(running)
    corrected_weights = jnp.einsum(
        "hij,hjk->hik",
        inverse,
        (beta * boost_factor)[:, :, None] * key_rows,
        precision=accurate_product,
    )
    corrected_values = jnp.einsum(
        "hij,hjk->hik", inverse, beta[:, :, None] * value_rows, precision=accurate_product
    )
    update_term = corrected_values - jnp.einsum(
        "fla,fas->fls", corrected_weights, carried_state, precision=accurate_product
    )
    scores = (
        jnp.einsum("hik,hjk->hij", query_rows_in, key_rows, precision=accurate_product)
        * fall_within
    )
    outcome_value = jnp.einsum(
        "fla,fas->fls",
        query_rows_in * boost_factor[:, :, None],
        carried_state,
        precision=accurate_product,
    )
    outcome_value = outcome_value + jnp.einsum(
        "hij,hjv->hiv", scores, update_term, precision=accurate_product
    )
    final_cumulative = running[:, -1]
    decayed_state = key_rows * jnp.exp(final_cumulative[:, None] - running)[:, :, None]
    updated_state = jnp.exp(final_cumulative)[:, None, None] * carried_state + jnp.einsum(
        "zad,zar->zdr", decayed_state, update_term, precision=accurate_product
    )
    return (updated_state, outcome_value)


def to_blocks(values, block_count):
    shaped = values.reshape((block_count, values.shape[0] // block_count) + values.shape[1:])
    return jnp.swapaxes(shaped, 1, 2)


def delta_rule(query_rows_in, key_rows, value_rows, decay, beta, block_starts):
    block_count = block_starts.shape[0]
    length, head_count, head_size = query_rows_in.shape
    initial = jnp.zeros((head_count, head_size, value_rows.shape[2]), jnp.float32)
    scanned = (
        to_blocks(query_rows_in, block_count),
        to_blocks(key_rows, block_count),
        to_blocks(value_rows, block_count),
        to_blocks(decay, block_count),
        to_blocks(beta, block_count),
        block_starts,
    )
    final_state, results = lax.scan(jax.checkpoint(block_step), initial, scanned)
    return jnp.swapaxes(results, 1, 2).reshape(length, head_count, value_rows.shape[2])


def mixer_inputs(query_pre, key_pre, value_pre, conv_f, offset, head_count):
    width = query_pre.shape[1]
    head_size = width // head_count
    conv_q = short_conv(query_pre, conv_f[:, :width], offset)
    conv_k = short_conv(key_pre, conv_f[:, width : 2 * width], offset)
    conv_v = short_conv(value_pre, conv_f[:, 2 * width :], offset)
    query_rows_in = unit_heads(conv_q, head_count) * head_size ** (-0.5)
    key_rows = unit_heads(conv_k, head_count)
    value_rows = conv_v.reshape(query_pre.shape[0], head_count, head_size)
    return (query_rows_in, key_rows, value_rows)


def mixer_core(
    query_rows_in,
    key_rows,
    value_rows,
    gate_pre,
    alpha_pre,
    beta_pre,
    decay_log,
    decay_bias,
    head_gain,
    block_starts,
):
    decay = -jnp.exp(decay_log) * jax.nn.softplus(alpha_pre + decay_bias)
    beta = jax.nn.sigmoid(beta_pre)
    mixed = delta_rule(query_rows_in, key_rows, value_rows, decay, beta, block_starts)
    normed = mixed * lax.rsqrt(jnp.mean(mixed * mixed, axis=-1, keepdims=True) + EPS) * head_gain
    gated = normed * jax.nn.silu(gate_pre.reshape(mixed.shape))
    return gated.reshape(gate_pre.shape)


def swiglu(gate_rows, up_rows):
    return jax.nn.silu(gate_rows) * up_rows


def on_device(
    tokens,
    seq_lengths,
    attn_gain,
    w_query,
    w_key,
    w_value,
    w_outgate,
    w_alpha,
    w_beta,
    conv_weight,
    decay_log,
    decay_bias,
    head_gain,
    w_output,
    mlp_gain,
    w_gate,
    w_up,
    w_down,
    cotangent,
):
    head_count = decay_log.shape[0]
    offset, block_starts, live_rows = segment_layout(seq_lengths[0], tokens.shape[0], BLOCK)
    (
        gain_one,
        full_query,
        full_key,
        full_value,
        full_outgate,
        full_alpha,
        full_beta,
        full_conv,
        full_output,
    ) = (
        lax.all_gather(attn_gain, "fsdp", axis=0, tiled=True),
        lax.all_gather(w_query, "fsdp", axis=0, tiled=True),
        lax.all_gather(w_key, "fsdp", axis=0, tiled=True),
        lax.all_gather(w_value, "fsdp", axis=0, tiled=True),
        lax.all_gather(w_outgate, "fsdp", axis=0, tiled=True),
        lax.all_gather(w_alpha, "fsdp", axis=0, tiled=True),
        lax.all_gather(w_beta, "fsdp", axis=0, tiled=True),
        lax.all_gather(conv_weight, "fsdp", axis=1, tiled=True),
        lax.all_gather(w_output, "fsdp", axis=0, tiled=True),
    )
    tokens_f = tokens.astype(jnp.float32)
    normed, norm_back = jax.vjp(rms_scale, tokens_f, gain_one.astype(jnp.float32))
    normed_b = normed.astype(jnp.bfloat16)
    query_pre = plain_product(normed_b, full_query)
    key_pre = plain_product(normed_b, full_key)
    value_pre = plain_product(normed_b, full_value)
    gate_pre = plain_product(normed_b, full_outgate)
    alpha_pre = plain_product(normed_b, full_alpha)
    beta_pre = plain_product(normed_b, full_beta)
    inputs_fn = partial(mixer_inputs, offset=offset, head_count=head_count)
    (query_rows_in, key_rows, value_rows), inputs_back = jax.vjp(
        inputs_fn, query_pre, key_pre, value_pre, full_conv.astype(jnp.float32)
    )
    core_fn = partial(mixer_core, block_starts=block_starts)
    gated, core_back = jax.vjp(
        core_fn,
        rounded(query_rows_in),
        rounded(key_rows),
        rounded(value_rows),
        gate_pre,
        alpha_pre,
        beta_pre,
        decay_log,
        decay_bias,
        head_gain,
    )
    gated_b = gated.astype(jnp.bfloat16)
    resid = tokens_f + plain_product(gated_b, full_output)
    gain_two, full_gate, full_up, full_down = (
        lax.all_gather(mlp_gain, "fsdp", axis=0, tiled=True),
        lax.all_gather(w_gate, "fsdp", axis=0, tiled=True),
        lax.all_gather(w_up, "fsdp", axis=0, tiled=True),
        lax.all_gather(w_down, "fsdp", axis=0, tiled=True),
    )
    normed_two, norm_two_back = jax.vjp(rms_scale, resid, gain_two.astype(jnp.float32))
    normed_two_b = normed_two.astype(jnp.bfloat16)
    gate_rows = plain_product(normed_two_b, full_gate)
    up_rows = plain_product(normed_two_b, full_up)
    hidden, swiglu_back = jax.vjp(swiglu, gate_rows, up_rows)
    hidden_b = hidden.astype(jnp.bfloat16)
    output = ((resid + plain_product(hidden_b, full_down)) * live_rows[:, None]).astype(
        jnp.bfloat16
    )
    full_gate, full_up, full_down = (
        lax.all_gather(w_gate, "fsdp", axis=0, tiled=True),
        lax.all_gather(w_up, "fsdp", axis=0, tiled=True),
        lax.all_gather(w_down, "fsdp", axis=0, tiled=True),
    )
    upstream = cotangent.astype(jnp.float32) * live_rows[:, None]
    upstream_b = upstream.astype(jnp.bfloat16)
    grad_w_down = rows_product(hidden_b, upstream_b)
    grad_hidden = cols_product(upstream_b, full_down)
    grad_gate_rows, grad_up_rows = swiglu_back(grad_hidden)
    gate_grad_b = grad_gate_rows.astype(jnp.bfloat16)
    up_grad_b = grad_up_rows.astype(jnp.bfloat16)
    grad_w_gate = rows_product(normed_two_b, gate_grad_b)
    grad_w_up = rows_product(normed_two_b, up_grad_b)
    grad_normed_two = cols_product(gate_grad_b, full_gate) + cols_product(up_grad_b, full_up)
    grad_resid_norm, grad_mlp_gain = norm_two_back(grad_normed_two)
    grad_resid = upstream + grad_resid_norm
    share_mlp_gain, share_gate, share_up, share_down = (
        lax.psum_scatter(
            grad_mlp_gain.astype(jnp.bfloat16), "fsdp", scatter_dimension=0, tiled=True
        ).astype(jnp.float32),
        lax.psum_scatter(
            grad_w_gate.astype(jnp.bfloat16), "fsdp", scatter_dimension=0, tiled=True
        ).astype(jnp.float32),
        lax.psum_scatter(
            grad_w_up.astype(jnp.bfloat16), "fsdp", scatter_dimension=0, tiled=True
        ).astype(jnp.float32),
        lax.psum_scatter(
            grad_w_down.astype(jnp.bfloat16), "fsdp", scatter_dimension=0, tiled=True
        ).astype(jnp.float32),
    )
    full_query, full_key, full_value, full_outgate, full_alpha, full_beta, full_output = (
        lax.all_gather(w_query, "fsdp", axis=0, tiled=True),
        lax.all_gather(w_key, "fsdp", axis=0, tiled=True),
        lax.all_gather(w_value, "fsdp", axis=0, tiled=True),
        lax.all_gather(w_outgate, "fsdp", axis=0, tiled=True),
        lax.all_gather(w_alpha, "fsdp", axis=0, tiled=True),
        lax.all_gather(w_beta, "fsdp", axis=0, tiled=True),
        lax.all_gather(w_output, "fsdp", axis=0, tiled=True),
    )
    branch_b = grad_resid.astype(jnp.bfloat16)
    grad_w_output = rows_product(gated_b, branch_b)
    grad_gated = cols_product(branch_b, full_output)
    (
        grad_query_rows,
        grad_key_rows,
        grad_value_rows,
        grad_gate_pre,
        grad_alpha_pre,
        grad_beta_pre,
        grad_decay_log,
        grad_decay_bias,
        grad_head_gain,
    ) = core_back(grad_gated)
    grad_query_pre, grad_key_pre, grad_value_pre, grad_conv_f = inputs_back(
        (rounded(grad_query_rows), rounded(grad_key_rows), rounded(grad_value_rows))
    )
    query_grad_b = grad_query_pre.astype(jnp.bfloat16)
    key_grad_b = grad_key_pre.astype(jnp.bfloat16)
    value_grad_b = grad_value_pre.astype(jnp.bfloat16)
    outgate_grad_b = grad_gate_pre.astype(jnp.bfloat16)
    alpha_grad_b = grad_alpha_pre.astype(jnp.bfloat16)
    beta_grad_b = grad_beta_pre.astype(jnp.bfloat16)
    grad_w_query = rows_product(normed_b, query_grad_b)
    grad_w_key = rows_product(normed_b, key_grad_b)
    grad_w_value = rows_product(normed_b, value_grad_b)
    grad_w_outgate = rows_product(normed_b, outgate_grad_b)
    grad_w_alpha = rows_product(normed_b, alpha_grad_b)
    grad_w_beta = rows_product(normed_b, beta_grad_b)
    grad_normed = cols_product(query_grad_b, full_query) + cols_product(key_grad_b, full_key)
    grad_normed = (
        grad_normed
        + cols_product(value_grad_b, full_value)
        + cols_product(outgate_grad_b, full_outgate)
    )
    grad_normed = (
        grad_normed + cols_product(alpha_grad_b, full_alpha) + cols_product(beta_grad_b, full_beta)
    )
    grad_tokens_norm, grad_attn_gain = norm_back(grad_normed)
    grad_tokens = (grad_resid + grad_tokens_norm).astype(jnp.bfloat16)
    sum_decay_log, sum_decay_bias, sum_head_gain = lax.psum(
        (grad_decay_log, grad_decay_bias, grad_head_gain), ("replica", "fsdp")
    )
    (
        share_attn_gain,
        share_query,
        share_key,
        share_value,
        share_outgate,
        share_alpha,
        share_beta,
        share_conv,
        share_output,
    ) = (
        lax.psum_scatter(
            grad_attn_gain.astype(jnp.bfloat16), "fsdp", scatter_dimension=0, tiled=True
        ).astype(jnp.float32),
        lax.psum_scatter(
            grad_w_query.astype(jnp.bfloat16), "fsdp", scatter_dimension=0, tiled=True
        ).astype(jnp.float32),
        lax.psum_scatter(
            grad_w_key.astype(jnp.bfloat16), "fsdp", scatter_dimension=0, tiled=True
        ).astype(jnp.float32),
        lax.psum_scatter(
            grad_w_value.astype(jnp.bfloat16), "fsdp", scatter_dimension=0, tiled=True
        ).astype(jnp.float32),
        lax.psum_scatter(
            grad_w_outgate.astype(jnp.bfloat16), "fsdp", scatter_dimension=0, tiled=True
        ).astype(jnp.float32),
        lax.psum_scatter(
            grad_w_alpha.astype(jnp.bfloat16), "fsdp", scatter_dimension=0, tiled=True
        ).astype(jnp.float32),
        lax.psum_scatter(
            grad_w_beta.astype(jnp.bfloat16), "fsdp", scatter_dimension=0, tiled=True
        ).astype(jnp.float32),
        lax.psum_scatter(
            grad_conv_f.astype(jnp.bfloat16), "fsdp", scatter_dimension=1, tiled=True
        ).astype(jnp.float32),
        lax.psum_scatter(
            grad_w_output.astype(jnp.bfloat16), "fsdp", scatter_dimension=0, tiled=True
        ).astype(jnp.float32),
    )
    (
        share_mlp_gain,
        share_gate,
        share_up,
        share_down,
        share_attn_gain,
        share_query,
        share_key,
        share_value,
        share_outgate,
        share_alpha,
        share_beta,
        share_conv,
        share_output,
    ) = (
        lax.psum(share_mlp_gain.astype(jnp.bfloat16), "replica").astype(jnp.float32),
        lax.psum(share_gate.astype(jnp.bfloat16), "replica").astype(jnp.float32),
        lax.psum(share_up.astype(jnp.bfloat16), "replica").astype(jnp.float32),
        lax.psum(share_down.astype(jnp.bfloat16), "replica").astype(jnp.float32),
        lax.psum(share_attn_gain.astype(jnp.bfloat16), "replica").astype(jnp.float32),
        lax.psum(share_query.astype(jnp.bfloat16), "replica").astype(jnp.float32),
        lax.psum(share_key.astype(jnp.bfloat16), "replica").astype(jnp.float32),
        lax.psum(share_value.astype(jnp.bfloat16), "replica").astype(jnp.float32),
        lax.psum(share_outgate.astype(jnp.bfloat16), "replica").astype(jnp.float32),
        lax.psum(share_alpha.astype(jnp.bfloat16), "replica").astype(jnp.float32),
        lax.psum(share_beta.astype(jnp.bfloat16), "replica").astype(jnp.float32),
        lax.psum(share_conv.astype(jnp.bfloat16), "replica").astype(jnp.float32),
        lax.psum(share_output.astype(jnp.bfloat16), "replica").astype(jnp.float32),
    )
    return (
        output,
        grad_tokens,
        share_attn_gain,
        share_query,
        share_key,
        share_value,
        share_outgate,
        share_alpha,
        share_beta,
        share_conv,
        sum_decay_log,
        sum_decay_bias,
        sum_head_gain,
        share_output,
        share_mlp_gain,
        share_gate,
        share_up,
        share_down,
    )


def solution(mesh):
    placed = (
        P(("replica", "fsdp"), None),
        P(("replica", "fsdp"), None),
        P("fsdp"),
        P("fsdp", None),
        P("fsdp", None),
        P("fsdp", None),
        P("fsdp", None),
        P("fsdp", None),
        P("fsdp", None),
        P(None, "fsdp"),
        P(),
        P(),
        P(),
        P("fsdp", None),
        P("fsdp"),
        P("fsdp", None),
        P("fsdp", None),
        P("fsdp", None),
        P(("replica", "fsdp"), None),
    )
    return jax.shard_map(
        on_device,
        mesh=mesh,
        in_specs=placed,
        out_specs=(
            P(("replica", "fsdp"), None),
            P(("replica", "fsdp"), None),
            P("fsdp"),
            P("fsdp", None),
            P("fsdp", None),
            P("fsdp", None),
            P("fsdp", None),
            P("fsdp", None),
            P("fsdp", None),
            P(None, "fsdp"),
            P(),
            P(),
            P(),
            P("fsdp", None),
            P("fsdp"),
            P("fsdp", None),
            P("fsdp", None),
            P("fsdp", None),
        ),
        check_vma=False,
    )
```

profile of v0, /device:TPU:1, one launch (start us, length us, event | category | flops | bytes accessed | tf_op | source)
XLA Modules:
  0.0 4662.7 jit_solution(16775975001139149426)
XLA Ops:
  12.8 18.1 all-gather
  31.2 24.7 all_gather.50
  57.5 24.6 all_gather.53
  82.7 13.3 all-gather.1
  99.4 24.8 all_gather.52
  125.3 13.5 all-gather.15.cloned.1.call-done
  138.8 6.1 fusion.210
  144.9 119.5 %all-gather.13.cloned.1.call-done = bf16[2048,2048]{1,0:T(8,128)(2,1)} async-done(((bf16[256,2048]{1,0:T(8,128)(2,1)}), bf16[2048,2048]{1,0:T(8,128)(2,1)}) %all-gather.13.cloned.1.call-update) | async-done | bytes 8388624 | tf_op jit(solution)/shard_map/all_gather | solution.py:214
  264.4 6.1 fusion.212
  270.6 6.2 multiply_bitcast_fusion.1
  281.0 108.7 %all-gather.11.cloned.1.call-done = bf16[2048,2048]{1,0:T(8,128)(2,1)} async-done(((bf16[256,2048]{1,0:T(8,128)(2,1)}), bf16[2048,2048]{1,0:T(8,128)(2,1)}) %all-gather.11.cloned.1.call-update) | async-done | bytes 8388624 | tf_op jit(solution)/shard_map/all_gather | solution.py:213
  389.7 5.8 fusion.215
  405.5 98.2 %while.44 = (s32[]{:T(128)}, f32[16,128,128]{2,1,0:T(8,128)S(1)}, f32[4,16,64,128]{3,2,1,0:T(8,128)}, f32[4,16,128,128]{3,2,1,0:T(8,128)}, f32[4,16,64]{2,1,0:T(...) while((s32[]{:T(128)}, f32[16,128,128]{2,1,0:T(8,128)S(1)}, ...), condition=%wide.region_8.9_spmd.clone.clone, body=%wide.region_6.8_spmd.clone.clone.sunk | while | flops 1614816256 | bytes 31614508 | solution.py:137
  506.1 4.2 copy.391
  510.2 4.5 all-gather.17.cloned.1.call-done
  516.4 7.1 multiply_convert_fusion.3
  526.5 113.4 %all-gather.19.cloned.1.call-done = bf16[2048,2048]{1,0:T(8,128)(2,1)} async-done(((bf16[256,2048]{1,0:T(8,128)(2,1)}), bf16[2048,2048]{1,0:T(8,128)(2,1)}) %all-gather.19.cloned.1.call-update) | async-done | bytes 8388624 | tf_op jit(solution)/shard_map/all_gather | solution.py:219
  639.9 5.8 multiply_reduce_fusion.22
  647.4 433.6 %all-gather.21.cloned.1.call-done = bf16[2048,5632]{1,0:T(8,128)(2,1)} async-done(((bf16[256,5632]{1,0:T(8,128)(2,1)}), bf16[2048,5632]{1,0:T(8,128)(2,1)}) %all-gather.21.cloned.1.call-update) | async-done | bytes 23068688 | tf_op jit(solution)/shard_map/all_gather | solution.py:251
  1081.0 13.2 fusion.244
  1094.2 429.4 %all-gather.23.cloned.1.call-done = bf16[2048,5632]{1,0:T(8,128)(2,1)} async-done(((bf16[256,5632]{1,0:T(8,128)(2,1)}), bf16[2048,5632]{1,0:T(8,128)(2,1)}) %all-gather.23.cloned.1.call-update) | async-done | bytes 23068688 | tf_op jit(solution)/shard_map/all_gather | solution.py:252
  1523.7 13.4 fusion.245
  1537.1 429.2 %all-gather.25.cloned.1.call-done = bf16[5632,2048]{1,0:T(8,128)(2,1)} async-done(((bf16[704,2048]{1,0:T(8,128)(2,1)}), bf16[5632,2048]{1,0:T(8,128)(2,1)}) %all-gather.25.cloned.1.call-update) | async-done | bytes 23068688 | tf_op jit(solution)/shard_map/all_gather | solution.py:253
  1966.3 25.8 multiply_convert_fusion
  1992.1 12.7 fusion.246
  2004.8 14.1 multiply_reduce_fusion.6
  2022.0 5.6 convolution_convert_fusion.3
  2027.6 10.0 fusion.161
  2049.2 380.2 %while.43 = (s32[]{:T(128)}, f32[16,128,128]{2,1,0:T(8,128)}, bf16[4,16,64,128]{3,1,2,0:T(8,128)(2,1)}, bf16[4,16,64,128]{3,1,2,0:T(8,128)(2,1)}, bf16[4,16,64,1...) while((s32[]{:T(128)}, f32[16,128,128]{2,1,0:T(8,128)}, ...), condition=%wide.region_25.26_spmd.clone, body=%wide.region_13.25_spmd.clone.sunk | while | flops 4341325824 | bytes 132221200 | solution.py:137
  2127.5 4.0 multiply_reduce_fusion.32
  2221.8 4.0 multiply_reduce_fusion.32
  2315.6 4.0 multiply_reduce_fusion.32
  2409.7 4.0 multiply_reduce_fusion.32
  2441.4 13.6 multiply_reduce_fusion.11
  2455.1 5.4 fusion.169
  2468.5 5.8 convolution_convert_fusion.5
  2475.0 4.4 add_convert_fusion.1
  2480.3 5.8 convolution_convert_fusion.6
  2486.8 3.8 add_convert_fusion.2
  2491.6 5.8 convolution_convert_fusion.7
  2498.7 5.7 convolution_convert_fusion.4
  2505.7 13.1 convolution_convert_fusion.2
  2518.8 13.0 convolution_convert_fusion.1
  2533.0 13.1 convolution_convert_fusion
  2553.0 39.8 all-reduce.36
  2592.8 31.0 reduce-scatter.18.cloned.1.call-done
  2623.9 151.7 %reduce-scatter.16.cloned.1.call-done = bf16[256,2048]{1,0:T(8,128)(2,1)} async-done(((bf16[2048,2048]{1,0:T(8,128)(2,1)}), bf16[256,2048]{1,0:T(8,128)(2,1)}) %reduce-scatter.16.cloned.1.call-update) | async-done | bytes 1048592 | tf_op jit(solution)/shard_map/reduce_scatter | solution.py:364
  2775.6 152.0 %reduce-scatter.14.cloned.1.call-done = bf16[256,2048]{1,0:T(8,128)(2,1)} async-done(((bf16[2048,2048]{1,0:T(8,128)(2,1)}), bf16[256,2048]{1,0:T(8,128)(2,1)}) %reduce-scatter.14.cloned.1.call-update) | async-done | bytes 1048592 | tf_op jit(solution)/shard_map/reduce_scatter | solution.py:361
  2927.5 151.7 %reduce-scatter.20.cloned.1.call-done = bf16[256,2048]{1,0:T(8,128)(2,1)} async-done(((bf16[2048,2048]{1,0:T(8,128)(2,1)}), bf16[256,2048]{1,0:T(8,128)(2,1)}) %reduce-scatter.20.cloned.1.call-update) | async-done | bytes 1048592 | tf_op jit(solution)/shard_map/reduce_scatter | solution.py:370
  3079.2 376.7 %reduce-scatter.28.cloned.1.call-done = bf16[256,5632]{1,0:T(8,128)(2,1)} async-done(((bf16[2048,5632]{1,0:T(8,128)(2,1)}), bf16[256,5632]{1,0:T(8,128)(2,1)}) %reduce-scatter.28.cloned.1.call-update) | async-done | bytes 2883600 | tf_op jit(solution)/shard_map/reduce_scatter | solution.py:285
  3456.0 376.4 %reduce-scatter.30.cloned.1.call-done = bf16[256,5632]{1,0:T(8,128)(2,1)} async-done(((bf16[2048,5632]{1,0:T(8,128)(2,1)}), bf16[256,5632]{1,0:T(8,128)(2,1)}) %reduce-scatter.30.cloned.1.call-update) | async-done | bytes 2883600 | tf_op jit(solution)/shard_map/reduce_scatter | solution.py:288
  3832.3 376.4 %reduce-scatter.32.cloned.1.call-done = bf16[704,2048]{1,0:T(8,128)(2,1)} async-done(((bf16[5632,2048]{1,0:T(8,128)(2,1)}), bf16[704,2048]{1,0:T(8,128)(2,1)}) %reduce-scatter.32.cloned.1.call-update) | async-done | bytes 2883600 | tf_op jit(solution)/shard_map/reduce_scatter | solution.py:291
  4210.0 7.2 fusion.247
  4217.2 6.6 convolution_add_fusion.40
  4223.9 3.7 convolution_add_fusion.39
  4227.6 4.0 convolution_add_fusion.38
  4234.5 16.3 all-reduce.37
  4254.4 12.0 fusion.143
  4266.4 9.7 reduce-scatter.34.cloned.1.call-done
  4277.1 54.1 %reduce-scatter.22.cloned.1.call-done = bf16[256,16]{0,1:T(8,128)(2,1)} async-done(((bf16[2048,16]{0,1:T(8,128)(2,1)}), bf16[256,16]{0,1:T(8,128)(2,1)}) %reduce-scatter.22.cloned.1.call-update) | async-done | bytes 8208 | tf_op jit(solution)/shard_map/reduce_scatter | solution.py:373
  4331.2 56.4 %reduce-scatter.24.cloned.1.call-done = bf16[256,16]{0,1:T(8,128)(2,1)} async-done(((bf16[2048,16]{0,1:T(8,128)(2,1)}), bf16[256,16]{0,1:T(8,128)(2,1)}) %reduce-scatter.24.cloned.1.call-update) | async-done | bytes 8208 | tf_op jit(solution)/shard_map/reduce_scatter | solution.py:376
  4387.6 13.8 all-reduce.38
  4404.3 231.9 %all-reduce.42.cloned.1.call-done = (bf16[256,2048]{1,0:T(8,128)(2,1)}, bf16[256,2048]{1,0:T(8,128)(2,1)}, bf16[256,2048]{1,0:T(8,128)(2,1)}, bf16[256,2048]{1,0...) async-done(((bf16[256,2048]{1,0:T(8,128)(2,1)}, bf16[256,2048]{1,0:T(8,128)(2,1)}, ...) | async-done | bytes 13893648 | tf_op jit(solution)/shard_map/psum | solution.py:406
  4636.2 5.2 convert_element_type.309
  (1201 shorter events, 550.6 us)
Async XLA Ops:
  7.2 131.6 %all-gather.15.cloned.1.call-start = ((), (), s32[]{:S(2)}) async-start(), calls=%async_computation.13 | async-start | bytes 9437184 | tf_op jit(solution)/shard_map/all_gather | solution.py:212
  7.9 256.4 %all-gather.13.cloned.1.call-start = ((), (), s32[]{:S(2)}) async-start(), calls=%async_computation.12 | async-start | bytes 9437184 | tf_op jit(solution)/shard_map/all_gather | solution.py:214
  8.7 381.0 %all-gather.11.cloned.1.call-start = ((), (), s32[]{:S(2)}) async-start(), calls=%async_computation.11 | async-start | bytes 9437184 | tf_op jit(solution)/shard_map/all_gather | solution.py:213
  9.4 505.4 %all-gather.17.cloned.1.call-start = ((), (), s32[]{:S(2)}) async-start(), calls=%async_computation.14 | async-start | bytes 9437184 | tf_op jit(solution)/shard_map/all_gather | solution.py:215
  10.0 629.9 %all-gather.19.cloned.1.call-start = ((), (), s32[]{:S(2)}) async-start(), calls=%async_computation.15 | async-start | bytes 9437184 | tf_op jit(solution)/shard_map/all_gather | solution.py:219
  10.6 1070.4 %all-gather.21.cloned.1.call-start = ((), (), s32[]{:S(2)}) async-start(), calls=%async_computation.16 | async-start | bytes 25952256 | tf_op jit(solution)/shard_map/all_gather | solution.py:251
  11.1 1512.5 %all-gather.23.cloned.1.call-start = ((), (), s32[]{:S(2)}) async-start(), calls=%async_computation.17 | async-start | bytes 25952256 | tf_op jit(solution)/shard_map/all_gather | solution.py:252
  11.9 19.1 copy-start.157
  11.9 19.2 copy-start.142
  11.9 44.0 copy-start.39
  11.9 44.2 copy-start.160
  12.0 44.3 copy-start.158
  12.0 1954.4 %all-gather.25.cloned.1.call-start = ((), (), s32[]{:S(2)}) async-start(), calls=%async_computation.18 | async-start | bytes 25952256 | tf_op jit(solution)/shard_map/all_gather | solution.py:253
  12.7 44.7 copy-start.143
  12.7 2580.1 %reduce-scatter.26.cloned.1.call-start = ((), (), s32[]{:S(2)}) async-start(), calls=%async_computation.25 | async-start | bytes 9437184 | tf_op jit(solution)/shard_map/reduce_scatter | solution.py:382
  31.0 484.4 %copy-start.82 = (f32[8,1,256]{2,1,0:T(1,128)}, f32[8,1,256]{2,1,0:T(1,128)S(1)}, u32[]{:S(2)}) copy-start(f32[8,1,256]{2,1,0:T(1,128)S(1)} %convert_element_type.314) | copy-start | bytes 24580
  55.9 26.7 copy-start.100
  56.2 26.5 copy-start.159
  56.2 26.4 copy-start.150
  56.2 459.2 %copy-start.105 = (f32[256]{0:T(256)}, f32[256]{0:T(256)S(1)}, u32[]{:S(2)}) copy-start(f32[256]{0:T(256)S(1)} %fusion.197) | copy-start | bytes 3076
  56.3 43.1 copy-start.144
  56.3 68.8 %copy-start.145 = (f32[128]{0:T(128)S(1)}, f32[128]{0:T(128)}, u32[]{:S(2)}) copy-start(f32[128]{0:T(128)} %param.35) | copy-start | bytes 1540
  82.1 43.1 copy-start.102
  82.6 42.5 copy-start.131
  97.5 298.0 %copy-start.136 = (pred[256]{0:T(512)(128)(4,1)}, pred[256]{0:T(512)(128)(4,1)S(1)}, u32[]{:S(2)}) copy-start(pred[256]{0:T(512)(128)(4,1)S(1)} %get-tuple-element.922) | copy-start | bytes 772
  97.5 298.0 %copy-start.138 = (pred[256]{0:T(512)(128)(4,1)}, pred[256]{0:T(512)(128)(4,1)S(1)}, u32[]{:S(2)}) copy-start(pred[256]{0:T(512)(128)(4,1)S(1)} %get-tuple-element.923) | copy-start | bytes 772
  97.5 298.0 %copy-start.140 = (pred[256]{0:T(512)(128)(4,1)}, pred[256]{0:T(512)(128)(4,1)S(1)}, u32[]{:S(2)}) copy-start(pred[256]{0:T(512)(128)(4,1)S(1)} %get-tuple-element.924) | copy-start | bytes 772
  124.9 1894.1 %copy-start.147 = (f32[256]{0:T(256)}, f32[256]{0:T(256)S(1)}, u32[]{:S(2)}) copy-start(f32[256]{0:T(256)S(1)} %compare_convert_fusion) | copy-start | bytes 3076
  125.2 145.3 %copy-start.107 = (f32[1,2048]{1,0:T(1,128)}, f32[1,2048]{1,0:T(1,128)S(1)}, u32[]{:S(2)}) copy-start(f32[1,2048]{1,0:T(1,128)S(1)} %get-tuple-element.907) | copy-start | bytes 24580
  125.2 145.3 %copy-start.111 = (f32[1,2048]{1,0:T(1,128)}, f32[1,2048]{1,0:T(1,128)S(1)}, u32[]{:S(2)}) copy-start(f32[1,2048]{1,0:T(1,128)S(1)} %get-tuple-element.911) | copy-start | bytes 24580
  125.2 145.3 %copy-start.113 = (f32[1,2048]{1,0:T(1,128)}, f32[1,2048]{1,0:T(1,128)S(1)}, u32[]{:S(2)}) copy-start(f32[1,2048]{1,0:T(1,128)S(1)} %get-tuple-element.908) | copy-start | bytes 24580
  125.2 145.3 %copy-start.115 = (f32[1,2048]{1,0:T(1,128)}, f32[1,2048]{1,0:T(1,128)S(1)}, u32[]{:S(2)}) copy-start(f32[1,2048]{1,0:T(1,128)S(1)} %get-tuple-element.912) | copy-start | bytes 24580
  125.3 145.3 %copy-start.119 = (f32[1,2048]{1,0:T(1,128)}, f32[1,2048]{1,0:T(1,128)S(1)}, u32[]{:S(2)}) copy-start(f32[1,2048]{1,0:T(1,128)S(1)} %get-tuple-element.909) | copy-start | bytes 24580
  125.3 145.3 %copy-start.121 = (f32[1,2048]{1,0:T(1,128)}, f32[1,2048]{1,0:T(1,128)S(1)}, u32[]{:S(2)}) copy-start(f32[1,2048]{1,0:T(1,128)S(1)} %get-tuple-element.913) | copy-start | bytes 24580
  125.3 145.3 %copy-start.125 = (f32[1,2048]{1,0:T(1,128)}, f32[1,2048]{1,0:T(1,128)S(1)}, u32[]{:S(2)}) copy-start(f32[1,2048]{1,0:T(1,128)S(1)} %get-tuple-element.910) | copy-start | bytes 24580
  125.3 145.3 %copy-start.127 = (f32[1,2048]{1,0:T(1,128)}, f32[1,2048]{1,0:T(1,128)S(1)}, u32[]{:S(2)}) copy-start(f32[1,2048]{1,0:T(1,128)S(1)} %get-tuple-element.914) | copy-start | bytes 24580
  125.3 270.2 %copy-start.109 = (f32[1,2048]{1,0:T(1,128)}, f32[1,2048]{1,0:T(1,128)S(1)}, u32[]{:S(2)}) copy-start(f32[1,2048]{1,0:T(1,128)S(1)} %get-tuple-element.915) | copy-start | bytes 24580
  125.3 270.2 %copy-start.117 = (f32[1,2048]{1,0:T(1,128)}, f32[1,2048]{1,0:T(1,128)S(1)}, u32[]{:S(2)}) copy-start(f32[1,2048]{1,0:T(1,128)S(1)} %get-tuple-element.916) | copy-start | bytes 24580
  125.3 270.2 %copy-start.123 = (f32[1,2048]{1,0:T(1,128)}, f32[1,2048]{1,0:T(1,128)S(1)}, u32[]{:S(2)}) copy-start(f32[1,2048]{1,0:T(1,128)S(1)} %get-tuple-element.917) | copy-start | bytes 24580
  125.3 270.2 %copy-start.129 = (f32[1,2048]{1,0:T(1,128)}, f32[1,2048]{1,0:T(1,128)S(1)}, u32[]{:S(2)}) copy-start(f32[1,2048]{1,0:T(1,128)S(1)} %get-tuple-element.918) | copy-start | bytes 24580
  144.9 125.7 %copy-start.18 = (f32[256,2048]{1,0:T(8,128)}, f32[256,2048]{1,0:T(8,128)S(1)}, u32[]{:S(2)}) copy-start(f32[256,2048]{1,0:T(8,128)S(1)} %fusion.210) | copy-start | bytes 6291460
  278.9 110.7 %copy-start.40 = (bf16[256,2048]{1,0:T(8,128)(2,1)S(1)}, bf16[256,2048]{1,0:T(8,128)(2,1)}, u32[]{:S(2)}) copy-start(bf16[256,2048]{1,0:T(8,128)(2,1)} %param.23) | copy-start | bytes 3145732
  523.5 116.4 %copy-start.80 = (bf16[256,2048]{1,0:T(8,128)(2,1)}, bf16[256,2048]{1,0:T(8,128)(2,1)S(1)}, u32[]{:S(2)}) copy-start(bf16[256,2048]{1,0:T(8,128)(2,1)S(1)} %get-tuple-element.936) | copy-start | bytes 3145732
  647.4 876.3 %copy-start.57 = (bf16[256,2048]{1,0:T(8,128)(2,1)}, bf16[256,2048]{1,0:T(8,128)(2,1)S(1)}, u32[]{:S(2)}) copy-start(bf16[256,2048]{1,0:T(8,128)(2,1)S(1)} %multiply_convert_fusion.2) | copy-start | bytes 3145732
  1094.2 872.1 %copy-start.65 = (bf16[256,2048]{1,0:T(8,128)(2,1)S(1)}, bf16[256,2048]{1,0:T(8,128)(2,1)}, u32[]{:S(2)}) copy-start(bf16[256,2048]{1,0:T(8,128)(2,1)} %param.41) | copy-start | bytes 3145732
  2045.2 578.7 %reduce-scatter.18.cloned.1.call-start = ((), (), s32[]{:S(2)}) async-start(), calls=%async_computation.21 | async-start | bytes 9437184 | tf_op jit(solution)/shard_map/reduce_scatter | solution.py:367
  2441.4 13.6 copy-start.126
  2441.4 13.6 copy-start.128
  2441.4 13.6 copy-start.130
  2441.4 13.6 copy-start.154
  2474.3 301.2 %reduce-scatter.16.cloned.1.call-start = ((), (), s32[]{:S(2)}) async-start(), calls=%async_computation.20 | async-start | bytes 9437184 | tf_op jit(solution)/shard_map/reduce_scatter | solution.py:364
  2486.2 441.4 %reduce-scatter.14.cloned.1.call-start = ((), (), s32[]{:S(2)}) async-start(), calls=%async_computation.19 | async-start | bytes 9437184 | tf_op jit(solution)/shard_map/reduce_scatter | solution.py:361
  2497.5 581.8 %reduce-scatter.20.cloned.1.call-start = ((), (), s32[]{:S(2)}) async-start(), calls=%async_computation.22 | async-start | bytes 9437184 | tf_op jit(solution)/shard_map/reduce_scatter | solution.py:370
  2504.4 951.5 %reduce-scatter.28.cloned.1.call-start = ((), (), s32[]{:S(2)}) async-start(), calls=%async_computation.26 | async-start | bytes 25952256 | tf_op jit(solution)/shard_map/reduce_scatter | solution.py:285
  2518.8 1313.6 %reduce-scatter.30.cloned.1.call-start = ((), (), s32[]{:S(2)}) async-start(), calls=%async_computation.27 | async-start | bytes 25952256 | tf_op jit(solution)/shard_map/reduce_scatter | solution.py:288
  2531.8 1676.9 %reduce-scatter.32.cloned.1.call-start = ((), (), s32[]{:S(2)}) async-start(), calls=%async_computation.28 | async-start | bytes 25952256 | tf_op jit(solution)/shard_map/reduce_scatter | solution.py:291
  2546.2 1729.9 %reduce-scatter.34.cloned.1.call-start = ((), (), s32[]{:S(2)}) async-start(), calls=%async_computation.29 | async-start | bytes 1769472
  2551.2 1779.9 %reduce-scatter.22.cloned.1.call-start = ((), (), s32[]{:S(2)}) async-start(), calls=%async_computation.23 | async-start | bytes 73728 | tf_op jit(solution)/shard_map/reduce_scatter | solution.py:373
  2551.8 1835.8 %reduce-scatter.24.cloned.1.call-start = ((), (), s32[]{:S(2)}) async-start(), calls=%async_computation.24 | async-start | bytes 73728 | tf_op jit(solution)/shard_map/reduce_scatter | solution.py:376
  2552.9 2083.2 %all-reduce.42.cloned.1.call-start = ((), (), s32[]{:S(2)}) async-start(), calls=%async_computation.30 | async-start | bytes 27787264 | tf_op jit(solution)/shard_map/psum | solution.py:406
  4210.0 13.9 slice-start
  4210.0 17.6 slice-start.2
  4232.5 18.5 copy-start.135
  4232.5 18.5 copy-start.54
  (249 other events, 697.7 us)
Sparse Core Ops, SparseCore 0:
  10.2 128.5 all-gather.14
  140.9 123.4 all-gather.12
  266.5 123.1 all-gather.10
  391.6 123.1 all-gather.16
  516.8 123.1 all-gather.18
  641.3 439.6 all-gather.20
  1082.5 441.0 all-gather.22
  1525.2 441.0 all-gather.24
  2045.3 148.7 reduce-scatter.25
  2474.4 149.3 reduce-scatter.17
  2627.5 148.0 reduce-scatter.15
  2779.5 148.0 reduce-scatter.13
  2931.2 148.0 reduce-scatter.19
  3083.5 372.4 reduce-scatter.27
  3460.2 372.0 reduce-scatter.29
  3836.6 372.1 reduce-scatter.31
  4213.0 63.0 reduce-scatter.33
  4279.6 51.5 reduce-scatter.21
  4334.9 52.6 reduce-scatter.23
  4390.6 245.4 all-reduce.41
where the time goes:
time: 4670 us; the launch traced here: 4660 us
  waiting for transfers between devices  3630 us (78%)
  matrix products  613 us (13%)
  blocking collectives  175 us (4%)
  other arithmetic  111 us (2%)
  local copies, waits for them, and re-layouts  100 us (2%)
    all_gather x1, waiting for transfers between devices, on_device(): lax.all_gather(w_gate, 'fsdp', axis=0, tiled=True)  434 us
    all_gather x1, waiting for transfers between devices, on_device(): lax.all_gather(w_up, 'fsdp', axis=0, tiled=True)  429 us
    all_gather x1, waiting for transfers between devices, on_device(): lax.all_gather(w_down, 'fsdp', axis=0, tiled=True)  429 us
    reduce_scatter x1, waiting for transfers between devices, on_device(): lax.psum_scatter(grad_w_gate.astype(jnp.bfloat16), 'fsdp', scatter_dimens...  377 us
    reduce_scatter x1, waiting for transfers between devices, on_device(): lax.psum_scatter(grad_w_down.astype(jnp.bfloat16), 'fsdp', scatter_dimens...  376 us
    reduce_scatter x1, waiting for transfers between devices, on_device(): lax.psum_scatter(grad_w_up.astype(jnp.bfloat16), 'fsdp', scatter_dimensio...  376 us
    psum x1, waiting for transfers between devices, on_device(): lax.psum(share_query.astype(jnp.bfloat16), 'replica').astype(jnp.float32)  232 us
    reduce_scatter x1, waiting for transfers between devices, on_device(): lax.psum_scatter(grad_w_query.astype(jnp.bfloat16), 'fsdp', scatter_dimen...  152 us
  transfers between devices with their start and end apart: 20, of which 19 were waited for; matrix products, arithmetic and copies ran while one was open for 15% of the time, Pallas kernels for 0%

commit v1 on v0

v1 whole, which is shorter than its diff:
```python
from functools import partial
import jax, jax.numpy as jnp
from jax import lax
from jax.experimental import pallas as pl
from jax.experimental.pallas import tpu as pltpu
from jax.sharding import PartitionSpec as P

EPS = 1e-06
BF = jnp.bfloat16
F32 = jnp.float32
NN = (((1,), (0,)), ((), ()))
NT = (((1,), (1,)), ((), ()))
TN = (((0,), (0,)), ((), ()))


def one_pass(left, right, dims=NN):
    return lax.dot_general(left.astype(BF), right.astype(BF), dims, preferred_element_type=F32)


def halves(value):
    high = value.astype(BF)
    return high, (value - high.astype(F32)).astype(BF)


def three_pass(left, right, dims=NN):
    lh, ll = left if isinstance(left, tuple) else halves(left)
    rh, rl = right if isinstance(right, tuple) else halves(right)
    total = lax.dot_general(lh, rh, dims, preferred_element_type=F32)
    total = total + lax.dot_general(lh, rl, dims, preferred_element_type=F32)
    return total + lax.dot_general(ll, rh, dims, preferred_element_type=F32)


def layout(length_of, count, rows):
    col = lax.broadcasted_iota(jnp.int32, (rows, 1), 0)
    row = lax.broadcasted_iota(jnp.int32, (1, rows), 1)
    bound = jnp.int32(0)
    start_col = jnp.zeros_like(col)
    start_row = jnp.zeros_like(row)
    for at in range(count):
        bound = bound + length_of(at)
        start_col = jnp.where(col >= bound, bound, start_col)
        start_row = jnp.where(row >= bound, bound, start_row)
    same = start_col == start_row
    within = same & (col >= row)
    strict = same & (col > row)
    return col, row, col - start_col, within, strict


def conv_sum(pre, taps, offset):
    total = pre * taps[0:1]
    for by in range(1, taps.shape[0]):
        moved = jnp.where(offset >= by, pltpu.roll(pre, by, 0), 0.0)
        total = total + moved * taps[by : by + 1]
    return total


def to_row(column, eye):
    return jnp.sum(jnp.where(eye, column, 0.0), axis=0, keepdims=True)


def lane_of(block, lane):
    lanes = lax.broadcasted_iota(jnp.int32, block.shape, 1)
    return jnp.sum(jnp.where(lanes == lane, block, 0.0), axis=1, keepdims=True)


def softplus(value):
    return jnp.maximum(value, 0.0) + jnp.log1p(jnp.exp(-jnp.abs(value)))


def head_parts(pre_ref, taps_ref, small, head, local, heads_local, head_size, heads_all, decay_log, decay_bias, geo):
    col, row, offset, within, strict, eye = geo
    width = heads_local * head_size
    at = lambda part: slice(part * width + local * head_size, part * width + (local + 1) * head_size)
    pres = [pre_ref[:, at(part)] for part in range(3)]
    taps = [taps_ref[:, at(part)] for part in range(3)]
    sums = [conv_sum(p, t, offset) for p, t in zip(pres, taps)]
    sigs = [jax.nn.sigmoid(s) for s in sums]
    convs = [s * g for s, g in zip(sums, sigs)]
    scale_q = lax.rsqrt(jnp.sum(convs[0] * convs[0], axis=1, keepdims=True) + EPS)
    scale_k = lax.rsqrt(jnp.sum(convs[1] * convs[1], axis=1, keepdims=True) + EPS)
    query = (convs[0] * scale_q * head_size**-0.5).astype(BF)
    key = (convs[1] * scale_k).astype(BF)
    value = convs[2].astype(BF)
    shifted = lane_of(small, head) + decay_bias
    beta = jax.nn.sigmoid(lane_of(small, heads_all + head))
    rate = -jnp.exp(jnp.full_like(shifted, decay_log))
    decay = rate * softplus(shifted)
    reach = jnp.where(within, to_row(decay, eye), 0.0)
    total_col = jnp.sum(reach, axis=1, keepdims=True)
    total_row = to_row(total_col, eye)
    fall = jnp.where(within, jnp.exp(jnp.where(within, total_col - total_row, 0.0)), 0.0)
    fall_strict = jnp.where(strict, fall, 0.0)
    keys = lax.dot_general(key, key, NT, preferred_element_type=F32)
    scores = lax.dot_general(query, key, NT, preferred_element_type=F32)
    return dict(pres=pres, taps=taps, sums=sums, sigs=sigs, convs=convs, scale_q=scale_q, scale_k=scale_k,
                query=query, key=key, value=value, shifted=shifted, beta=beta, rate=rate, decay=decay,
                fall=fall, fall_strict=fall_strict, keys=keys, scores=scores,
                gate=pre_ref[:, at(3)])


def unit_inverse(lower, col, row, dot):
    size = lower.shape[0]
    both = col ^ row
    eye = (both == 0).astype(F32)
    inverse = eye - jnp.where((both == 1) & (col > row), lower, 0.0)
    reach = 2
    while reach < size:
        if reach >= 64:
            rows = []
            for first in range(0, size, 2 * reach):
                a, b, c = first, first + reach, first + 2 * reach
                low = dot(inverse[b:c, b:c], dot(lower[b:c, a:b], inverse[a:b, a:b]))
                pad_l = [jnp.zeros((2 * reach, first), F32)] if first else []
                pad_r = [jnp.zeros((2 * reach, size - c), F32)] if size > c else []
                mid = jnp.concatenate([inverse[a:b, a:b], jnp.zeros((reach, reach), F32)], axis=1)
                end = jnp.concatenate([-low, inverse[b:c, b:c]], axis=1)
                rows.append(jnp.concatenate(pad_l + [jnp.concatenate([mid, end], axis=0)] + pad_r, axis=1))
            inverse = rows[0] if len(rows) == 1 else jnp.concatenate(rows, axis=0)
        else:
            corner = jnp.where((both >= reach) & (both < 2 * reach) & (col > row), lower, 0.0)
            inverse = inverse - dot(inverse, dot(corner, inverse))
        reach *= 2
    return inverse


def forward_kernel(cfg, rank_ref, len_ref, log_ref, bias_ref, pre_ref, taps_ref, gain_ref, gated_ref, inv_ref):
    heads_local, head_size, heads_all, dot_inv, dot_use = cfg
    rows = pre_ref.shape[0]
    step = pl.program_id(0)
    col, row, offset, within, strict = layout(lambda at: len_ref[step, at], len_ref.shape[1], rows)
    eye = col == row
    geo = (col, row, offset, within, strict, eye)
    small = pre_ref[:, 4 * heads_local * head_size :]
    for local in range(heads_local):
        head = rank_ref[0] * heads_local + local
        p = head_parts(pre_ref, taps_ref, small, head, local, heads_local, head_size, heads_all, log_ref[head], bias_ref[head], geo)
        inverse = unit_inverse(p["beta"] * p["fall_strict"] * p["keys"], col, row, dot_inv)
        inv_ref[0, local] = inverse.astype(inv_ref.dtype)
        update = dot_use(inverse, p["beta"] * p["value"].astype(F32))
        mixed = dot_use(p["scores"] * p["fall"], update)
        scale = lax.rsqrt(jnp.mean(mixed * mixed, axis=1, keepdims=True) + EPS)
        gate = p["gate"]
        out = mixed * scale * gain_ref[...] * (gate * jax.nn.sigmoid(gate))
        gated_ref[:, local * head_size : (local + 1) * head_size] = out.astype(BF)


def backward_kernel(cfg, rank_ref, len_ref, log_ref, bias_ref, pre_ref, taps_ref, gain_ref, inv_ref, grad_ref,
                    dpre_ref, dtaps_ref, dgain_ref, ddecay_ref):
    heads_local, head_size, heads_all, dot_inv, dot_use = cfg
    rows = pre_ref.shape[0]
    step = pl.program_id(0)

    @pl.when(step == 0)
    def _():
        dtaps_ref[...] = jnp.zeros_like(dtaps_ref)
        dgain_ref[...] = jnp.zeros_like(dgain_ref)
        ddecay_ref[...] = jnp.zeros_like(ddecay_ref)

    col, row, offset, within, strict = layout(lambda at: len_ref[step, at], len_ref.shape[1], rows)
    eye = col == row
    geo = (col, row, offset, within, strict, eye)
    width = heads_local * head_size
    small = pre_ref[:, 4 * width :]
    dsmall = jnp.zeros_like(small)
    lanes = lax.broadcasted_iota(jnp.int32, small.shape, 1)
    row_lanes = lax.broadcasted_iota(jnp.int32, (1, ddecay_ref.shape[1]), 1)
    for local in range(heads_local):
        head = rank_ref[0] * heads_local + local
        p = head_parts(pre_ref, taps_ref, small, head, local, heads_local, head_size, heads_all, log_ref[head], bias_ref[head], geo)
        at = lambda part: slice(part * width + local * head_size, part * width + (local + 1) * head_size)
        query, key, value, beta = p["query"], p["key"], p["value"], p["beta"]
        value_f = value.astype(F32)
        inverse = halves(inv_ref[0, local].astype(F32)) if inv_ref.dtype == F32 else (inv_ref[0, local], None)
        use = (lambda a, b, d=NN: dot_use(a, b, d)) if inv_ref.dtype == F32 else (lambda a, b, d=NN: one_pass(a[0], b, d))
        update = use(inverse, beta * value_f)
        attn = p["scores"] * p["fall"]
        mixed = dot_use(attn, update)
        grad, gate, gain = grad_ref[:, local * head_size : (local + 1) * head_size].astype(F32), p["gate"], gain_ref[...]
        sig = jax.nn.sigmoid(gate)
        opened = gate * sig
        scale = lax.rsqrt(jnp.mean(mixed * mixed, axis=1, keepdims=True) + EPS)
        normed = mixed * scale
        dgate = grad * normed * gain * (sig * (1.0 + gate * (1.0 - sig)))
        dgain_ref[...] += jnp.sum(grad * opened * normed, axis=0, keepdims=True)
        dnormed = grad * opened * gain
        dmixed = scale * (dnormed - normed * jnp.mean(dnormed * normed, axis=1, keepdims=True))
        dupdate = dot_use(attn, dmixed, TN)
        dattn = jnp.where(within, dot_use(dmixed, update, NT), 0.0)
        dright = use(inverse, dupdate, TN)
        dlower = jnp.where(strict, -dot_use(dright, update, NT), 0.0)
        dvalue = beta * dright
        spread_keys = p["fall_strict"] * p["keys"]
        dbeta = jnp.sum(dright * value_f, axis=1, keepdims=True) + jnp.sum(dlower * spread_keys, axis=1, keepdims=True)
        dscores = dattn * p["fall"]
        dkeys = dlower * beta * p["fall_strict"]
        dquery = dot_use(dscores, key.astype(F32))
        dkey = dot_use(dscores, query.astype(F32), TN) + dot_use(dkeys, key.astype(F32)) + dot_use(dkeys, key.astype(F32), TN)
        pairs = dattn * attn + dlower * beta * spread_keys
        dtotal_row = to_row(jnp.sum(pairs, axis=1, keepdims=True), eye) - jnp.sum(pairs, axis=0, keepdims=True)
        later = (col <= row) & (col - offset == row_start(row, len_ref, step))
        ddecay = jnp.sum(jnp.where(later, dtotal_row, 0.0), axis=1, keepdims=True)
        dshifted = ddecay * p["rate"] * jax.nn.sigmoid(p["shifted"])
        dlog = jnp.sum(ddecay * p["decay"], axis=0, keepdims=True)
        dbias = jnp.sum(dshifted, axis=0, keepdims=True)
        ddecay_ref[0:1] += jnp.where(row_lanes == head, dlog, 0.0)
        ddecay_ref[1:2] += jnp.where(row_lanes == head, dbias, 0.0)
        dsmall = dsmall + jnp.where(lanes == head, dshifted, 0.0)
        dsmall = dsmall + jnp.where(lanes == heads_all + head, dbeta * beta * (1.0 - beta), 0.0)
        rounded = [g.astype(BF).astype(F32) for g in (dquery, dkey, dvalue)]
        cq, ck = p["convs"][0], p["convs"][1]
        gq = rounded[0] * head_size**-0.5
        dconvs = [
            p["scale_q"] * (gq - cq * (p["scale_q"] * p["scale_q"] * jnp.sum(gq * cq, axis=1, keepdims=True))),
            p["scale_k"] * (rounded[1] - ck * (p["scale_k"] * p["scale_k"] * jnp.sum(rounded[1] * ck, axis=1, keepdims=True))),
            rounded[2],
        ]
        for part in range(3):
            sig_c, total, taps, pre = p["sigs"][part], p["sums"][part], p["taps"][part], p["pres"][part]
            dsum = dconvs[part] * (sig_c * (1.0 + total * (1.0 - sig_c)))
            dpre = dsum * taps[0:1]
            dtaps_ref[0:1, at(part)] += jnp.sum(dsum * pre, axis=0, keepdims=True)
            for by in range(1, taps.shape[0]):
                kept = jnp.where(offset >= by, dsum, 0.0)
                dtaps_ref[by : by + 1, at(part)] += jnp.sum(kept * pltpu.roll(pre, by, 0), axis=0, keepdims=True)
                dpre = dpre + pltpu.roll(kept, rows - by, 0) * taps[by : by + 1]
            dpre_ref[:, at(part)] = dpre.astype(BF)
        dpre_ref[:, at(3)] = dgate.astype(BF)
    dpre_ref[:, 4 * width :] = dsmall.astype(BF)


def row_start(row, len_ref, step):
    bound = jnp.int32(0)
    start = jnp.zeros_like(row)
    for at in range(len_ref.shape[1]):
        bound = bound + len_ref[step, at]
        start = jnp.where(row >= bound, bound, start)
    return start


def mixer_forward(rank, lengths, decay_log, decay_bias, pre, taps, gain, heads_local, dot_inv=three_pass, dot_use=three_pass, inv_dtype=F32):
    buffers = lengths.shape[0]
    rows = pre.shape[0] // buffers
    head_size = gain.shape[1]
    cfg = (heads_local, head_size, decay_log.shape[0], dot_inv, dot_use)
    smem = pl.BlockSpec(memory_space=pltpu.SMEM)
    whole = lambda a: pl.BlockSpec(a.shape, lambda i: (0,) * a.ndim)
    return pl.pallas_call(
        partial(forward_kernel, cfg),
        grid=(buffers,),
        in_specs=[smem, smem, smem, smem, pl.BlockSpec((rows, pre.shape[1]), lambda i: (i, 0)), whole(taps), whole(gain)],
        out_specs=[pl.BlockSpec((rows, heads_local * head_size), lambda i: (i, 0)),
                   pl.BlockSpec((1, heads_local, rows, rows), lambda i: (i, 0, 0, 0))],
        out_shape=[jax.ShapeDtypeStruct((buffers * rows, heads_local * head_size), BF),
                   jax.ShapeDtypeStruct((buffers, heads_local, rows, rows), inv_dtype)],
        compiler_params=pltpu.CompilerParams(vmem_limit_bytes=48 << 20),
        name="mixer_forward",
    )(rank, lengths, decay_log, decay_bias, pre, taps, gain)


def mixer_backward(rank, lengths, decay_log, decay_bias, pre, taps, gain, inverse, grad, heads_local, dot_inv=three_pass, dot_use=three_pass):
    buffers = lengths.shape[0]
    rows = pre.shape[0] // buffers
    head_size = gain.shape[1]
    cfg = (heads_local, head_size, decay_log.shape[0], dot_inv, dot_use)
    smem = pl.BlockSpec(memory_space=pltpu.SMEM)
    whole = lambda s: pl.BlockSpec(s, lambda i: (0,) * len(s))
    by_rows = lambda a: pl.BlockSpec((rows, a.shape[1]), lambda i: (i, 0))
    return pl.pallas_call(
        partial(backward_kernel, cfg),
        grid=(buffers,),
        in_specs=[smem, smem, smem, smem, by_rows(pre), whole(taps.shape), whole(gain.shape),
                  pl.BlockSpec((1, heads_local, rows, rows), lambda i: (i, 0, 0, 0)), by_rows(grad)],
        out_specs=[by_rows(pre), whole(taps.shape), whole(gain.shape), whole((8, 128))],
        out_shape=[jax.ShapeDtypeStruct(pre.shape, BF), jax.ShapeDtypeStruct(taps.shape, F32),
                   jax.ShapeDtypeStruct(gain.shape, F32), jax.ShapeDtypeStruct((8, 128), F32)],
        compiler_params=pltpu.CompilerParams(vmem_limit_bytes=48 << 20),
        name="mixer_backward",
    )(rank, lengths, decay_log, decay_bias, pre, taps, gain, inverse, grad)


def dot(left, right, dims=NN):
    return lax.dot_general(left, right, dims, preferred_element_type=F32)


def place_rows(pieces, row_starts, col_starts, shape):
    whole = jnp.zeros(shape, pieces[0].dtype)
    for piece, row, col in zip(pieces, row_starts, col_starts):
        whole = lax.dynamic_update_slice(whole, piece, (row, col))
    return whole


def program(shards, ranks):
    ring = shards // 2
    reach = (ring - 1) // 2
    even = ring % 2 == 0

    def shift(value, by):
        return lax.ppermute(value, "fsdp", [(f, ((f // 2 + by) % ring) * 2 + f % 2) for f in range(shards)])

    def pair(value):
        return lax.ppermute(value, "fsdp", [(f, f ^ 1) for f in range(shards)])

    def across(value, bits):
        return lax.ppermute(value, "replica", [(r, r ^ bits) for r in range(ranks)])

    def gather_pair_first(piece):
        up = down = (piece, pair(piece))
        got = {(0, 0): up[0], (0, 1): up[1]}
        for d in range(1, reach + 1):
            up = tuple(shift(v, 1) for v in up)
            down = tuple(shift(v, -1) for v in down)
            for dy in range(2):
                got[-d % ring, dy] = up[dy]
                got[d % ring, dy] = down[dy]
        if even:
            got[ring // 2, 0] = shift(up[0], 1)
            got[ring // 2, 1] = shift(down[1], -1)
        return got

    def gather_ring_first(first, second):
        up = down = (first, second)
        got = [{}, {}]
        for at in range(2):
            got[at][0, 0] = up[at]
        for d in range(1, reach + 1):
            up = tuple(shift(v, 1) for v in up)
            down = tuple(shift(v, -1) for v in down)
            for at in range(2):
                got[at][-d % ring, 0] = up[at]
                got[at][d % ring, 0] = down[at]
        if even:
            got[0][ring // 2, 0] = shift(up[0], 1)
            got[1][ring // 2, 0] = shift(down[1], -1)
        for at in range(2):
            for (dz, _), value in list(got[at].items()):
                got[at][dz, 1] = pair(value)
        return got

    def plus(*terms):
        total = terms[0].astype(F32)
        for term in terms[1:]:
            total = total + term.astype(F32)
        return total.astype(BF)

    def ring_sum(part, by, top):
        total = part(by * top)
        for d in range(top, 0, -1):
            moved = shift(total, by)
            if d == 1:
                return moved
            total = plus(part(by * (d - 1)), moved)

    def ring_total(part, long_up):
        tops = (ring // 2 if even and long_up else reach, ring // 2 if even and not long_up else reach)
        terms = [part(0)]
        for by, top in zip((1, -1), tops):
            if top:
                terms.append(ring_sum(part, by, top))
        return plus(*terms)

    def scatter_ring_first(part):
        kept = ring_total(lambda dz: part(dz, 0), True)
        given = ring_total(lambda dz: part(dz, 1), False)
        return plus(kept, pair(given))

    def scatter_pair_first(part, long_up):
        summed = {dz % ring: plus(part(dz, 0), pair(part(dz, 1))) for dz in range(ring)}
        return ring_total(lambda dz: summed[dz % ring], long_up)

    def swap_slots(value, bits):
        shaped = value.reshape((2, 2) + value.shape[1:])
        shaped = lax.rev(shaped, [1 - at for at in range(2) if bits >> at & 1])
        return shaped.reshape(value.shape)

    def gather_rows(value):
        two = across(value, 2)
        return [value, across(value, 1), two, across(two, 1)]

    def gather_columns(value, buffers):
        rows, cols = value.shape[0] // buffers, value.shape[1]
        pieces = gather_rows(value)
        starts, offsets, parts = [], [], []
        for j, piece in enumerate(pieces):
            for k in range(buffers):
                starts.append(k * rows)
                offsets.append(j * cols)
                parts.append(lax.slice_in_dim(piece, (k ^ j) * rows, ((k ^ j) + 1) * rows, axis=0))
        blocks = [jnp.concatenate(parts[j * buffers : (j + 1) * buffers], axis=0) for j in range(ranks)]
        return jnp.concatenate(blocks, axis=1)

    def scatter_columns(blocks):
        far = plus(blocks[2], swap_slots(across(blocks[3], 1), 1))
        far = across(far, 2)
        near = across(blocks[1], 1)
        return blocks[0].astype(F32) + swap_slots(near, 1).astype(F32) + swap_slots(far, 2).astype(F32)

    def scatter_slots(slots):
        far = across(plus(slots[2], across(slots[3], 1)), 2)
        return slots[0].astype(F32) + across(slots[1], 1).astype(F32) + far.astype(F32)

    def group_sum(value):
        value = value + swap_slots(across(value, 1), 1)
        return value + swap_slots(across(value, 2), 2)

    def by_rank(pieces, rank):
        low, high = rank % 2 == 1, rank // 2 == 1
        a, b, c, d = pieces
        a, b, c, d = (jnp.where(low, *p) for p in ((b, a), (a, b), (d, c), (c, d)))
        return [jnp.where(high, *p) for p in ((c, a), (d, b), (a, c), (b, d))]

    def to_tokens(value, rank):
        pieces = [value[0]] + [across(value[j], j) for j in range(1, ranks)]
        return jnp.concatenate(by_rank(pieces, rank), axis=1)

    def on_device(
        tokens, seq_lengths, attn_gain, w_query, w_key, w_value, w_outgate, w_alpha, w_beta, conv_weight,
        decay_log, decay_bias, head_gain, w_output, mlp_gain, w_gate, w_up, w_down, cotangent,
    ):
        rows, model = tokens.shape
        heads = decay_log.shape[0]
        heads_local = heads // ranks
        width = model // ranks
        piece_rows = w_query.shape[0]
        hidden_piece = w_down.shape[0] // ranks
        taps_count = conv_weight.shape[0]
        rank = lax.axis_index("replica")
        place = lax.axis_index("fsdp")
        z, y = place // 2, place % 2

        def owner(dz, dy):
            return ((z + dz) % ring) * 2 + (y ^ dy)

        own = lambda w: lax.dynamic_slice_in_dim(w, rank * width, width, axis=1)

        conv_cols = conv_weight.size // piece_rows
        small = jnp.concatenate(
            [w_alpha, w_beta, attn_gain[:, None], mlp_gain[:, None], conv_weight.reshape(piece_rows, conv_cols)], axis=1
        )
        small = jnp.pad(small, ((0, 0), (0, 128 - small.shape[1])))
        shard_qk = jnp.concatenate([own(w_query), own(w_key)], axis=1)
        shard_v = own(w_value)
        shard_g = jnp.concatenate([own(w_outgate), small], axis=1)
        shard_o = own(w_output)
        hidden = lambda w: lax.dynamic_index_in_dim(
            w.reshape(piece_rows, shards, ranks, hidden_piece), rank, 2, keepdims=False
        ).reshape(piece_rows, shards * hidden_piece)
        shard_gu = jnp.concatenate([hidden(w_gate), hidden(w_up)], axis=1)
        shard_d = lax.dynamic_slice_in_dim(w_down, rank * hidden_piece, hidden_piece, axis=0)

        lengths_own = seq_lengths[0]
        live = (jnp.arange(rows, dtype=jnp.int32) < jnp.sum(lengths_own)).astype(F32)[:, None]
        upstream_own = cotangent * live.astype(BF)

        token_slots = gather_rows(tokens)
        lengths = jnp.concatenate(gather_rows(seq_lengths), axis=0)
        got_qk = gather_pair_first(shard_qk)
        got_v, got_g = gather_ring_first(shard_v, shard_g)
        half = width // 2
        got_o = gather_ring_first(shard_o[:, :half], shard_o[:, half:])
        upstream_slots = gather_rows(upstream_own)
        got_d = gather_ring_first(shard_d[:, : model // 2], shard_d[:, model // 2 :])
        got_gu = gather_pair_first(shard_gu)

        def placed(parts, start_of, shape):
            pieces, starts, cols = [], [], []
            for col, got in parts:
                for (dz, dy), piece in got.items():
                    pieces.append(piece)
                    starts.append(start_of(owner(dz, dy)))
                    cols.append(col)
            return place_rows(pieces, starts, cols, shape)

        whole_rows = lambda f: f * piece_rows
        per_group = shards // ranks
        group_rows = lambda f: ((f // per_group) ^ rank) * width + (f % per_group) * piece_rows
        hidden_rows = lambda f: f * hidden_piece

        in_cols = 4 * width + 128
        full_in = placed([(0, got_qk), (2 * width, got_v), (3 * width, got_g)], whole_rows, (model, in_cols))

        smalls = full_in[:, 4 * width :]
        at = 2 * heads
        gain_one = smalls[:, at].astype(F32)
        gain_two = lax.dynamic_slice_in_dim(smalls[:, at + 1], rank * width, width).astype(F32)
        conv_all = smalls[:, at + 2 : at + 2 + conv_cols].reshape(shards, taps_count, -1)
        conv_all = jnp.swapaxes(conv_all, 0, 1).reshape(taps_count, 3, model)
        taps = lax.dynamic_slice_in_dim(conv_all, rank * width, width, axis=2).reshape(taps_count, 3 * width).astype(F32)

        buffers = ranks
        group = buffers * rows
        x_all = jnp.concatenate(token_slots, axis=0)
        x_f = x_all.astype(F32)
        normed = (x_f * lax.rsqrt(jnp.mean(x_f * x_f, axis=-1, keepdims=True) + EPS) * gain_one).astype(BF)
        pre = dot(normed, full_in)
        rank_arr = rank[None].astype(jnp.int32)
        gated, inverse = mixer_forward(
            rank_arr, lengths, decay_log, decay_bias, pre, taps, head_gain[None], heads_local
        )

        gated_all = gather_columns(gated, buffers)
        full_out = placed([(0, got_o[0]), (half, got_o[1])], group_rows, (model, width))
        branch = dot(gated_all, full_out)
        resid = own(x_all).astype(F32) + branch
        branch_own = to_tokens(branch.astype(BF).reshape(buffers, rows, width), rank).astype(F32)

        scaled = (resid * gain_two).astype(BF)
        scaled_all = gather_columns(scaled, buffers)
        squares = group_sum(jnp.sum(resid * resid, axis=1).reshape(buffers, rows)).reshape(group, 1)
        inv_two = lax.rsqrt(squares / model + EPS)

        hidden_cols = shards * hidden_piece
        full_gu = placed([(0, got_gu)], group_rows, (model, 2 * hidden_cols))
        full_down = placed([(0, got_d[0]), (model // 2, got_d[1])], hidden_rows, (hidden_cols, model))
        raw = dot(scaled_all, full_gu)
        raw_gate, raw_up = raw[:, :hidden_cols], raw[:, hidden_cols:]
        gate_rows, up_rows = raw_gate * inv_two, raw_up * inv_two
        sig = jax.nn.sigmoid(gate_rows)
        opened = gate_rows * sig
        hidden_b = (opened * up_rows).astype(BF)
        upstream = jnp.concatenate(upstream_slots, axis=0)
        grad_hidden = dot(upstream, full_down, NT)
        grad_gate = (inv_two * (grad_hidden * up_rows * (sig * (1.0 + gate_rows * (1.0 - sig))))).astype(BF)
        grad_up = (inv_two * (grad_hidden * opened)).astype(BF)
        grad_gu = jnp.concatenate([grad_gate, grad_up], axis=1)
        stat = jnp.sum(raw_gate * grad_gate.astype(F32) + raw_up * grad_up.astype(F32), axis=1)
        stat = group_sum(stat.reshape(buffers, rows)).reshape(group, 1)

        blocks = [
            dot(grad_gu, full_gu[j * width : (j + 1) * width], NT).astype(BF).reshape(buffers, rows, width)
            for j in range(ranks)
        ]
        grad_two = scatter_columns(blocks).reshape(group, width)
        grad_resid = own(upstream).astype(F32) + gain_two * grad_two - resid * (inv_two * inv_two * stat / model)
        grad_mlp_gain = jnp.sum(grad_two * resid, axis=0)
        grad_branch = grad_resid.astype(BF)

        pieces_of = lambda whole, start_of, count, first, cols: (
            lambda dz, dy: lax.dynamic_slice(whole, (start_of(owner(dz, dy)), first), (count, cols))
        )
        d_gu = dot(scaled_all, grad_gu, TN).astype(BF)
        d_down = dot(hidden_b, upstream, TN).astype(BF)
        share_gu = scatter_ring_first(pieces_of(d_gu, group_rows, piece_rows, 0, 2 * hidden_cols))
        share_d = jnp.concatenate(
            [
                scatter_pair_first(pieces_of(d_down, hidden_rows, hidden_piece, side * (model // 2), model // 2), side == 0)
                for side in range(2)
            ],
            axis=1,
        )

        down = dot(hidden_b, full_down).astype(BF).reshape(buffers, rows, model)
        output = ((tokens.astype(F32) + branch_own + scatter_slots(down)) * live).astype(BF)

        blocks = [
            dot(grad_branch, full_out[j * width : (j + 1) * width], NT).astype(BF).reshape(buffers, rows, width)
            for j in range(ranks)
        ]
        grad_gated = scatter_columns(blocks).reshape(group, width)
        grad_resid_own = to_tokens(grad_branch.reshape(buffers, rows, width), rank).astype(F32)
        d_out = dot(gated_all, grad_branch, TN).astype(BF)
        d_pre, d_taps, d_head_gain, d_decay = mixer_backward(
            rank_arr, lengths, decay_log, decay_bias, pre, taps, head_gain[None], inverse, grad_gated, heads_local
        )
        d_in = dot(normed, d_pre, TN).astype(BF)
        grad_normed = dot(d_pre, full_in, NT).astype(BF).reshape(buffers, rows, model)
        share_o = jnp.concatenate(
            [scatter_pair_first(pieces_of(d_out, group_rows, piece_rows, side * half, half), side == 0) for side in range(2)],
            axis=1,
        )
        share_qk = scatter_ring_first(pieces_of(d_in, whole_rows, piece_rows, 0, 2 * width))
        share_v = scatter_pair_first(pieces_of(d_in, whole_rows, piece_rows, 2 * width, width), True)
        share_g = scatter_pair_first(pieces_of(d_in, whole_rows, piece_rows, 3 * width, width + 128), False)

        grad_one = scatter_slots(grad_normed)
        x_own = tokens.astype(F32)
        inv_one = lax.rsqrt(jnp.mean(x_own * x_own, axis=-1, keepdims=True) + EPS)
        grad_attn_gain = jnp.sum(grad_one * x_own * inv_one, axis=0)
        pulled = gain_one * grad_one
        grad_x = inv_one * pulled - x_own * (inv_one**3 * jnp.mean(pulled * x_own, axis=-1, keepdims=True))
        grad_tokens = (grad_resid_own + grad_x).astype(BF)

        own_cols = lambda value: lax.dynamic_update_slice_in_dim(
            jnp.zeros(value.shape[:-1] + (model,), F32), value, rank * width, axis=value.ndim - 1
        )
        packed = jnp.concatenate(
            [
                own_cols(d_taps.reshape(taps_count, 3, width)).reshape(-1),
                own_cols(grad_mlp_gain),
                grad_attn_gain,
                d_head_gain[0],
                d_decay[0, :heads],
                d_decay[1, :heads],
            ]
        )
        total = jnp.pad(packed, (0, -packed.size % 1024)).reshape(-1, 128)
        for bits in (1, 2):
            total = total + across(total, bits)
        bits = 1
        while bits < shards:
            total = total + lax.ppermute(total, "fsdp", [(f, f ^ bits) for f in range(shards)])
            bits *= 2
        total = total.reshape(-1)
        conv_size = taps_count * 3 * model
        sum_conv = total[:conv_size].reshape(taps_count, shards, -1)
        sum_conv = lax.dynamic_index_in_dim(sum_conv, place, 1, keepdims=False)
        at = conv_size
        sum_mlp_gain = lax.dynamic_slice_in_dim(total, at + place * piece_rows, piece_rows)
        sum_attn_gain = lax.dynamic_slice_in_dim(total, at + model + place * piece_rows, piece_rows)
        at += 2 * model
        sum_head_gain = total[at : at + head_gain.size]
        at += head_gain.size
        sum_log, sum_bias = total[at : at + heads], total[at + heads : at + 2 * heads]

        wide = lambda share: jnp.concatenate(by_rank(gather_rows(share), rank), axis=1).astype(F32)
        qk_all = by_rank(gather_rows(share_qk), rank)
        out_query = jnp.concatenate([p[:, :width] for p in qk_all], axis=1).astype(F32)
        out_key = jnp.concatenate([p[:, width:] for p in qk_all], axis=1).astype(F32)
        g_all = gather_rows(share_g)
        out_outgate = jnp.concatenate([p[:, :width] for p in by_rank(g_all, rank)], axis=1).astype(F32)
        low = (g_all[0][:, width:].astype(F32) + g_all[1][:, width:]) + (g_all[2][:, width:].astype(F32) + g_all[3][:, width:])
        out_alpha, out_beta = low[:, :heads], low[:, heads : 2 * heads]
        gu_all = by_rank(gather_rows(share_gu), rank)
        unhide = lambda first: (
            jnp.stack([p[:, first : first + hidden_cols].reshape(piece_rows, shards, hidden_piece) for p in gu_all], axis=2)
            .reshape(piece_rows, shards * ranks * hidden_piece)
            .astype(F32)
        )
        out_down = jnp.concatenate(by_rank(gather_rows(share_d), rank), axis=0).astype(F32)
        return (
            output, grad_tokens, sum_attn_gain, out_query, out_key, wide(share_v), out_outgate, out_alpha, out_beta,
            sum_conv, sum_log, sum_bias, sum_head_gain, wide(share_o), sum_mlp_gain, unhide(0), unhide(hidden_cols), out_down,
        )

    return on_device


def solution(mesh):
    rows, cols = P("fsdp", None), P("fsdp")
    tokens = P(("replica", "fsdp"), None)
    return jax.shard_map(
        program(mesh.shape["fsdp"], mesh.shape["replica"]),
        mesh=mesh,
        in_specs=(
            tokens, tokens, cols, rows, rows, rows, rows, rows, rows, P(None, "fsdp"), P(), P(), P(), rows, cols,
            rows, rows, rows, tokens,
        ),
        out_specs=(
            tokens, tokens, cols, rows, rows, rows, rows, rows, rows, P(None, "fsdp"), P(), P(), P(), rows, cols,
            rows, rows, rows,
        ),
        check_vma=False,
    )
```

time: 4670 us -> 1450 us (0.31)
  waiting for transfers between devices: 3630 us -> 437 us
  matrix products: 613 us -> 190 us
  starting transfers between devices: 1.38 us -> 256 us
  blocking collectives: 175 us -> 0 us
  local copies, waits for them, and re-layouts: 100 us -> 264 us
  Pallas kernels: 0 us -> 124 us
  other arithmetic: 111 us -> 159 us
    reduce_scatter x10 -> x0, waiting for transfers between devices: 1730 us -> none  [the longest x1 377 us: on_device(): lax.psum_scatter(grad_w_gate.astype(jnp.bfloat16), 'fsdp', scatter_dimens...]
    all_gather x8 -> x0, waiting for transfers between devices: 1650 us -> none  [the longest x1 434 us: on_device(): lax.all_gather(w_gate, 'fsdp', axis=0, tiled=True)]
    ppermute x0 -> x172, waiting for transfers between devices: none -> 437 us  [the longest x60 228 us: shift(): lax.ppermute(value, 'fsdp', [(f, (f // 2 + by) % ring * 2 + f % 2) for f...]
    dot_general x306 -> x18, matrix products: 613 us -> 190 us  [dot(): return lax.dot_general(left, right, dims, preferred_element_type=F32)]
    ppermute x0 -> x172, starting transfers between devices: none -> 256 us  [the longest x57 138 us: across(): return lax.ppermute(value, 'replica', [(r, r ^ bits) for r in range(ranks)])]
    psum x1 -> x0, waiting for transfers between devices: 232 us -> none  [on_device(): lax.psum(share_query.astype(jnp.bfloat16), 'replica').astype(jnp.float32)]
    pallas_call x0 -> x2, Pallas kernels: none -> 124 us  [the longest x1 77.2 us: mixer_forward(): pl.pallas_call(partial(forward_kernel, cfg), grid=(buffers,), in_specs=[s...]
    all_gather x5 -> x0, blocking collectives: 106 us -> none  [the longest x1 24.8 us: on_device(): lax.all_gather(conv_weight, 'fsdp', axis=1, tiled=True)]
  transfers between devices with their start and end apart: 20 -> 172, of which waited for: 19 -> 55; matrix products, arithmetic and copies ran while one was open for 15% -> 30% of each run, Pallas kernels for 0% -> 9%
where the time goes in v1:
time: 1450 us; the launch traced here: 1430 us
  waiting for transfers between devices  437 us (30%)
  local copies, waits for them, and re-layouts  264 us (18%)
  starting transfers between devices  256 us (18%)
  matrix products  190 us (13%)
  other arithmetic  159 us (11%)
  Pallas kernels  124 us (9%)
    ppermute x60, waiting for transfers between devices, shift(): lax.ppermute(value, 'fsdp', [(f, (f // 2 + by) % ring * 2 + f % 2) for f...  228 us
    dot_general x18, matrix products, dot(): return lax.dot_general(left, right, dims, preferred_element_type=F32)  190 us
    ppermute x57, starting transfers between devices, across(): return lax.ppermute(value, 'replica', [(r, r ^ bits) for r in range(ranks)])  138 us
    ppermute x57, waiting for transfers between devices, across(): return lax.ppermute(value, 'replica', [(r, r ^ bits) for r in range(ranks)])  103 us
    ppermute x52, waiting for transfers between devices, pair(): return lax.ppermute(value, 'fsdp', [(f, f ^ 1) for f in range(shards)])  103 us
    dynamic_update_slice x63, local copies, waits for them, and re-layouts, place_rows(): whole = lax.dynamic_update_slice(whole, piece, (row, col))  91.7 us
    pallas_call x1, Pallas kernels, mixer_forward(): pl.pallas_call(partial(forward_kernel, cfg), grid=(buffers,), in_specs=[s...  77.2 us
    ppermute x60, starting transfers between devices, shift(): lax.ppermute(value, 'fsdp', [(f, (f // 2 + by) % ring * 2 + f % 2) for f...  76.2 us
  transfers between devices with their start and end apart: 172, of which 55 were waited for; matrix products, arithmetic and copies ran while one was open for 30% of the time, Pallas kernels for 9%

profile of v1, /device:TPU:1, one launch (start us, length us, event | category | flops | bytes accessed | tf_op | source)
XLA Modules:
  0.0 1433.6 jit_solution(14533523495636331355)
XLA Ops:
  19.2 4.5 copy.93
  23.7 4.6 copy.92
  30.6 4.5 broadcast_in_dim.40
  37.3 5.8 broadcast_in_dim.45
  52.1 3.6 collective-permute-start.31
  66.8 5.7 collective-permute-done.32
  72.8 6.8 collective-permute-start.60
  88.9 9.9 collective-permute-done.60
  132.0 3.8 collective-permute-done.38
  152.6 5.7 collective-permute-done.41
  177.6 22.0 %collective-permute-done.43 = bf16[256,256]{1,0:T(8,128)(2,1)S(1)} collective-permute-done((bf16[256,256]{1,0:T(8,128)(2,1)}, bf16[256,256]{1,0:T(8,128)(2,1)S(1)}, u32[]{:S(2)}, u32[]{:S(2)}) %collective-permute-start.43) | collective-permute-done | bytes 131104 | tf_op jit(solution)/shard_map/ppermute | solution.py:301
  201.3 5.3 collective-permute-done.26
  218.0 7.7 collective-permute-start.3
  252.5 41.7 %collective-permute-done.12 = bf16[256,1024]{1,0:T(8,128)(2,1)S(1)} collective-permute-done((bf16[256,1024]{1,0:T(8,128)(2,1)}, bf16[256,1024]{1,0:T(8,128)(2,1)S(1)}, u32[]{:S(2)}, u32[]{:S(2)}) %collective-permute-start.12) | collective-permute-done | bytes 524320 | tf_op jit(solution)/shard_map/ppermute | solution.py:298
  325.9 17.2 %fusion.39.pre_ref = f32[1024,2176]{1,0:T(8,128)} fusion(bf16[2048,2176]{0,1:T(8,128)(2,1)} %constant_dynamic-update-slice_fusion.48, bf16[1024,2048]{0,1:T(8,128)(2,1)S(1)} %get-tuple-element.80, f32[2048]{0:T(1024)S(1)} %bitcast.126, f32[1024]{0:T(1024)S(1)} %add_rsqrt_fusion.1), kind=kOutput, calls=%fused_computation.87 | convolution fusion | flops 9135194112 | bytes 22032384 | tf_op jit(solution)/shard_map/dot_general | solution.py:282
  343.1 77.2 %mixer_forward.1 = (bf16[1024,512]{1,0:T(8,128)(2,1)S(1)}, f32[4,4,256,256]{3,2,1,0:T(8,128)S(1)}) custom-call(s32[1]{0:T(128)} %bitcast.rank_ref, s32[4,2]{1,0:T(4,128)S(1)} %pad_add_fusion.len_ref, f32[16]{0:T(128)S(1)} %copy-done.7, f32[16]{0:T(128)S(1)} %copy-done.9, f32[1024,2176]{1,0:T(8,128)} %fusion.39.pre_ref, f32[4,1536]{1,0:T(4,128)S(1)} %bitcast.95, ...), custom_call_target="tpu_custom_call" | custom-call | tf_op jit(solution)/shard_map/mixer_forward/pallas_call | solution.py:247
  422.9 4.5 collective-permute-start.76
  432.0 7.0 collective-permute-done.71
  450.5 7.3 collective-permute-done.72
  464.5 64.4 %maximum_maximum_fusion = bf16[1024,2048]{1,0:T(8,128)(2,1)S(1)} fusion(bf16[256,512]{1,0:T(8,128)(2,1)S(1)} %get-tuple-element.206, bf16[256,512]{1,0:T(8,128)(2,1)S(1)} %get-tuple-element.207, bf16[256,512]{1,0:T(8,128)(2,1)S(1)} %get-tuple-element.208, bf16[256,512]{1,0:T(8,128)(2,1)S(1)} %get-tuple-element.205, ...), kind=kLoop, calls=%fused_computation.18 | loop fusion | flops 46137344 | bytes 8388608 | tf_op jit(solution)/shard_map/concatenate | solution.py:389
  528.9 7.3 multiply_reduce_fusion.1
  538.7 61.4 %collective-permute-start.57 = (f32[4,256]{1,0:T(4,128)S(1)}, f32[4,256]{1,0:T(4,128)S(1)}, u32[]{:S(2)}, u32[]{:S(2)}) collective-permute-start(f32[4,256]{1,0:T(4,128)S(1)} %reshape.329), channel_id=1, source_target_pairs={{0,8},{8,0},{16,24},{24,16},{1,9},{9,1},{17,25},{25,17},{2,10},{10... | collective-permute-start | bytes 12296 | tf_op jit(solution)/shard_map/ppermute | solution.py:304
  605.8 6.3 collective-permute-start.49
  617.9 25.1 %fusion.51 = f32[1024,2816]{1,0:T(8,128)} fusion(bf16[2048,2816]{0,1:T(8,128)(2,1)} %constant_dynamic-update-slice_fusion.8, bf16[256,512]{0,1:T(8,128)(2,1)} %get-tuple-element.196, bf16[256,512]{0,1:T(8,128)(2,1)} %get-tuple-element.197, bf16[256,512]{0,1:T(8,128)(2,1)} %get-tuple-element.198, bf16[256,512]{0,1:T(8,128)(2,1)} %get-tuple-element.195, ...), kind=kOutput, calls=%fused_computation.332 | convolution fusion | flops 11857297408 | bytes 27262976 | tf_op jit(solution)/shard_map/dot_general | solution.py:282
  643.0 18.0 %add_reduce_fusion = (f32[1024]{0:T(1024)S(1)}, bf16[1024,1408]{1,0:T(8,128)(2,1)}, bf16[1024,1408]{1,0:T(8,128)(2,1)}, bf16[1024,1408]{1,0:T(8,128)(2,1)}) fusion(f32[1024,2816]{1,0:T(8,128)} %fusion.51, f32[1024]{0:T(1024)S(1)} %add_rsqrt_fusion, bf16[1408,2048]{1,0:T(8,128)(2,1)} %constant_dynamic-update-slice_fusion.32, ...), kind=kOutput, calls=%fused_computation.9 | convolution fusion | flops 5958401024 | bytes 30154752 | tf_op jit(solution)/shard_map/dot_general | solution.py:282
  661.0 7.8 fusion.30
  668.8 6.0 fusion.33
  674.8 32.1 %convolution_convert_fusion = bf16[2048,2816]{1,0:T(8,128)(2,1)} fusion(bf16[1024,1408]{1,0:T(8,128)(2,1)} %get-tuple-element.70, bf16[1024,1408]{1,0:T(8,128)(2,1)} %get-tuple-element.69, bf16[256,512]{0,1:T(8,128)(2,1)} %get-tuple-element.196, bf16[256,512]{0,1:T(8,128)(2,1)} %get-tuple-element.197, bf16[256,512]{0,1:T(8,128)(2,1)} %get-tuple-element.198, ...), kind=kOutput, calls=%fused_computation | convolution fusion | flops 11874598912 | bytes 21495808 | tf_op jit(solution)/shard_map/dot_general | solution.py:282
  706.9 11.9 convolution_convert_fusion.4
  718.8 6.5 convolution_convert_fusion.2
  730.7 5.9 fusion.27
  748.4 5.6 collective-permute-done.160
  761.8 7.7 collective-permute-done.166
  771.2 5.3 constant_dynamic-slice_fusion.9
  793.0 5.5 rev.32
  803.3 49.2 %collective-permute-done.167 = bf16[176,1024]{1,0:T(8,128)(2,1)} collective-permute-done((bf16[176,1024]{1,0:T(8,128)(2,1)}, bf16[176,1024]{1,0:T(8,128)(2,1)}, u32[]{:S(2)}, u32[]{:S(2)}) %collective-permute-start.167) | collective-permute-done | bytes 360480 | tf_op jit(solution)/shard_map/ppermute | solution.py:298
  857.3 4.9 add_convert_fusion.4
  863.1 9.1 collective-permute-done.168
  878.9 10.6 multiply_reduce_fusion
  940.6 46.6 %collective-permute-done.140 = bf16[256,256]{0,1:T(8,128)(2,1)S(1)} collective-permute-done((bf16[256,256]{0,1:T(8,128)(2,1)S(1)}, bf16[256,256]{0,1:T(8,128)(2,1)S(1)}, u32[]{:S(2)}, u32[]{:S(2)}) %collective-permute-start.140) | collective-permute-done | bytes 131104 | tf_op jit(solution)/shard_map/ppermute | solution.py:298
  1000.9 4.0 collective-permute-done.169
  1006.2 3.8 add_convert_fusion.1
  1032.4 13.9 collective-permute-done.89
  1050.2 46.9 %mixer_backward.1 = (bf16[1024,2176]{1,0:T(8,128)(2,1)}, f32[4,1536]{1,0:T(4,128)S(1)}, f32[1,128]{1,0:T(1,128)S(1)}, f32[8,128]{1,0:T(8,128)S(1)}) custom-call(s32[1]{0:T(128)} %bitcast.rank_ref, s32[4,2]{1,0:T(4,128)S(1)} %copy-done.6, f32[16]{0:T(128)S(1)} %copy-done.8, f32[16]{0:T(128)S(1)} %copy-done.10, f32[1024,2176]{1,0:T(8,128)} %fusion.39.pre_ref, ...), custom_call_target="tpu_custom_call" | custom-call | tf_op jit(solution)/shard_map/mixer_backward/pallas_call | solution.py:268
  1097.1 14.0 convolution_convert_fusion.3
  1111.2 14.5 %convolution_convert_fusion.1 = bf16[2048,2176]{0,1:T(8,128)(2,1)S(1)} fusion(bf16[1024,2176]{1,0:T(8,128)(2,1)} %get-tuple-element.26, bf16[1024,2048]{0,1:T(8,128)(2,1)} %copy-done.23, f32[2048]{0:T(1024)S(1)} %bitcast.127, f32[1024]{0:T(1024)S(1)} %copy-done.95), kind=kOutput, calls=%fused_computation.1 | convolution fusion | flops 9139650560 | bytes 17575936 | tf_op jit(solution)/shard_map/dot_general | solution.py:282
  1135.3 4.2 collective-permute-done.109
  1141.8 4.8 collective-permute-done.119
  1147.9 5.6 collective-permute-done.122
  1154.8 4.4 collective-permute-done.113
  1173.7 4.5 add_convert_fusion
  1180.9 3.6 collective-permute-done.98
  1184.4 10.0 collective-permute-done.102
  1194.8 5.2 collective-permute-done.114
  1205.0 9.0 collective-permute-done.112
  1226.8 5.4 collective-permute-done.101
  1233.6 21.6 %collective-permute-done.103 = bf16[256,1024]{0,1:T(8,128)(2,1)S(1)} collective-permute-done((bf16[256,1024]{0,1:T(8,128)(2,1)S(1)}, bf16[256,1024]{0,1:T(8,128)(2,1)S(1)}, u32[]{:S(2)}, u32[]{:S(2)}) %collective-permute-start.103) | collective-permute-done | bytes 524320 | tf_op jit(solution)/shard_map/ppermute | solution.py:298
  1262.2 4.6 collective-permute-done.125
  1279.3 38.3 %collective-permute-done.92 = bf16[256,2048]{0,1:T(8,128)(2,1)S(1)} collective-permute-done((bf16[256,2048]{0,1:T(8,128)(2,1)}, bf16[256,2048]{0,1:T(8,128)(2,1)S(1)}, u32[]{:S(2)}, u32[]{:S(2)}) %collective-permute-start.92) | collective-permute-done | bytes 1048608 | tf_op jit(solution)/shard_map/ppermute | solution.py:304
  1327.4 34.9 %collective-permute-done.94 = f32[232,128]{1,0:T(8,128)S(1)} collective-permute-done((f32[232,128]{1,0:T(8,128)S(1)}, f32[232,128]{1,0:T(8,128)S(1)}, u32[]{:S(2)}, u32[]{:S(2)}) %collective-permute-start.94) | collective-permute-done | bytes 118816 | tf_op jit(solution)/shard_map/ppermute | solution.py:304
  1369.0 4.8 fusion.19
  1389.7 4.7 broadcast_select_fusion.7
  1412.7 6.5 copy.120
  1426.9 6.3 copy.121
  (789 shorter events, 513.3 us)
Async XLA Ops:
  2.6 57.8 %collective-permute-start.13 = (bf16[256,512]{1,0:T(8,128)(2,1)}, bf16[256,512]{1,0:T(8,128)(2,1)}, u32[]{:S(2)}, u32[]{:S(2)}) collective-permute-start(bf16[256,512]{1,0:T(8,128)(2,1)} %constant_dynamic-slice_fusion.25), channel_id=1, source_target_pairs={{0,2},{1,3},{2,4},{3,5},{4,6},{5,7},{6,0},{7,1},{8,10},{9,11},{10,... | collective-permute-start | bytes 786440 | tf_op jit(solution)/shard_map/ppermute | solution.py:298
  4.7 55.9 %collective-permute-start.14 = (bf16[256,512]{1,0:T(8,128)(2,1)}, bf16[256,512]{1,0:T(8,128)(2,1)}, u32[]{:S(2)}, u32[]{:S(2)}) collective-permute-start(bf16[256,512]{1,0:T(8,128)(2,1)} %constant_dynamic-slice_fusion.25), channel_id=1, source_target_pairs={{0,6},{1,7},{2,0},{3,1},{4,2},{5,3},{6,4},{7,5},{8,14},{9,15},{10,... | collective-permute-start | bytes 786440 | tf_op jit(solution)/shard_map/ppermute | solution.py:298
  6.8 55.4 %collective-permute-start.16 = (bf16[256,512]{1,0:T(8,128)(2,1)}, bf16[256,512]{1,0:T(8,128)(2,1)}, u32[]{:S(2)}, u32[]{:S(2)}) collective-permute-start(bf16[256,512]{1,0:T(8,128)(2,1)} %constant_dynamic-slice_fusion.25), channel_id=1, source_target_pairs={{0,1},{1,0},{2,3},{3,2},{4,5},{5,4},{6,7},{7,6},{8,9},{9,8},{10,11... | collective-permute-start | bytes 786440 | tf_op jit(solution)/shard_map/ppermute | solution.py:301
  8.0 40.4 %collective-permute-start.1 = (s32[1,2]{1,0:T(1,128)}, s32[1,2]{1,0:T(1,128)S(1)}, u32[]{:S(2)}, u32[]{:S(2)}) collective-permute-start(s32[1,2]{1,0:T(1,128)} %param.20), channel_id=1, source_target_pairs={{0,16},{8,24},{16,0},{24,8},{1,17},{9,25},{17,1},{25,9},{2,18},{10... | collective-permute-start | bytes 32 | tf_op jit(solution)/shard_map/ppermute | solution.py:304
  12.3 43.4 %collective-permute-start.30 = (bf16[256,256]{1,0:T(8,128)(2,1)}, bf16[256,256]{1,0:T(8,128)(2,1)}, u32[]{:S(2)}, u32[]{:S(2)}) collective-permute-start(bf16[256,256]{1,0:T(8,128)(2,1)} %get-tuple-element.78), channel_id=1, source_target_pairs={{0,2},{1,3},{2,4},{3,5},{4,6},{5,7},{6,0},{7,1},{8,10},{9,11},{10,... | collective-permute-start | bytes 393224 | tf_op jit(solution)/shard_map/ppermute | solution.py:298
  72.8 26.0 %collective-permute-start.60 = (bf16[176,1024]{1,0:T(8,128)(2,1)}, bf16[176,1024]{1,0:T(8,128)(2,1)}, u32[]{:S(2)}, u32[]{:S(2)}) collective-permute-start(bf16[176,1024]{1,0:T(8,128)(2,1)} %get-tuple-element.74), channel_id=1, source_target_pairs={{0,6},{1,7},{2,0},{3,1},{4,2},{5,3},{6,4},{7,5},{8,14},{9,15},{10,... | collective-permute-start | bytes 1081352 | tf_op jit(solution)/shard_map/ppermute | solution.py:298
  81.1 33.2 %collective-permute-start.6 = (bf16[256,1024]{1,0:T(8,128)(2,1)S(1)}, bf16[256,1024]{1,0:T(8,128)(2,1)}, u32[]{:S(2)}, u32[]{:S(2)}) collective-permute-start(bf16[256,1024]{1,0:T(8,128)(2,1)S(1)} %copy-done.31), channel_id=1, source_target_pairs={{0,1},{1,0},{2,3},{3,2},{4,5},{5,4},{6,7},{7,6},{8,9},{9,8},{10,11... | collective-permute-start | bytes 1572872 | tf_op jit(solution)/shard_map/ppermute | solution.py:301
  84.2 27.3 %collective-permute-start.62 = (bf16[176,1024]{1,0:T(8,128)(2,1)}, bf16[176,1024]{1,0:T(8,128)(2,1)}, u32[]{:S(2)}, u32[]{:S(2)}) collective-permute-start(bf16[176,1024]{1,0:T(8,128)(2,1)} %get-tuple-element.74), channel_id=1, source_target_pairs={{0,1},{1,0},{2,3},{3,2},{4,5},{5,4},{6,7},{7,6},{8,9},{9,8},{10,11... | collective-permute-start | bytes 1081352 | tf_op jit(solution)/shard_map/ppermute | solution.py:301
  85.0 33.0 %collective-permute-start.7 = (bf16[256,1024]{1,0:T(8,128)(2,1)S(1)}, bf16[256,1024]{1,0:T(8,128)(2,1)}, u32[]{:S(2)}, u32[]{:S(2)}) collective-permute-start(bf16[256,1024]{1,0:T(8,128)(2,1)S(1)} %copy-done.31), channel_id=1, source_target_pairs={{0,2},{1,3},{2,4},{3,5},{4,6},{5,7},{6,0},{7,1},{8,10},{9,11},{10,... | collective-permute-start | bytes 1572872 | tf_op jit(solution)/shard_map/ppermute | solution.py:298
  85.7 36.1 %collective-permute-start.8 = (bf16[256,1024]{1,0:T(8,128)(2,1)S(1)}, bf16[256,1024]{1,0:T(8,128)(2,1)}, u32[]{:S(2)}, u32[]{:S(2)}) collective-permute-start(bf16[256,1024]{1,0:T(8,128)(2,1)S(1)} %copy-done.31), channel_id=1, source_target_pairs={{0,6},{1,7},{2,0},{3,1},{4,2},{5,3},{6,4},{7,5},{8,14},{9,15},{10,... | collective-permute-start | bytes 1572872 | tf_op jit(solution)/shard_map/ppermute | solution.py:298
  158.3 48.7 %collective-permute-start.9 = (bf16[256,1024]{1,0:T(8,128)(2,1)}, bf16[256,1024]{1,0:T(8,128)(2,1)S(1)}, u32[]{:S(2)}, u32[]{:S(2)}) collective-permute-start(bf16[256,1024]{1,0:T(8,128)(2,1)} %collective-permute-done.6), channel_id=1, source_target_pairs={{0,2},{1,3},{2,4},{3,5},{4,6},{5,7},{6,0},{7,1},{8,10},{9,11},{10,... | collective-permute-start | bytes 1572872 | tf_op jit(solution)/shard_map/ppermute | solution.py:298
  163.0 82.9 %collective-permute-start.50 = (bf16[256,2816]{0,1:T(8,128)(2,1)}, bf16[256,2816]{0,1:T(8,128)(2,1)}, u32[]{:S(2)}, u32[]{:S(2)}) collective-permute-start(bf16[256,2816]{0,1:T(8,128)(2,1)} %get-tuple-element.171), channel_id=1, source_target_pairs={{0,1},{1,0},{2,3},{3,2},{4,5},{5,4},{6,7},{7,6},{8,9},{9,8},{10,11... | collective-permute-start | bytes 4325384 | tf_op jit(solution)/shard_map/ppermute | solution.py:301
  164.2 35.4 %collective-permute-start.43 = (bf16[256,256]{1,0:T(8,128)(2,1)}, bf16[256,256]{1,0:T(8,128)(2,1)S(1)}, u32[]{:S(2)}, u32[]{:S(2)}) collective-permute-start(bf16[256,256]{1,0:T(8,128)(2,1)} %collective-permute-done.39), channel_id=1, source_target_pairs={{0,1},{1,0},{2,3},{3,2},{4,5},{5,4},{6,7},{7,6},{8,9},{9,8},{10,11... | collective-permute-start | bytes 393224 | tf_op jit(solution)/shard_map/ppermute | solution.py:301
  164.4 42.2 %collective-permute-start.26 = (bf16[256,640]{1,0:T(8,128)(2,1)}, bf16[256,640]{1,0:T(8,128)(2,1)}, u32[]{:S(2)}, u32[]{:S(2)}) collective-permute-start(bf16[256,640]{1,0:T(8,128)(2,1)} %collective-permute-done.22), channel_id=1, source_target_pairs={{0,1},{1,0},{2,3},{3,2},{4,5},{5,4},{6,7},{7,6},{8,9},{9,8},{10,11... | collective-permute-start | bytes 983048 | tf_op jit(solution)/shard_map/ppermute | solution.py:301
  174.4 43.7 %collective-permute-start.10 = (bf16[256,1024]{1,0:T(8,128)(2,1)}, bf16[256,1024]{1,0:T(8,128)(2,1)}, u32[]{:S(2)}, u32[]{:S(2)}) collective-permute-start(bf16[256,1024]{1,0:T(8,128)(2,1)} %collective-permute-done.6), channel_id=1, source_target_pairs={{0,6},{1,7},{2,0},{3,1},{4,2},{5,3},{6,4},{7,5},{8,14},{9,15},{10,... | collective-permute-start | bytes 1572872 | tf_op jit(solution)/shard_map/ppermute | solution.py:298
  199.6 28.2 %collective-permute-start.11 = (bf16[256,1024]{1,0:T(8,128)(2,1)}, bf16[256,1024]{1,0:T(8,128)(2,1)}, u32[]{:S(2)}, u32[]{:S(2)}) collective-permute-start(bf16[256,1024]{1,0:T(8,128)(2,1)} %collective-permute-done.7), channel_id=1, source_target_pairs={{0,2},{1,3},{2,4},{3,5},{4,6},{5,7},{6,0},{7,1},{8,10},{9,11},{10,... | collective-permute-start | bytes 1572872 | tf_op jit(solution)/shard_map/ppermute | solution.py:298
  206.6 37.7 %collective-permute-start.4 = (bf16[256,2048]{0,1:T(8,128)(2,1)S(1)}, bf16[256,2048]{0,1:T(8,128)(2,1)}, u32[]{:S(2)}, u32[]{:S(2)}) collective-permute-start(bf16[256,2048]{0,1:T(8,128)(2,1)S(1)} %copy.60), channel_id=1, source_target_pairs={{0,16},{8,24},{16,0},{24,8},{1,17},{9,25},{17,1},{25,9},{2,18},{10... | collective-permute-start | bytes 3145736 | tf_op jit(solution)/shard_map/ppermute | solution.py:304
  207.0 42.8 %collective-permute-start.51 = (bf16[256,2816]{0,1:T(8,128)(2,1)}, bf16[256,2816]{0,1:T(8,128)(2,1)}, u32[]{:S(2)}, u32[]{:S(2)}) collective-permute-start(bf16[256,2816]{0,1:T(8,128)(2,1)} %get-tuple-element.171), channel_id=1, source_target_pairs={{0,2},{1,3},{2,4},{3,5},{4,6},{5,7},{6,0},{7,1},{8,10},{9,11},{10,... | collective-permute-start | bytes 4325384 | tf_op jit(solution)/shard_map/ppermute | solution.py:298
  218.0 102.1 %collective-permute-start.3 = (bf16[256,2048]{0,1:T(8,128)(2,1)S(1)}, bf16[256,2048]{0,1:T(8,128)(2,1)}, u32[]{:S(2)}, u32[]{:S(2)}) collective-permute-start(bf16[256,2048]{0,1:T(8,128)(2,1)S(1)} %copy.60), channel_id=1, source_target_pairs={{0,8},{8,0},{16,24},{24,16},{1,9},{9,1},{17,25},{25,17},{2,10},{10... | collective-permute-start | bytes 3145736 | tf_op jit(solution)/shard_map/ppermute | solution.py:304
  238.1 184.7 %collective-permute-start.52 = (bf16[256,2816]{0,1:T(8,128)(2,1)}, bf16[256,2816]{0,1:T(8,128)(2,1)}, u32[]{:S(2)}, u32[]{:S(2)}) collective-permute-start(bf16[256,2816]{0,1:T(8,128)(2,1)} %get-tuple-element.171), channel_id=1, source_target_pairs={{0,6},{1,7},{2,0},{3,1},{4,2},{5,3},{6,4},{7,5},{8,14},{9,15},{10,... | collective-permute-start | bytes 4325384 | tf_op jit(solution)/shard_map/ppermute | solution.py:298
  244.3 49.9 %collective-permute-start.12 = (bf16[256,1024]{1,0:T(8,128)(2,1)}, bf16[256,1024]{1,0:T(8,128)(2,1)S(1)}, u32[]{:S(2)}, u32[]{:S(2)}) collective-permute-start(bf16[256,1024]{1,0:T(8,128)(2,1)} %collective-permute-done.10), channel_id=1, source_target_pairs={{0,6},{1,7},{2,0},{3,1},{4,2},{5,3},{6,4},{7,5},{8,14},{9,15},{10,... | collective-permute-start | bytes 1572872 | tf_op jit(solution)/shard_map/ppermute | solution.py:298
  245.8 76.1 %collective-permute-start.5 = (bf16[256,2048]{0,1:T(8,128)(2,1)}, bf16[256,2048]{0,1:T(8,128)(2,1)}, u32[]{:S(2)}, u32[]{:S(2)}) collective-permute-start(bf16[256,2048]{0,1:T(8,128)(2,1)} %collective-permute-done.4), channel_id=1, source_target_pairs={{0,8},{8,0},{16,24},{24,16},{1,9},{9,1},{17,25},{25,17},{2,10},{10... | collective-permute-start | bytes 3145736 | tf_op jit(solution)/shard_map/ppermute | solution.py:304
  249.8 71.4 %collective-permute-start.66 = (bf16[176,1024]{1,0:T(8,128)(2,1)}, bf16[176,1024]{1,0:T(8,128)(2,1)}, u32[]{:S(2)}, u32[]{:S(2)}) collective-permute-start(bf16[176,1024]{1,0:T(8,128)(2,1)} %get-tuple-element.72), channel_id=1, source_target_pairs={{0,2},{1,3},{2,4},{3,5},{4,6},{5,7},{6,0},{7,1},{8,10},{9,11},{10,... | collective-permute-start | bytes 1081352 | tf_op jit(solution)/shard_map/ppermute | solution.py:298
  295.0 26.6 %collective-permute-start.67 = (bf16[176,1024]{1,0:T(8,128)(2,1)}, bf16[176,1024]{1,0:T(8,128)(2,1)}, u32[]{:S(2)}, u32[]{:S(2)}) collective-permute-start(bf16[176,1024]{1,0:T(8,128)(2,1)} %get-tuple-element.72), channel_id=1, source_target_pairs={{0,6},{1,7},{2,0},{3,1},{4,2},{5,3},{6,4},{7,5},{8,14},{9,15},{10,... | collective-permute-start | bytes 1081352 | tf_op jit(solution)/shard_map/ppermute | solution.py:298
  320.1 100.2 %collective-permute-start.77 = (bf16[256,2048]{0,1:T(8,128)(2,1)S(1)}, bf16[256,2048]{0,1:T(8,128)(2,1)S(1)}, u32[]{:S(2)}, u32[]{:S(2)}) collective-permute-start(bf16[256,2048]{0,1:T(8,128)(2,1)S(1)} %broadcast_multiply_fusion), channel_id=1, source_target_pairs={{0,16},{8,24},{16,0},{24,8},{1,17},{9,25},{17,1},{25,9},{2,18},{10... | collective-permute-start | bytes 3145736 | tf_op jit(solution)/shard_map/ppermute | solution.py:304
  321.2 106.2 %collective-permute-start.69 = (bf16[176,1024]{1,0:T(8,128)(2,1)}, bf16[176,1024]{1,0:T(8,128)(2,1)S(1)}, u32[]{:S(2)}, u32[]{:S(2)}) collective-permute-start(bf16[176,1024]{1,0:T(8,128)(2,1)} %get-tuple-element.72), channel_id=1, source_target_pairs={{0,1},{1,0},{2,3},{3,2},{4,5},{5,4},{6,7},{7,6},{8,9},{9,8},{10,11... | collective-permute-start | bytes 1081352 | tf_op jit(solution)/shard_map/ppermute | solution.py:301
  321.5 107.7 %collective-permute-start.68 = (bf16[176,1024]{1,0:T(8,128)(2,1)}, bf16[176,1024]{1,0:T(8,128)(2,1)S(1)}, u32[]{:S(2)}, u32[]{:S(2)}) collective-permute-start(bf16[176,1024]{1,0:T(8,128)(2,1)} %collective-permute-done.67), channel_id=1, source_target_pairs={{0,6},{1,7},{2,0},{3,1},{4,2},{5,3},{6,4},{7,5},{8,14},{9,15},{10,... | collective-permute-start | bytes 1081352 | tf_op jit(solution)/shard_map/ppermute | solution.py:298
  321.9 107.3 %collective-permute-start.70 = (bf16[176,1024]{1,0:T(8,128)(2,1)}, bf16[176,1024]{1,0:T(8,128)(2,1)S(1)}, u32[]{:S(2)}, u32[]{:S(2)}) collective-permute-start(bf16[176,1024]{1,0:T(8,128)(2,1)} %collective-permute-done.66), channel_id=1, source_target_pairs={{0,1},{1,0},{2,3},{3,2},{4,5},{5,4},{6,7},{7,6},{8,9},{9,8},{10,11... | collective-permute-start | bytes 1081352 | tf_op jit(solution)/shard_map/ppermute | solution.py:301
  429.2 33.4 %collective-permute-start.54 = (bf16[256,2816]{0,1:T(8,128)(2,1)}, bf16[256,2816]{0,1:T(8,128)(2,1)}, u32[]{:S(2)}, u32[]{:S(2)}) collective-permute-start(bf16[256,2816]{0,1:T(8,128)(2,1)} %collective-permute-done.50), channel_id=1, source_target_pairs={{0,6},{1,7},{2,0},{3,1},{4,2},{5,3},{6,4},{7,5},{8,14},{9,15},{10,... | collective-permute-start | bytes 4325384 | tf_op jit(solution)/shard_map/ppermute | solution.py:298
  446.8 90.6 %collective-permute-start.53 = (bf16[256,2816]{0,1:T(8,128)(2,1)}, bf16[256,2816]{0,1:T(8,128)(2,1)S(1)}, u32[]{:S(2)}, u32[]{:S(2)}) collective-permute-start(bf16[256,2816]{0,1:T(8,128)(2,1)} %collective-permute-done.50), channel_id=1, source_target_pairs={{0,2},{1,3},{2,4},{3,5},{4,6},{5,7},{6,0},{7,1},{8,10},{9,11},{10,... | collective-permute-start | bytes 4325384 | tf_op jit(solution)/shard_map/ppermute | solution.py:298
  457.7 145.2 %collective-permute-start.55 = (bf16[256,2816]{0,1:T(8,128)(2,1)}, bf16[256,2816]{0,1:T(8,128)(2,1)}, u32[]{:S(2)}, u32[]{:S(2)}) collective-permute-start(bf16[256,2816]{0,1:T(8,128)(2,1)} %collective-permute-done.51), channel_id=1, source_target_pairs={{0,2},{1,3},{2,4},{3,5},{4,6},{5,7},{6,0},{7,1},{8,10},{9,11},{10,... | collective-permute-start | bytes 4325384 | tf_op jit(solution)/shard_map/ppermute | solution.py:298
  462.6 149.5 %collective-permute-start.56 = (bf16[256,2816]{0,1:T(8,128)(2,1)}, bf16[256,2816]{0,1:T(8,128)(2,1)}, u32[]{:S(2)}, u32[]{:S(2)}) collective-permute-start(bf16[256,2816]{0,1:T(8,128)(2,1)} %collective-permute-done.54), channel_id=1, source_target_pairs={{0,6},{1,7},{2,0},{3,1},{4,2},{5,3},{6,4},{7,5},{8,14},{9,15},{10,... | collective-permute-start | bytes 4325384 | tf_op jit(solution)/shard_map/ppermute | solution.py:298
  536.1 69.7 %collective-permute-start.48 = (bf16[1024,512]{0,1:T(8,128)(2,1)}, bf16[1024,512]{0,1:T(8,128)(2,1)S(1)}, u32[]{:S(2)}, u32[]{:S(2)}) collective-permute-start(bf16[1024,512]{0,1:T(8,128)(2,1)} %get-tuple-element.111), channel_id=1, source_target_pairs={{0,16},{8,24},{16,0},{24,8},{1,17},{9,25},{17,1},{25,9},{2,18},{10... | collective-permute-start | bytes 3145736 | tf_op jit(solution)/shard_map/ppermute | solution.py:304
  538.7 64.1 %collective-permute-start.57 = (f32[4,256]{1,0:T(4,128)S(1)}, f32[4,256]{1,0:T(4,128)S(1)}, u32[]{:S(2)}, u32[]{:S(2)}) collective-permute-start(f32[4,256]{1,0:T(4,128)S(1)} %reshape.329), channel_id=1, source_target_pairs={{0,8},{8,0},{16,24},{24,16},{1,9},{9,1},{17,25},{25,17},{2,10},{10... | collective-permute-start | bytes 12296 | tf_op jit(solution)/shard_map/ppermute | solution.py:304
  738.2 31.3 %collective-permute-start.166 = (bf16[176,1024]{1,0:T(8,128)(2,1)}, bf16[176,1024]{1,0:T(8,128)(2,1)}, u32[]{:S(2)}, u32[]{:S(2)}) collective-permute-start(bf16[176,1024]{1,0:T(8,128)(2,1)} %get-tuple-element.116), channel_id=1, source_target_pairs={{0,1},{1,0},{2,3},{3,2},{4,5},{5,4},{6,7},{7,6},{8,9},{9,8},{10,11... | collective-permute-start | bytes 1081352 | tf_op jit(solution)/shard_map/ppermute | solution.py:301
  746.2 40.0 %collective-permute-start.80 = (bf16[4,256,512]{2,1,0:T(8,128)(2,1)}, bf16[4,256,512]{2,1,0:T(8,128)(2,1)S(1)}, u32[]{:S(2)}, u32[]{:S(2)}) collective-permute-start(bf16[4,256,512]{2,1,0:T(8,128)(2,1)} %bitcast.140), channel_id=1, source_target_pairs={{0,8},{8,0},{16,24},{24,16},{1,9},{9,1},{17,25},{25,17},{2,10},{10... | collective-permute-start | bytes 3145736 | tf_op jit(solution)/shard_map/ppermute | solution.py:304
  753.9 32.4 %collective-permute-start.74 = (bf16[256,2048]{0,1:T(8,128)(2,1)}, bf16[256,2048]{0,1:T(8,128)(2,1)S(1)}, u32[]{:S(2)}, u32[]{:S(2)}) collective-permute-start(bf16[256,2048]{0,1:T(8,128)(2,1)} %get-tuple-element.132), channel_id=1, source_target_pairs={{0,8},{8,0},{16,24},{24,16},{1,9},{9,1},{17,25},{25,17},{2,10},{10... | collective-permute-start | bytes 3145736 | tf_op jit(solution)/shard_map/ppermute | solution.py:304
  779.7 74.2 %collective-permute-start.145 = (bf16[256,2816]{1,0:T(8,128)(2,1)}, bf16[256,2816]{1,0:T(8,128)(2,1)}, u32[]{:S(2)}, u32[]{:S(2)}) collective-permute-start(bf16[256,2816]{1,0:T(8,128)(2,1)} %get-tuple-element.84), channel_id=1, source_target_pairs={{0,2},{1,3},{2,4},{3,5},{4,6},{5,7},{6,0},{7,1},{8,10},{9,11},{10,... | collective-permute-start | bytes 4325384 | tf_op jit(solution)/shard_map/ppermute | solution.py:298
  780.9 76.4 %collective-permute-start.149 = (bf16[256,2816]{1,0:T(8,128)(2,1)}, bf16[256,2816]{1,0:T(8,128)(2,1)}, u32[]{:S(2)}, u32[]{:S(2)}) collective-permute-start(bf16[256,2816]{1,0:T(8,128)(2,1)} %get-tuple-element.85), channel_id=1, source_target_pairs={{0,6},{1,7},{2,0},{3,1},{4,2},{5,3},{6,4},{7,5},{8,14},{9,15},{10,... | collective-permute-start | bytes 4325384 | tf_op jit(solution)/shard_map/ppermute | solution.py:298
  786.3 66.2 %collective-permute-start.167 = (bf16[176,1024]{1,0:T(8,128)(2,1)}, bf16[176,1024]{1,0:T(8,128)(2,1)}, u32[]{:S(2)}, u32[]{:S(2)}) collective-permute-start(bf16[176,1024]{1,0:T(8,128)(2,1)} %get-tuple-element.113), channel_id=1, source_target_pairs={{0,6},{1,7},{2,0},{3,1},{4,2},{5,3},{6,4},{7,5},{8,14},{9,15},{10,... | collective-permute-start | bytes 1081352 | tf_op jit(solution)/shard_map/ppermute | solution.py:298
  788.9 73.3 %collective-permute-start.162 = (bf16[176,1024]{1,0:T(8,128)(2,1)}, bf16[176,1024]{1,0:T(8,128)(2,1)}, u32[]{:S(2)}, u32[]{:S(2)}) collective-permute-start(bf16[176,1024]{1,0:T(8,128)(2,1)} %get-tuple-element.119), channel_id=1, source_target_pairs={{0,1},{1,0},{2,3},{3,2},{4,5},{5,4},{6,7},{7,6},{8,9},{9,8},{10,11... | collective-permute-start | bytes 1081352 | tf_op jit(solution)/shard_map/ppermute | solution.py:301
  801.7 72.8 %collective-permute-start.81 = (bf16[4,256,512]{2,1,0:T(8,128)(2,1)S(1)}, bf16[4,256,512]{2,1,0:T(8,128)(2,1)S(1)}, u32[]{:S(2)}, u32[]{:S(2)}) collective-permute-start(bf16[4,256,512]{2,1,0:T(8,128)(2,1)S(1)} %fusion.23), channel_id=1, source_target_pairs={{0,16},{8,24},{16,0},{24,8},{1,17},{9,25},{17,1},{25,9},{2,18},{10... | collective-permute-start | bytes 3145736 | tf_op jit(solution)/shard_map/ppermute | solution.py:304
  918.4 80.4 %collective-permute-start.148 = (bf16[256,2816]{1,0:T(8,128)(2,1)}, bf16[256,2816]{1,0:T(8,128)(2,1)}, u32[]{:S(2)}, u32[]{:S(2)}) collective-permute-start(bf16[256,2816]{1,0:T(8,128)(2,1)} %get-tuple-element.86), channel_id=1, source_target_pairs={{0,2},{1,3},{2,4},{3,5},{4,6},{5,7},{6,0},{7,1},{8,10},{9,11},{10,... | collective-permute-start | bytes 4325384 | tf_op jit(solution)/shard_map/ppermute | solution.py:298
  920.6 85.6 %collective-permute-start.150 = (bf16[256,2816]{1,0:T(8,128)(2,1)}, bf16[256,2816]{1,0:T(8,128)(2,1)}, u32[]{:S(2)}, u32[]{:S(2)}) collective-permute-start(bf16[256,2816]{1,0:T(8,128)(2,1)} %get-tuple-element.83), channel_id=1, source_target_pairs={{0,6},{1,7},{2,0},{3,1},{4,2},{5,3},{6,4},{7,5},{8,14},{9,15},{10,... | collective-permute-start | bytes 4325384 | tf_op jit(solution)/shard_map/ppermute | solution.py:298
  932.2 57.3 %collective-permute-start.45 = (bf16[256,512]{0,1:T(8,128)(2,1)}, bf16[256,512]{0,1:T(8,128)(2,1)S(1)}, u32[]{:S(2)}, u32[]{:S(2)}) collective-permute-start(bf16[256,512]{0,1:T(8,128)(2,1)} %get-tuple-element.187), channel_id=1, source_target_pairs={{0,16},{8,24},{16,0},{24,8},{1,17},{9,25},{17,1},{25,9},{2,18},{10... | collective-permute-start | bytes 786440 | tf_op jit(solution)/shard_map/ppermute | solution.py:304
  933.0 56.9 %collective-permute-start.46 = (bf16[256,512]{0,1:T(8,128)(2,1)}, bf16[256,512]{0,1:T(8,128)(2,1)S(1)}, u32[]{:S(2)}, u32[]{:S(2)}) collective-permute-start(bf16[256,512]{0,1:T(8,128)(2,1)} %get-tuple-element.186), channel_id=1, source_target_pairs={{0,8},{8,0},{16,24},{24,16},{1,9},{9,1},{17,25},{25,17},{2,10},{10... | collective-permute-start | bytes 786440 | tf_op jit(solution)/shard_map/ppermute | solution.py:304
  938.3 48.9 %collective-permute-start.140 = (bf16[256,256]{0,1:T(8,128)(2,1)S(1)}, bf16[256,256]{0,1:T(8,128)(2,1)S(1)}, u32[]{:S(2)}, u32[]{:S(2)}) collective-permute-start(bf16[256,256]{0,1:T(8,128)(2,1)S(1)} %get-tuple-element.138), channel_id=1, source_target_pairs={{0,6},{1,7},{2,0},{3,1},{4,2},{5,3},{6,4},{7,5},{8,14},{9,15},{10,... | collective-permute-start | bytes 393224 | tf_op jit(solution)/shard_map/ppermute | solution.py:298
  998.8 167.6 %collective-permute-start.147 = (bf16[256,2816]{1,0:T(8,128)(2,1)}, bf16[256,2816]{1,0:T(8,128)(2,1)}, u32[]{:S(2)}, u32[]{:S(2)}) collective-permute-start(bf16[256,2816]{1,0:T(8,128)(2,1)} %get-tuple-element.87), channel_id=1, source_target_pairs={{0,6},{1,7},{2,0},{3,1},{4,2},{5,3},{6,4},{7,5},{8,14},{9,15},{10,... | collective-permute-start | bytes 4325384 | tf_op jit(solution)/shard_map/ppermute | solution.py:298
  1010.0 158.9 %collective-permute-start.146 = (bf16[256,2816]{1,0:T(8,128)(2,1)}, bf16[256,2816]{1,0:T(8,128)(2,1)}, u32[]{:S(2)}, u32[]{:S(2)}) collective-permute-start(bf16[256,2816]{1,0:T(8,128)(2,1)} %get-tuple-element.82), channel_id=1, source_target_pairs={{0,2},{1,3},{2,4},{3,5},{4,6},{5,7},{6,0},{7,1},{8,10},{9,11},{10,... | collective-permute-start | bytes 4325384 | tf_op jit(solution)/shard_map/ppermute | solution.py:298
  1027.6 142.2 %collective-permute-start.151 = (bf16[256,2816]{1,0:T(8,128)(2,1)}, bf16[256,2816]{1,0:T(8,128)(2,1)}, u32[]{:S(2)}, u32[]{:S(2)}) collective-permute-start(bf16[256,2816]{1,0:T(8,128)(2,1)} %add_convert_fusion.1), channel_id=1, source_target_pairs={{0,1},{1,0},{2,3},{3,2},{4,5},{5,4},{6,7},{7,6},{8,9},{9,8},{10,11... | collective-permute-start | bytes 4325384 | tf_op jit(solution)/shard_map/ppermute | solution.py:301
  1166.4 56.7 %collective-permute-start.91 = (bf16[256,2048]{0,1:T(8,128)(2,1)S(1)}, bf16[256,2048]{0,1:T(8,128)(2,1)S(1)}, u32[]{:S(2)}, u32[]{:S(2)}) collective-permute-start(bf16[256,2048]{0,1:T(8,128)(2,1)S(1)} %get-tuple-element.130), channel_id=1, source_target_pairs={{0,8},{8,0},{16,24},{24,16},{1,9},{9,1},{17,25},{25,17},{2,10},{10... | collective-permute-start | bytes 3145736 | tf_op jit(solution)/shard_map/ppermute | solution.py:304
  1173.6 26.4 %collective-permute-start.114 = (bf16[256,512]{0,1:T(8,128)(2,1)S(1)}, bf16[256,512]{0,1:T(8,128)(2,1)S(1)}, u32[]{:S(2)}, u32[]{:S(2)}) collective-permute-start(bf16[256,512]{0,1:T(8,128)(2,1)S(1)} %get-tuple-element.99), channel_id=1, source_target_pairs={{0,6},{1,7},{2,0},{3,1},{4,2},{5,3},{6,4},{7,5},{8,14},{9,15},{10,... | collective-permute-start | bytes 786440 | tf_op jit(solution)/shard_map/ppermute | solution.py:298
  1179.5 35.6 %collective-permute-start.118 = (bf16[256,640]{0,1:T(8,128)(2,1)S(1)}, bf16[256,640]{0,1:T(8,128)(2,1)S(1)}, u32[]{:S(2)}, u32[]{:S(2)}) collective-permute-start(bf16[256,640]{0,1:T(8,128)(2,1)S(1)} %get-tuple-element.88), channel_id=1, source_target_pairs={{0,1},{1,0},{2,3},{3,2},{4,5},{5,4},{6,7},{7,6},{8,9},{9,8},{10,11... | collective-permute-start | bytes 983048 | tf_op jit(solution)/shard_map/ppermute | solution.py:301
  1184.4 34.0 %collective-permute-start.120 = (bf16[256,640]{0,1:T(8,128)(2,1)S(1)}, bf16[256,640]{0,1:T(8,128)(2,1)S(1)}, u32[]{:S(2)}, u32[]{:S(2)}) collective-permute-start(bf16[256,640]{0,1:T(8,128)(2,1)S(1)} %get-tuple-element.92), channel_id=1, source_target_pairs={{0,2},{1,3},{2,4},{3,5},{4,6},{5,7},{6,0},{7,1},{8,10},{9,11},{10,... | collective-permute-start | bytes 983048 | tf_op jit(solution)/shard_map/ppermute | solution.py:298
  1215.1 55.0 %collective-permute-start.100 = (bf16[256,1024]{0,1:T(8,128)(2,1)}, bf16[256,1024]{0,1:T(8,128)(2,1)}, u32[]{:S(2)}, u32[]{:S(2)}) collective-permute-start(bf16[256,1024]{0,1:T(8,128)(2,1)} %get-tuple-element.105), channel_id=1, source_target_pairs={{0,6},{1,7},{2,0},{3,1},{4,2},{5,3},{6,4},{7,5},{8,14},{9,15},{10,... | collective-permute-start | bytes 1572872 | tf_op jit(solution)/shard_map/ppermute | solution.py:298
  1218.4 36.8 %collective-permute-start.103 = (bf16[256,1024]{0,1:T(8,128)(2,1)S(1)}, bf16[256,1024]{0,1:T(8,128)(2,1)S(1)}, u32[]{:S(2)}, u32[]{:S(2)}) collective-permute-start(bf16[256,1024]{0,1:T(8,128)(2,1)S(1)} %get-tuple-element.101), channel_id=1, source_target_pairs={{0,6},{1,7},{2,0},{3,1},{4,2},{5,3},{6,4},{7,5},{8,14},{9,15},{10,... | collective-permute-start | bytes 1572872 | tf_op jit(solution)/shard_map/ppermute | solution.py:298
  1221.5 49.8 %collective-permute-start.99 = (bf16[256,1024]{0,1:T(8,128)(2,1)}, bf16[256,1024]{0,1:T(8,128)(2,1)}, u32[]{:S(2)}, u32[]{:S(2)}) collective-permute-start(bf16[256,1024]{0,1:T(8,128)(2,1)} %get-tuple-element.100), channel_id=1, source_target_pairs={{0,2},{1,3},{2,4},{3,5},{4,6},{5,7},{6,0},{7,1},{8,10},{9,11},{10,... | collective-permute-start | bytes 1572872 | tf_op jit(solution)/shard_map/ppermute | solution.py:298
  1223.1 32.8 %collective-permute-start.115 = (bf16[256,512]{0,1:T(8,128)(2,1)S(1)}, bf16[256,512]{0,1:T(8,128)(2,1)S(1)}, u32[]{:S(2)}, u32[]{:S(2)}) collective-permute-start(bf16[256,512]{0,1:T(8,128)(2,1)S(1)} %add_convert_fusion.30), channel_id=1, source_target_pairs={{0,16},{8,24},{16,0},{24,8},{1,17},{9,25},{17,1},{25,9},{2,18},{10... | collective-permute-start | bytes 786440 | tf_op jit(solution)/shard_map/ppermute | solution.py:304
  1261.1 106.9 %collective-permute-start.73 = (bf16[256,2048]{0,1:T(8,128)(2,1)}, bf16[256,2048]{0,1:T(8,128)(2,1)}, u32[]{:S(2)}, u32[]{:S(2)}) collective-permute-start(bf16[256,2048]{0,1:T(8,128)(2,1)} %get-tuple-element.131), channel_id=1, source_target_pairs={{0,8},{8,0},{16,24},{24,16},{1,9},{9,1},{17,25},{25,17},{2,10},{10... | collective-permute-start | bytes 3145736 | tf_op jit(solution)/shard_map/ppermute | solution.py:304
  1270.1 98.6 %collective-permute-start.75 = (bf16[256,2048]{0,1:T(8,128)(2,1)}, bf16[256,2048]{0,1:T(8,128)(2,1)}, u32[]{:S(2)}, u32[]{:S(2)}) collective-permute-start(bf16[256,2048]{0,1:T(8,128)(2,1)} %add_convert_fusion.6), channel_id=1, source_target_pairs={{0,16},{8,24},{16,0},{24,8},{1,17},{9,25},{17,1},{25,9},{2,18},{10... | collective-permute-start | bytes 3145736 | tf_op jit(solution)/shard_map/ppermute | solution.py:304
  1272.5 45.0 %collective-permute-start.92 = (bf16[256,2048]{0,1:T(8,128)(2,1)}, bf16[256,2048]{0,1:T(8,128)(2,1)S(1)}, u32[]{:S(2)}, u32[]{:S(2)}) collective-permute-start(bf16[256,2048]{0,1:T(8,128)(2,1)} %add_convert_fusion.5), channel_id=1, source_target_pairs={{0,16},{8,24},{16,0},{24,8},{1,17},{9,25},{17,1},{25,9},{2,18},{10... | collective-permute-start | bytes 3145736 | tf_op jit(solution)/shard_map/ppermute | solution.py:304
  1275.1 93.0 %collective-permute-start.152 = (bf16[256,2816]{1,0:T(8,128)(2,1)}, bf16[256,2816]{1,0:T(8,128)(2,1)}, u32[]{:S(2)}, u32[]{:S(2)}) collective-permute-start(bf16[256,2816]{1,0:T(8,128)(2,1)} %add_convert_fusion), channel_id=1, source_target_pairs={{0,16},{8,24},{16,0},{24,8},{1,17},{9,25},{17,1},{25,9},{2,18},{10... | collective-permute-start | bytes 4325384 | tf_op jit(solution)/shard_map/ppermute | solution.py:304
  1279.3 89.3 %collective-permute-start.105 = (bf16[256,1024]{0,1:T(8,128)(2,1)}, bf16[256,1024]{0,1:T(8,128)(2,1)}, u32[]{:S(2)}, u32[]{:S(2)}) collective-permute-start(bf16[256,1024]{0,1:T(8,128)(2,1)} %add_convert_fusion.7), channel_id=1, source_target_pairs={{0,16},{8,24},{16,0},{24,8},{1,17},{9,25},{17,1},{25,9},{2,18},{10... | collective-permute-start | bytes 1572872 | tf_op jit(solution)/shard_map/ppermute | solution.py:304
  1322.6 39.6 %collective-permute-start.94 = (f32[232,128]{1,0:T(8,128)S(1)}, f32[232,128]{1,0:T(8,128)S(1)}, u32[]{:S(2)}, u32[]{:S(2)}) collective-permute-start(f32[232,128]{1,0:T(8,128)S(1)} %fusion.50), channel_id=1, source_target_pairs={{0,16},{8,24},{16,0},{24,8},{1,17},{9,25},{17,1},{25,9},{2,18},{10... | collective-permute-start | bytes 356360 | tf_op jit(solution)/shard_map/ppermute | solution.py:304
  (216 other events, 3924.8 us)

commit v2 on v1

v2 whole, which is shorter than its diff:
```python
import copy
from functools import partial

import jax
import jax.numpy as jnp
import numpy as np
from jax import lax
from jax.experimental import pallas as pl
from jax.experimental.pallas import tpu as pltpu
from jax.sharding import PartitionSpec as P

EPS = 1e-06
BF = jnp.bfloat16
F32 = jnp.float32
NN = (((1,), (0,)), ((), ()))
NT = (((1,), (1,)), ((), ()))
TN = (((0,), (0,)), ((), ()))


def one_pass(left, right, dims=NN):
    return lax.dot_general(left.astype(BF), right.astype(BF), dims, preferred_element_type=F32)


def halves(value):
    high = value.astype(BF)
    return high, (value - high.astype(F32)).astype(BF)


def three_pass(left, right, dims=NN):
    lh, ll = left if isinstance(left, tuple) else halves(left)
    rh, rl = right if isinstance(right, tuple) else halves(right)
    total = lax.dot_general(lh, rh, dims, preferred_element_type=F32)
    total = total + lax.dot_general(lh, rl, dims, preferred_element_type=F32)
    return total + lax.dot_general(ll, rh, dims, preferred_element_type=F32)


def layout(length_of, count, rows):
    col = lax.broadcasted_iota(jnp.int32, (rows, 1), 0)
    row = lax.broadcasted_iota(jnp.int32, (1, rows), 1)
    bound = jnp.int32(0)
    start_col = jnp.zeros_like(col)
    start_row = jnp.zeros_like(row)
    for at in range(count):
        bound = bound + length_of(at)
        start_col = jnp.where(col >= bound, bound, start_col)
        start_row = jnp.where(row >= bound, bound, start_row)
    same = start_col == start_row
    within = same & (col >= row)
    strict = same & (col > row)
    return col, row, col - start_col, within, strict


def conv_sum(pre, taps, offset):
    total = pre * taps[0:1]
    for by in range(1, taps.shape[0]):
        moved = jnp.where(offset >= by, pltpu.roll(pre, by, 0), 0.0)
        total = total + moved * taps[by : by + 1]
    return total


def to_row(column, eye):
    return jnp.sum(jnp.where(eye, column, 0.0), axis=0, keepdims=True)


def lane_of(block, lane):
    lanes = lax.broadcasted_iota(jnp.int32, block.shape, 1)
    return jnp.sum(jnp.where(lanes == lane, block, 0.0), axis=1, keepdims=True)


def softplus(value):
    return jnp.maximum(value, 0.0) + jnp.log1p(jnp.exp(-jnp.abs(value)))


def head_parts(pre_ref, taps_ref, small, head, local, heads_local, head_size, heads_all, decay_log, decay_bias, geo):
    col, row, offset, within, strict, eye = geo
    width = heads_local * head_size
    at = lambda part: slice(part * width + local * head_size, part * width + (local + 1) * head_size)
    pres = [pre_ref[:, at(part)] for part in range(3)]
    taps = [taps_ref[:, at(part)] for part in range(3)]
    sums = [conv_sum(p, t, offset) for p, t in zip(pres, taps)]
    sigs = [jax.nn.sigmoid(s) for s in sums]
    convs = [s * g for s, g in zip(sums, sigs)]
    scale_q = lax.rsqrt(jnp.sum(convs[0] * convs[0], axis=1, keepdims=True) + EPS)
    scale_k = lax.rsqrt(jnp.sum(convs[1] * convs[1], axis=1, keepdims=True) + EPS)
    query = (convs[0] * scale_q * head_size**-0.5).astype(BF)
    key = (convs[1] * scale_k).astype(BF)
    value = convs[2].astype(BF)
    shifted = lane_of(small, head) + decay_bias
    beta = jax.nn.sigmoid(lane_of(small, heads_all + head))
    rate = -jnp.exp(jnp.full_like(shifted, decay_log))
    decay = rate * softplus(shifted)
    reach = jnp.where(within, to_row(decay, eye), 0.0)
    total_col = jnp.sum(reach, axis=1, keepdims=True)
    total_row = to_row(total_col, eye)
    fall = jnp.where(within, jnp.exp(jnp.where(within, total_col - total_row, 0.0)), 0.0)
    fall_strict = jnp.where(strict, fall, 0.0)
    keys = lax.dot_general(key, key, NT, preferred_element_type=F32)
    scores = lax.dot_general(query, key, NT, preferred_element_type=F32)
    return dict(pres=pres, taps=taps, sums=sums, sigs=sigs, convs=convs, scale_q=scale_q, scale_k=scale_k,
                query=query, key=key, value=value, shifted=shifted, beta=beta, rate=rate, decay=decay,
                fall=fall, fall_strict=fall_strict, keys=keys, scores=scores,
                gate=pre_ref[:, at(3)])


def two_pass(left, right, dims=NN):
    high, low = halves(left)
    return lax.dot_general(high, right, dims, preferred_element_type=F32) + lax.dot_general(
        low, right, dims, preferred_element_type=F32
    )


def unit_inverses(lowers):
    half = lowers[0].shape[0] // 2
    col = lax.broadcasted_iota(jnp.int32, (half, half), 0)
    row = lax.broadcasted_iota(jnp.int32, (half, half), 1)
    both = jnp.where(col > row, col ^ row, 0)
    eye = (col == row).astype(F32)
    blocks = [low[at : at + half, at : at + half] for low in lowers for at in (0, half)]
    inverses = [eye - jnp.where(both == 1, block, 0.0) for block in blocks]
    reach = 2
    while reach < half:
        corner = (both >= reach) & (both < 2 * reach)
        small = [inverse.astype(BF) for inverse in inverses]
        steps = [one_pass(jnp.where(corner, block, 0.0), inverse) for block, inverse in zip(blocks, small)]
        inverses = [inverse - one_pass(s, step) for inverse, s, step in zip(inverses, small, steps)]
        reach *= 2
    small = [inverse.astype(BF) for inverse in inverses]
    steps = [one_pass(low[half:, :half], small[2 * at]) for at, low in enumerate(lowers)]
    corners = [one_pass(small[2 * at + 1], step) for at, step in enumerate(steps)]
    zero = jnp.zeros((half, half), BF)
    return [
        jnp.concatenate(
            [
                jnp.concatenate([small[2 * at], zero], axis=1),
                jnp.concatenate([(-corner).astype(BF), small[2 * at + 1]], axis=1),
            ],
            axis=0,
        )
        for at, corner in enumerate(corners)
    ]


def solve(lower, inverse, right, dims=NN):
    result = one_pass(inverse, right, dims)
    return result + one_pass(inverse, right - result - three_pass(lower, result, dims), dims)


def forward_kernel(cfg, step, rank_ref, len_ref, log_ref, bias_ref, pre_ref, taps_ref, gain_ref, *refs):
    heads_local, head_size, heads_all, dot_use = cfg
    rows = pre_ref.shape[0]
    gated_ref, inv_ref = refs[-2:]
    col, row, offset, within, strict = layout(lambda at: len_ref[step, at], len_ref.shape[1], rows)
    eye = col == row
    geo = (col, row, offset, within, strict, eye)
    small = pre_ref[:, 4 * heads_local * head_size :]
    parts = []
    for local in range(heads_local):
        head = rank_ref[0] * heads_local + local
        parts.append(head_parts(pre_ref, taps_ref, small, head, local, heads_local, head_size, heads_all, log_ref[head], bias_ref[head], geo))
    lowers = [p["beta"] * p["fall_strict"] * p["keys"] for p in parts]
    inverses = unit_inverses(lowers)
    for local, (p, lower, inverse) in enumerate(zip(parts, lowers, inverses)):
        inv_ref[0, local] = inverse
        update = solve(lower, inverse, p["beta"] * p["value"].astype(F32))
        mixed = dot_use(p["scores"] * p["fall"], update)
        scale = lax.rsqrt(jnp.mean(mixed * mixed, axis=1, keepdims=True) + EPS)
        gate = p["gate"]
        out = mixed * scale * gain_ref[...] * (gate * jax.nn.sigmoid(gate))
        gated_ref[:, local * head_size : (local + 1) * head_size] = out.astype(BF)


def backward_kernel(cfg, step, rank_ref, len_ref, log_ref, bias_ref, pre_ref, taps_ref, gain_ref, inv_ref, own_ref, near_ref, far_ref, *refs):
    heads_local, head_size, heads_all, dot_use = cfg
    rows = pre_ref.shape[0]
    dpre_ref, dtaps_ref, dgain_ref, ddecay_ref = refs[-4:]
    for sum_ref, at in zip((dtaps_ref, dgain_ref, ddecay_ref), range(1, 4)):
        sum_ref[...] = refs[at][...] if step else jnp.zeros_like(sum_ref)

    col, row, offset, within, strict = layout(lambda at: len_ref[step, at], len_ref.shape[1], rows)
    eye = col == row
    geo = (col, row, offset, within, strict, eye)
    width = heads_local * head_size
    small = pre_ref[:, 4 * width :]
    dsmall = jnp.zeros_like(small)
    lanes = lax.broadcasted_iota(jnp.int32, small.shape, 1)
    row_lanes = lax.broadcasted_iota(jnp.int32, (1, ddecay_ref.shape[1]), 1)
    for local in range(heads_local):
        head = rank_ref[0] * heads_local + local
        p = head_parts(pre_ref, taps_ref, small, head, local, heads_local, head_size, heads_all, log_ref[head], bias_ref[head], geo)
        at = lambda part: slice(part * width + local * head_size, part * width + (local + 1) * head_size)
        query, key, value, beta = p["query"], p["key"], p["value"], p["beta"]
        value_f = value.astype(F32)
        inverse = inv_ref[0, local]
        spread_keys = p["fall_strict"] * p["keys"]
        lower = beta * spread_keys
        update = solve(lower, inverse, beta * value_f)
        attn = p["scores"] * p["fall"]
        mixed = dot_use(attn, update)
        lanes_of = slice(local * head_size, (local + 1) * head_size)
        grad = own_ref[:, lanes_of].astype(F32) + near_ref[:, lanes_of].astype(F32) + far_ref[:, lanes_of].astype(F32)
        gate, gain = p["gate"], gain_ref[...]
        sig = jax.nn.sigmoid(gate)
        opened = gate * sig
        scale = lax.rsqrt(jnp.mean(mixed * mixed, axis=1, keepdims=True) + EPS)
        normed = mixed * scale
        dgate = grad * normed * gain * (sig * (1.0 + gate * (1.0 - sig)))
        dgain_ref[...] += jnp.sum(grad * opened * normed, axis=0, keepdims=True)
        dnormed = grad * opened * gain
        dmixed = scale * (dnormed - normed * jnp.mean(dnormed * normed, axis=1, keepdims=True))
        dupdate = dot_use(attn, dmixed, TN)
        dattn = jnp.where(within, dot_use(dmixed, update, NT), 0.0)
        dright = solve(lower, inverse, dupdate, TN)
        dlower = jnp.where(strict, -dot_use(dright, update, NT), 0.0)
        dvalue = beta * dright
        dbeta = jnp.sum(dright * value_f, axis=1, keepdims=True) + jnp.sum(dlower * spread_keys, axis=1, keepdims=True)
        dscores = dattn * p["fall"]
        dkeys = dlower * beta * p["fall_strict"]
        dquery = two_pass(dscores, key)
        dkey = two_pass(dscores, query, TN) + two_pass(dkeys, key) + two_pass(dkeys, key, TN)
        pairs = dattn * attn + dlower * lower
        dtotal_row = to_row(jnp.sum(pairs, axis=1, keepdims=True), eye) - jnp.sum(pairs, axis=0, keepdims=True)
        later = (col <= row) & (col - offset == row_start(row, len_ref, step))
        ddecay = jnp.sum(jnp.where(later, dtotal_row, 0.0), axis=1, keepdims=True)
        dshifted = ddecay * p["rate"] * jax.nn.sigmoid(p["shifted"])
        dlog = jnp.sum(ddecay * p["decay"], axis=0, keepdims=True)
        dbias = jnp.sum(dshifted, axis=0, keepdims=True)
        ddecay_ref[0:1] += jnp.where(row_lanes == head, dlog, 0.0)
        ddecay_ref[1:2] += jnp.where(row_lanes == head, dbias, 0.0)
        dsmall = dsmall + jnp.where(lanes == head, dshifted, 0.0)
        dsmall = dsmall + jnp.where(lanes == heads_all + head, dbeta * beta * (1.0 - beta), 0.0)
        rounded = [g.astype(BF).astype(F32) for g in (dquery, dkey, dvalue)]
        cq, ck = p["convs"][0], p["convs"][1]
        gq = rounded[0] * head_size**-0.5
        dconvs = [
            p["scale_q"] * (gq - cq * (p["scale_q"] * p["scale_q"] * jnp.sum(gq * cq, axis=1, keepdims=True))),
            p["scale_k"] * (rounded[1] - ck * (p["scale_k"] * p["scale_k"] * jnp.sum(rounded[1] * ck, axis=1, keepdims=True))),
            rounded[2],
        ]
        for part in range(3):
            sig_c, total, taps, pre = p["sigs"][part], p["sums"][part], p["taps"][part], p["pres"][part]
            dsum = dconvs[part] * (sig_c * (1.0 + total * (1.0 - sig_c)))
            dpre = dsum * taps[0:1]
            dtaps_ref[0:1, at(part)] += jnp.sum(dsum * pre, axis=0, keepdims=True)
            for by in range(1, taps.shape[0]):
                kept = jnp.where(offset >= by, dsum, 0.0)
                dtaps_ref[by : by + 1, at(part)] += jnp.sum(kept * pltpu.roll(pre, by, 0), axis=0, keepdims=True)
                dpre = dpre + pltpu.roll(kept, rows - by, 0) * taps[by : by + 1]
            dpre_ref[:, at(part)] = dpre.astype(BF)
        dpre_ref[:, at(3)] = dgate.astype(BF)
    dpre_ref[:, 4 * width :] = dsmall.astype(BF)


def row_start(row, len_ref, step):
    bound = jnp.int32(0)
    start = jnp.zeros_like(row)
    for at in range(len_ref.shape[1]):
        bound = bound + len_ref[step, at]
        start = jnp.where(row >= bound, bound, start)
    return start


def mixer_forward(at, rank, lengths, decay_log, decay_bias, pre, taps, gain, heads_local, made):
    buffers = lengths.shape[0]
    rows = pre.shape[0] // buffers
    head_size = gain.shape[1]
    cfg = (heads_local, head_size, decay_log.shape[0], three_pass)
    smem = pl.BlockSpec(memory_space=pltpu.SMEM)
    entire = lambda a: pl.BlockSpec(a.shape, lambda i, rank: (0,) * a.ndim)
    by_rows = lambda cols: pl.BlockSpec((rows, cols), lambda i, rank: (at ^ rank[0], 0))
    width = heads_local * head_size
    return pl.pallas_call(
        partial(forward_kernel, cfg, at),
        grid_spec=pltpu.PrefetchScalarGridSpec(
            num_scalar_prefetch=1,
            grid=(1,),
            in_specs=[smem, smem, smem, by_rows(pre.shape[1]), entire(taps), entire(gain)]
            + [pl.BlockSpec(memory_space=pl.ANY)] * len(made),
            out_specs=[by_rows(width), pl.BlockSpec((1, heads_local, rows, rows), lambda i, rank: (at ^ rank[0], 0, 0, 0))],
        ),
        out_shape=[jax.ShapeDtypeStruct((buffers * rows, width), BF),
                   jax.ShapeDtypeStruct((buffers, heads_local, rows, rows), BF)],
        input_output_aliases={7 + n: n for n in range(len(made))},
        compiler_params=pltpu.CompilerParams(vmem_limit_bytes=48 << 20),
        cost_estimate=pl.CostEstimate(flops=int(19e6), bytes_accessed=1 << 10, transcendentals=0),
        name="mixer_forward",
    )(rank, lengths, decay_log, decay_bias, pre, taps, gain, *made)


def mixer_backward(at, rank, lengths, decay_log, decay_bias, pre, taps, gain, inverse, grads, heads_local, made):
    buffers = lengths.shape[0]
    rows = pre.shape[0] // buffers
    head_size = gain.shape[1]
    cfg = (heads_local, head_size, decay_log.shape[0], three_pass)
    smem = pl.BlockSpec(memory_space=pltpu.SMEM)
    entire = lambda s: pl.BlockSpec(s, lambda i, rank: (0,) * len(s))
    by_rows = lambda a: pl.BlockSpec((rows, a.shape[1]), lambda i, rank: (at ^ rank[0], 0))
    sums = [entire(taps.shape), entire(gain.shape), entire((8, 128))]
    return pl.pallas_call(
        partial(backward_kernel, cfg, at),
        grid_spec=pltpu.PrefetchScalarGridSpec(
            num_scalar_prefetch=1,
            grid=(1,),
            in_specs=[smem, smem, smem, by_rows(pre), entire(taps.shape), entire(gain.shape),
                      pl.BlockSpec((1, heads_local, rows, rows), lambda i, rank: (at ^ rank[0], 0, 0, 0)),
                      *[by_rows(g) for g in grads]]
            + ([pl.BlockSpec(memory_space=pl.ANY)] + sums if made else []),
            out_specs=[by_rows(pre)] + sums,
        ),
        out_shape=[jax.ShapeDtypeStruct(pre.shape, BF), jax.ShapeDtypeStruct(taps.shape, F32),
                   jax.ShapeDtypeStruct(gain.shape, F32), jax.ShapeDtypeStruct((8, 128), F32)],
        input_output_aliases={11: 0} if made else {},
        compiler_params=pltpu.CompilerParams(vmem_limit_bytes=48 << 20),
        cost_estimate=pl.CostEstimate(flops=int(12e6), bytes_accessed=1 << 10, transcendentals=0),
        name="mixer_backward",
    )(rank, lengths, decay_log, decay_bias, pre, taps, gain, inverse, *grads, *made)


def dot(left, right, dims=NN):
    return lax.dot_general(left, right, dims, preferred_element_type=F32)


ANY = pl.BlockSpec(memory_space=pl.ANY)
LIMIT = 56 << 20
INV, OWN, RANK = 0, 1, 2


def whole(array):
    return pl.BlockSpec(array.shape, lambda i, info: (0,) * array.ndim)


def to_col(row, eye):
    return jnp.sum(jnp.where(eye, row, 0.0), axis=1, keepdims=True)


def diagonal(rows):
    return lax.broadcasted_iota(jnp.int32, (rows, rows), 0) == lax.broadcasted_iota(jnp.int32, (rows, rows), 1)


class Pieces:
    def __init__(self, parts, rows, first=0, columns=None):
        self.arrays, self.starts = [a for a, _ in parts], [jnp.asarray(s, jnp.int32) for _, s in parts]
        self.first, self.shape = first, (rows, columns or parts[0][0].shape[1])

    def copies(self, info, base, sources, target, sem, sem_base):
        made = []
        for at, source in enumerate(sources):
            rows, cols = source.shape[0], self.shape[1]
            source = source.at[:, pl.ds(self.first, cols)]
            place = target.at[pl.ds(pl.multiple_of(info[base + at], 16), rows)]
            made.append(pltpu.make_async_copy(source, place, sem.at[sem_base + at]))
        return made


def kernel_call(body, name, cost, grid, info, ins, weights, outs, scratch=(), onto=()):
    lead = len(info)
    scalars = jnp.stack([jnp.asarray(v, jnp.int32) for v in info] + [s for w in weights for s in w.starts])
    counts = [len(w.arrays) for w in weights]
    total = sum(counts)

    def kernel(info_ref, *refs):
        in_refs, refs = refs[: len(ins)], refs[len(ins) :]
        piece_refs, refs = refs[:total], refs[total:]
        refs = refs[len(onto) :]
        out_refs, refs = refs[: len(outs)], refs[len(outs) :]
        full_refs, refs = refs[: len(weights)], refs[len(weights) :]
        extra = refs[: len(scratch)]
        if total:
            sem = refs[len(scratch)]

            @pl.when(pl.program_id(0) == 0)
            def _():
                made, at = [], 0
                for w, full, count in zip(weights, full_refs, counts):
                    made += w.copies(info_ref, lead + at, piece_refs[at : at + count], full, sem, at)
                    at += count
                for move in made:
                    move.start()
                for move in made:
                    move.wait()

        body(info_ref, in_refs, full_refs, out_refs, extra)

    return pl.pallas_call(
        kernel,
        grid_spec=pltpu.PrefetchScalarGridSpec(
            num_scalar_prefetch=1,
            grid=grid,
            in_specs=[spec for _, spec in ins] + [ANY] * (total + len(onto)),
            out_specs=[spec for _, _, spec in outs],
            scratch_shapes=[pltpu.VMEM(w.shape, BF) for w in weights]
            + list(scratch)
            + ([pltpu.SemaphoreType.DMA((total,))] if total else []),
        ),
        out_shape=[jax.ShapeDtypeStruct(shape, kind) for shape, kind, _ in outs],
        input_output_aliases={1 + len(ins) + total + at: at for at in range(len(onto))},
        compiler_params=pltpu.CompilerParams(vmem_limit_bytes=LIMIT),
        cost_estimate=estimate(cost),
        name=name,
    )(scalars, *[a for a, _ in ins], *[p for w in weights for p in w.arrays], *onto)


COST = 1e6


def estimate(micros):
    return pl.CostEstimate(flops=int(micros * COST), bytes_accessed=1 << 10, transcendentals=0)


def program(shards, ranks):
    ring = shards // 2
    by_line = ring == 4

    def after(value, *others):
        return lax.optimization_barrier((value,) + others)[0] if others else value

    last = {}

    def send(lane, value, axis, pairs):
        sent = lax.ppermute(after(value, *last.get(lane, ())), axis, pairs)
        last[lane] = (sent,)
        return sent

    def pair(value):
        return send("pair", value, "fsdp", [(f, f ^ 1) for f in range(shards)])

    def across(value, bits):
        return send(("rank", min(bits, 2)), value, "replica", [(r, r ^ bits) for r in range(ranks)])

    def hop(value, by, sources):
        return send(by, value, "fsdp", [(2 * at + y, 2 * (at + by) + y) for at in sources for y in range(2)])

    def gather(piece, z, y, *ahead):
        got = [(piece, z * 2 + y)]

        def exchange(value, at):
            other = pair(value)
            got.extend([(value, at * 2 + y), (other, at * 2 + (y ^ 1))] if at is not z else [(other, at * 2 + (y ^ 1))])
            return other

        up1, down1 = hop(piece, 1, (0, 1, 2)), hop(piece, -1, (1, 2, 3))
        other = exchange(piece, z)
        up2, down2 = hop(after(up1, other, *ahead), 1, (1, 2)), hop(after(down1, other, *ahead), -1, (1, 2))
        other = exchange(jnp.where(z == 3, up1, down1), jnp.where(z == 3, 2, z + 1))
        up3, down3 = hop(after(up2, other), 1, (2,)), hop(after(down2, other), -1, (1,))
        exchange(jnp.where(z >= 2, up2, down2), (z + 2) % 4)
        far = jnp.where(z == 0, down3, jnp.where(z == 3, up3, up1))
        exchange(far, jnp.where(z == 0, 3, jnp.where(z == 3, 0, z - 1)))
        return got

    def gather_whole(piece):
        return lax.all_gather(piece, "fsdp", axis=0, tiled=True)

    def plus(*terms):
        total = terms[0].astype(F32)
        for term in terms[1:]:
            total = total + term.astype(F32)
        return total.astype(BF)

    def line_sum(part):
        up = down = None
        for k in range(1, 4):
            up = hop(plus(part(4 - k), *([] if up is None else [up])), 1, range(k))
            down = hop(plus(part(k), *([] if down is None else [down])), -1, range(4 - k, 4))
        return [up, down]

    def scatter_whole(value):
        return lax.psum_scatter(value, "fsdp", scatter_dimension=0, tiled=True)

    def scatter(part):
        given = pair(jnp.stack([part(dz, 1) for dz in range(4)]))
        return lambda *events: finish([plus(after(part(dz, 0), *events), given[dz]) for dz in range(4)])

    def finish(summed):
        return plus(summed[0], *line_sum(lambda dz: summed[dz]))

    def scatter_along(value):
        lines = [[2 * at + y for at in range(ring)] for y in range(2)]
        flat = value.reshape((-1,) + value.shape[2:])
        return lax.psum_scatter(flat, "fsdp", scatter_dimension=0, tiled=True, axis_index_groups=lines)

    def gather_group(value):
        two = across(value, 2)
        return [value, across(value, 1), two, across(two, 1)]

    def scatter_group(parts):
        far = across(plus(parts[2], across(parts[3], 1)), 2)
        return parts[0], across(parts[1], 1), far

    def by_rank(pieces, rank):
        low, high = rank % 2 == 1, rank // 2 == 1
        a, b, c, d = pieces
        a, b, c, d = (jnp.where(low, *p) for p in ((b, a), (a, b), (d, c), (c, d)))
        return [jnp.where(high, *p) for p in ((c, a), (d, b), (a, c), (b, d))]

    def on_device(
        tokens, seq_lengths, attn_gain, w_query, w_key, w_value, w_outgate, w_alpha, w_beta, conv_weight,
        decay_log, decay_bias, head_gain, w_output, mlp_gain, w_gate, w_up, w_down, cotangent,
    ):
        rows, model = tokens.shape
        heads = decay_log.shape[0]
        heads_local = heads // ranks
        width = model // ranks
        piece_rows = w_query.shape[0]
        hidden_piece = w_down.shape[0] // ranks
        hidden_cols = shards * hidden_piece
        taps_count = conv_weight.shape[0]
        buffers = ranks
        group = buffers * rows
        rank = lax.axis_index("replica")
        place = lax.axis_index("fsdp")
        z, y = place // 2, place % 2

        def owner(dz, dy):
            return ((z + dz) % ring) * 2 + (y ^ dy)

        own = lambda w: lax.dynamic_slice_in_dim(w, rank * width, width, axis=1)

        conv_parts = conv_weight.shape[1] // piece_rows
        conv_cols = conv_weight.T.reshape(conv_parts, piece_rows, taps_count)
        conv_cols = jnp.swapaxes(conv_cols, 0, 1).reshape(piece_rows, conv_parts * taps_count)
        small = jnp.concatenate([w_alpha, w_beta, attn_gain[:, None], mlp_gain[:, None], conv_cols], axis=1)
        small = jnp.pad(small, ((0, 0), (0, 128 - small.shape[1])))
        shard_in = jnp.concatenate([own(w_query), own(w_key), own(w_value), own(w_outgate), small, own(w_output)], axis=1)
        hidden = lambda w: lax.dynamic_index_in_dim(
            w.reshape(piece_rows, shards, ranks, hidden_piece), rank, 2, keepdims=False
        ).reshape(piece_rows, hidden_cols)
        shard_gu = jnp.concatenate([hidden(w_gate), hidden(w_up)], axis=1)
        shard_d = lax.dynamic_slice_in_dim(w_down, rank * hidden_piece, hidden_piece, axis=0)

        live = (jnp.arange(rows, dtype=jnp.int32) < jnp.sum(seq_lengths[0])).astype(F32)[:, None]
        note = jnp.pad(seq_lengths.astype(BF), ((0, 15), (0, model - seq_lengths.shape[1])))
        tokens_noted = jnp.concatenate([tokens, note], axis=0)
        upstream_own = cotangent * live.astype(BF)

        token_slots = gather_group(tokens_noted)
        whole_in = gather_whole(shard_in)
        upstream_slots = gather_group(upstream_own)
        lengths = jnp.stack([t[rows, : seq_lengths.shape[1]] for t in token_slots]).astype(jnp.int32)
        if by_line:
            got_d = [(piece, f * hidden_piece) for piece, f in gather(shard_d, z, y, token_slots[2])]
        else:
            got_d = [(gather_whole(shard_d), 0)]
        ahead = [*token_slots[1:], *upstream_slots[1:], *[piece for piece, _ in got_d[1:]]]
        whole_gu = gather_whole(after(shard_gu, whole_in, *ahead))

        in_cols = 4 * width + 128
        full_in = Pieces([(whole_in, 0)], model, 0, in_cols)
        full_out = Pieces([(whole_in, 0)], model, in_cols, width)
        full_gu = Pieces([(whole_gu, 0)], model)
        full_down = Pieces(got_d, hidden_cols)

        info = [rank]
        by_slot = lambda cols: pl.BlockSpec((rows, cols), lambda i, info: (i ^ info[0], 0))
        by_row = lambda cols: pl.BlockSpec((rows, cols), lambda i, info: (i, 0))
        a_row = pl.BlockSpec((1, 1, rows), lambda i, info: (i, 0, 0))
        lanes_of = lambda info, j: pl.ds(pl.multiple_of((info[0] ^ j) * width, 128), width)
        own_lanes = lambda info: lanes_of(info, 0)
        gain_rows = 16

        def enter_body(info, ins, weights, outs, extra):
            (w_ref,) = weights
            x_refs = ins
            pre_ref, normed_ref, x_own_ref, lane_ref = outs
            (x_ref,) = extra
            step = pl.program_id(0)

            @pl.when(step == 0)
            def _():
                picked = lax.broadcasted_iota(jnp.int32, (gain_rows, 128), 0) + 2 * heads
                picked = (picked == lax.broadcasted_iota(jnp.int32, (gain_rows, 128), 1)).astype(BF)
                for first in range(0, model, 256):
                    block = w_ref[first : first + 256, 4 * width :]
                    lane_ref[:, first : first + 256] = dot(picked, block, NT)

            for j in range(len(x_refs)):
                @pl.when(step == j)
                def _():
                    x_ref[...] = x_refs[j][:rows]

            x_own_ref[...] = x_ref[:, own_lanes(info)]
            x = x_ref[...].astype(F32)
            scale = lax.rsqrt(jnp.mean(x * x, axis=1, keepdims=True) + EPS)
            normed = (x * scale * lane_ref[0:1]).astype(BF)
            normed_ref[...] = normed
            pre_ref[...] = dot(normed, w_ref[...])

        slot = pl.BlockSpec((rows, model), lambda i, info: (0, 0))
        entered = []
        for first in (0, 2):
            some = lambda cols: pl.BlockSpec((rows, cols), lambda i, info: ((i + info[1]) ^ info[0], 0))
            entered.append(kernel_call(
                enter_body, "enter", 11, (2,), [rank, first],
                [(x, whole(x)) for x in token_slots[first : first + 2]], [full_in],
                [
                    ((group, in_cols), F32, some(in_cols)), ((group, model), BF, some(model)),
                    ((group, width), BF, some(width)),
                    ((gain_rows, model), F32, pl.BlockSpec((gain_rows, model), lambda i, info: (0, 0))),
                ],
                [pltpu.VMEM((rows, model), BF)], entered[0][:3] if entered else (),
            ))
        pre, normed, x_cols = entered[1][:3]
        lanes = entered[0][3]
        gain_one = lanes[0]
        own_gain = pl.BlockSpec((1, width), lambda i, info: (0, 0))
        gain_two = lax.dynamic_slice_in_dim(lanes[1:2], rank * width, width, axis=1)
        conv_all = lanes[2 : 2 + conv_parts * taps_count].reshape(conv_parts, taps_count, shards, piece_rows)
        conv_all = conv_all.transpose(1, 2, 0, 3).reshape(taps_count, 3, model)
        taps = lax.dynamic_slice_in_dim(conv_all, rank * width, width, axis=2).reshape(taps_count, 3 * width)

        rank_arr = rank[None].astype(jnp.int32)
        made = ()
        for at in range(buffers):
            source = entered[at // 2][0]
            if at == 2:
                source = pre
            made = mixer_forward(
                at, rank_arr, lengths, decay_log, decay_bias, source, taps, head_gain[None], heads_local, made
            )
        gated, inverse = made

        def leave_body(info, ins, weights, outs, extra):
            (w_ref,) = weights
            x_ref, gain_ref = ins[ranks:]
            all_ref, resid_ref, branch_ref, scaled_ref, square_ref = outs
            for j in range(ranks):
                all_ref[:, lanes_of(info, j)] = ins[j][...]
            branch = dot(all_ref[...], w_ref[...])
            resid = x_ref[...].astype(F32) + branch
            resid_ref[...] = resid
            branch_ref[...] = branch
            scaled_ref[...] = (resid * gain_ref[...]).astype(BF)
            square_ref[0] = to_row(jnp.sum(resid * resid, axis=1, keepdims=True), diagonal(rows))

        gated_all, resid, branch, scaled, square = kernel_call(
            leave_body, "leave", 9, (buffers,), info,
            [(g, by_row(width)) for g in gather_group(gated)] + [(x_cols, by_row(width)), (gain_two, own_gain)],
            [full_out],
            [
                ((group, model), BF, by_row(model)), ((group, width), F32, by_row(width)),
                ((group, width), F32, by_row(width)), ((group, width), BF, by_row(width)),
                ((buffers, 1, rows), F32, a_row),
            ],
        )
        squares = gather_group(square)

        def inverse_scale(square_refs):
            total = square_refs[0][0]
            for ref in square_refs[1:]:
                total = total + ref[0]
            return lax.rsqrt(to_col(total, diagonal(rows)) / model + EPS)

        def hidden_body(info, ins, weights, outs, extra):
            w_ref, d_ref = weights
            all_ref, hidden_ref, grad_ref, stat_ref, u_ref, u_own_ref = outs
            for j in range(ranks):
                @pl.when(pl.program_id(0) ^ info[0] == j)
                def _():
                    u_ref[...] = ins[2 * ranks + j][...]

            u_own_ref[...] = u_ref[:, own_lanes(info)]
            for j in range(ranks):
                all_ref[:, lanes_of(info, j)] = ins[j][...]
            inv = inverse_scale(ins[ranks : 2 * ranks])
            raw_gate = dot(all_ref[...], w_ref[:, :hidden_cols])
            raw_up = dot(all_ref[...], w_ref[:, hidden_cols:])
            grad_hidden = dot(u_ref[...], d_ref[...], NT)
            gate, up = raw_gate * inv, raw_up * inv
            sig = jax.nn.sigmoid(gate)
            opened = gate * sig
            hidden_ref[...] = (opened * up).astype(BF)
            grad_hidden = grad_hidden * inv
            grad_gate = (grad_hidden * up * (sig * (1.0 + gate * (1.0 - sig)))).astype(BF)
            grad_up = (grad_hidden * opened).astype(BF)
            grad_ref[:, :hidden_cols] = grad_gate
            grad_ref[:, hidden_cols:] = grad_up
            stat = jnp.sum(raw_gate * grad_gate.astype(F32) + raw_up * grad_up.astype(F32), axis=1, keepdims=True)
            stat_ref[0] = to_row(stat, diagonal(rows))

        scaled_all, hidden_b, grad_gu, stat, upstream, u_cols = kernel_call(
            hidden_body, "hidden", 33, (buffers,), info,
            [(s, by_row(width)) for s in gather_group(scaled)] + [(s, a_row) for s in squares]
            + [(u, slot) for u in upstream_slots],
            [full_gu, full_down],
            [
                ((group, model), BF, by_row(model)), ((group, hidden_cols), BF, by_row(hidden_cols)),
                ((group, 2 * hidden_cols), BF, by_row(2 * hidden_cols)), ((buffers, 1, rows), F32, a_row),
                ((group, model), BF, by_row(model)), ((group, width), BF, by_row(width)),
            ],
        )
        stats = gather_group(stat)

        def back_body(info, ins, weights, outs, extra):
            for j in range(ranks):
                outs[j][...] = dot(ins[0][...], weights[0][lanes_of(info, j)], NT).astype(BF)

        d_gu = dot(scaled_all, grad_gu, TN).astype(BF)
        share_gu = scatter_whole(d_gu)
        parts = kernel_call(
            back_body, "back", 19, (buffers,), info, [(after(grad_gu, d_gu), by_row(2 * hidden_cols))], [full_gu],
            [((group, width), BF, by_row(width))] * ranks,
        )
        terms_two = scatter_group(parts)

        def scattered(value, piece):
            if not by_line:
                return lambda *events: scatter_whole(value)
            return scatter(lambda dz, dy: lax.dynamic_slice_in_dim(value, owner(dz, dy) * piece, piece, axis=0))

        d_down = dot(hidden_b, upstream, TN).astype(BF)
        end_d = scattered(d_down, hidden_piece)

        def turn_body(info, ins, weights, outs, extra):
            (w_ref,) = weights
            own_ref, near_ref, far_ref, resid_ref, u_ref, gain_ref = ins[:6]
            grad_ref, out_refs, gain_out_ref = outs[0], outs[1 : 1 + ranks], outs[1 + ranks]

            @pl.when(pl.program_id(0) == 0)
            def _():
                gain_out_ref[...] = jnp.zeros_like(gain_out_ref)

            grad_two = own_ref[...].astype(F32) + near_ref[...].astype(F32) + far_ref[...].astype(F32)
            resid = resid_ref[...]
            inv = inverse_scale(ins[6 : 6 + ranks])
            total = ins[6 + ranks][0]
            for ref in ins[7 + ranks :]:
                total = total + ref[0]
            stat = to_col(total, diagonal(rows))
            gain_out_ref[...] += jnp.sum(grad_two * resid, axis=0, keepdims=True)
            grad = u_ref[...].astype(F32) + gain_ref[...] * grad_two - resid * (inv * inv * stat / model)
            grad = grad.astype(BF)
            grad_ref[...] = grad
            for j in range(ranks):
                out_refs[j][...] = dot(grad, w_ref[lanes_of(info, j)], NT).astype(BF)

        turned = kernel_call(
            turn_body, "turn", 9, (buffers,), info,
            [(t, by_row(width)) for t in terms_two]
            + [(after(resid, d_down), by_row(width)), (u_cols, by_row(width)), (gain_two, own_gain)]
            + [(s, a_row) for s in squares] + [(s, a_row) for s in stats],
            [full_out],
            [((group, width), BF, by_row(width))] * (1 + ranks) + [((1, width), F32, own_gain)],
        )
        grad_branch, grad_mlp_gain = turned[0], turned[1 + ranks][0]
        terms_gated = scatter_group(turned[1 : 1 + ranks])
        d_out = dot(gated_all, grad_branch, TN).astype(BF)
        own_block = lambda value, j: lax.dynamic_slice_in_dim(value, (rank ^ j) * rows, rows, axis=0)

        def to_tokens(value):
            pieces = [own_block(value, 0)] + [across(own_block(value, j), j) for j in range(1, ranks)]
            return jnp.concatenate(by_rank(pieces, rank), axis=1).astype(F32)

        def down_body(info, ins, weights, outs, extra):
            (full,) = extra
            full[...] = dot(ins[0][...], weights[0][...])
            full[:, own_lanes(info)] += ins[1][...]
            for j in range(ranks):
                @pl.when(pl.program_id(0) == j)
                def _():
                    outs[j][...] = full[...].astype(BF)

        down = kernel_call(
            down_body, "down", 14, (ranks,), info, [(hidden_b, by_slot(hidden_cols)), (branch, by_slot(width))], [full_down],
            [((rows, model), BF, slot)] * ranks, [pltpu.VMEM((rows, model), F32)],
        )
        down_terms = scatter_group(down)
        output = tokens.astype(F32)
        for term in down_terms:
            output = output + term.astype(F32)
        output = (output * live).astype(BF)
        grad_resid_own = to_tokens(grad_branch)

        made = ()
        ahead = [(d_out, *down), (), (down_terms[2],), (grad_resid_own,)]
        for at in range(buffers):
            made = mixer_backward(
                at, rank_arr, lengths, decay_log, decay_bias, after(pre, *ahead[at]), taps, head_gain[None], inverse,
                terms_gated, heads_local, made,
            )
        d_pre, d_taps, d_head_gain, d_decay = made
        cuts = ((0, 2 * width), (2 * width, 2 * width + 128))
        d_in = [dot(normed, d_pre[:, first : first + count], TN).astype(BF) for first, count in cuts]
        in_sums = []
        for value in d_in:
            if by_line:
                placed = value.reshape(ring, 2, piece_rows, value.shape[1])
                given = pair(lax.dynamic_index_in_dim(placed, 1 - y, 1, keepdims=False))
                in_sums.append(plus(lax.dynamic_index_in_dim(placed, y, 1, keepdims=False), given))
            else:
                in_sums.append(value)
        along = scatter_along if by_line else scatter_whole
        share_a = along(after(in_sums[0], share_gu))
        share_b = along(after(in_sums[1], share_a))
        end_o = scattered(d_out, piece_rows)

        def first_body(info, ins, weights, outs, extra):
            result = dot(ins[0][...], weights[0][...], NT).astype(BF)
            for j in range(ranks):
                @pl.when(pl.program_id(0) == j)
                def _():
                    outs[j][...] = result

        grad_slots = kernel_call(
            first_body, "first", 19, (ranks,), info, [(after(d_pre, *d_in), by_slot(in_cols))], [full_in],
            [((rows, model), BF, slot)] * ranks,
        )
        grad_one = sum(t.astype(F32) for t in scatter_group(grad_slots))
        gu_slots = gather_group(share_gu)
        share_d = end_d(grad_slots[0], down[0])
        share_o = end_o(grad_slots[0], down[0])
        d_slots, o_slots = gather_group(share_d), gather_group(share_o)
        x_own = tokens.astype(F32)
        inv_one = lax.rsqrt(jnp.mean(x_own * x_own, axis=-1, keepdims=True) + EPS)
        grad_attn_gain = jnp.sum(grad_one * x_own * inv_one, axis=0)
        pulled = gain_one * grad_one
        grad_x = inv_one * pulled - x_own * (inv_one**3 * jnp.mean(pulled * x_own, axis=-1, keepdims=True))
        grad_tokens = (grad_resid_own + grad_x).astype(BF)

        own_cols = lambda value: lax.dynamic_update_slice_in_dim(
            jnp.zeros(value.shape[:-1] + (model,), F32), value, rank * width, axis=value.ndim - 1
        )
        packed = jnp.concatenate(
            [
                own_cols(d_taps.reshape(taps_count, 3, width)).reshape(-1),
                own_cols(grad_mlp_gain),
                grad_attn_gain,
                d_head_gain[0],
                d_decay[0, :heads],
                d_decay[1, :heads],
            ]
        )
        total = jnp.pad(packed, (0, -packed.size % 1024)).reshape(-1, 128)
        for bits in (1, 2):
            total = total + lax.ppermute(total, "replica", [(r, r ^ bits) for r in range(ranks)])
        bits = 1
        while bits < shards:
            total = total + lax.ppermute(total, "fsdp", [(f, f ^ bits) for f in range(shards)])
            bits *= 2
        total = total.reshape(-1)
        conv_size = taps_count * 3 * model
        sum_conv = total[:conv_size].reshape(taps_count, shards, -1)
        sum_conv = lax.dynamic_index_in_dim(sum_conv, place, 1, keepdims=False)
        at = conv_size
        sum_mlp_gain = lax.dynamic_slice_in_dim(total, at + place * piece_rows, piece_rows)
        sum_attn_gain = lax.dynamic_slice_in_dim(total, at + model + place * piece_rows, piece_rows)
        at += 2 * model
        sum_head_gain = total[at : at + head_gain.size]
        at += head_gain.size
        sum_log, sum_bias = total[at : at + heads], total[at + heads : at + 2 * heads]

        gu_all = by_rank(gu_slots, rank)
        unhide = lambda first: (
            jnp.stack([p[:, first : first + hidden_cols].reshape(piece_rows, shards, hidden_piece) for p in gu_all], axis=2)
            .reshape(piece_rows, shards * ranks * hidden_piece)
            .astype(F32)
        )
        out_gate, out_up = unhide(0), unhide(hidden_cols)
        out_down = jnp.concatenate(by_rank(d_slots, rank), axis=0).astype(F32)
        out_output = jnp.concatenate(by_rank(o_slots, rank), axis=1).astype(F32)
        a_all = by_rank(gather_group(share_a), rank)
        out_query, out_key = (
            jnp.concatenate([p[:, at * width : (at + 1) * width] for p in a_all], axis=1).astype(F32) for at in range(2)
        )
        finished = (out_gate, out_up, out_down, out_output, output, grad_tokens, sum_conv, out_query, out_key)
        share_b, *finished = lax.optimization_barrier((share_b, *finished))
        out_gate, out_up, out_down, out_output, output, grad_tokens, sum_conv, out_query, out_key = finished
        b_slots = gather_group(share_b)
        b_all = by_rank(b_slots, rank)
        out_value, out_outgate = (
            jnp.concatenate([p[:, at * width : (at + 1) * width] for p in b_all], axis=1).astype(F32) for at in range(2)
        )
        low = [p[:, 2 * width :].astype(F32) for p in b_slots]
        low = (low[0] + low[1]) + (low[2] + low[3])
        out_alpha, out_beta = low[:, :heads], low[:, heads : 2 * heads]
        return (
            output, grad_tokens, sum_attn_gain, out_query, out_key, out_value, out_outgate, out_alpha, out_beta,
            sum_conv, sum_log, sum_bias, sum_head_gain, out_output, sum_mlp_gain, out_gate, out_up, out_down,
        )

    return on_device


def solution(mesh):
    rows, cols = P("fsdp", None), P("fsdp")
    tokens = P(("replica", "fsdp"), None)
    return jax.shard_map(
        program(mesh.shape["fsdp"], mesh.shape["replica"]),
        mesh=mesh,
        in_specs=(
            tokens, tokens, cols, rows, rows, rows, rows, rows, rows, P(None, "fsdp"), P(), P(), P(), rows, cols,
            rows, rows, rows, tokens,
        ),
        out_specs=(
            tokens, tokens, cols, rows, rows, rows, rows, rows, rows, P(None, "fsdp"), P(), P(), P(), rows, cols,
            rows, rows, rows,
        ),
        check_vma=False,
    )
```

time: 1450 us -> 954 us (0.66)
  local copies, waits for them, and re-layouts: 264 us -> 103 us
  starting transfers between devices: 256 us -> 114 us
  matrix products: 190 us -> 49.4 us
  Pallas kernels: 124 us -> 235 us
  waiting for transfers between devices: 437 us -> 351 us
  other arithmetic: 159 us -> 76.2 us
    dot_general x18 -> x5, matrix products: 190 us -> 49.4 us  [dot(): return lax.dot_general(left, right, dims, preferred_element_type=F32)]
    ppermute x169 -> x76, starting transfers between devices: 253 us -> 113 us  [the longest x74 113 us: send(): sent = lax.ppermute(after(value, *last.get(lane, ())), axis, pairs)]
    ppermute x169 -> x76, waiting for transfers between devices: 435 us -> 301 us  [the longest x74 300 us: send(): sent = lax.ppermute(after(value, *last.get(lane, ())), axis, pairs)]
    pallas_call x2 -> x16, Pallas kernels: 124 us -> 235 us  [the longest x8 135 us: kernel_call(): pl.pallas_call(kernel, grid_spec=pltpu.PrefetchScalarGridSpec(num_scalar_...]
    dynamic_update_slice x63 -> x0, local copies, waits for them, and re-layouts: 91.7 us -> none  [place_rows(): whole = lax.dynamic_update_slice(whole, piece, (row, col))]
    concatenate x7 -> x1, other arithmetic: 67.7 us -> 2.35 us  [on_device(): tokens_noted = jnp.concatenate([tokens, note], axis=0)]
    all_gather x0 -> x2, waiting for transfers between devices: none -> 44.3 us  [gather_whole(): return lax.all_gather(piece, 'fsdp', axis=0, tiled=True)]
    ppermute x21 -> x0, local copies, waits for them, and re-layouts: 35.9 us -> none  [the longest x12 20 us: shift(): lax.ppermute(value, 'fsdp', [(f, (f // 2 + by) % ring * 2 + f % 2) for f...]
  transfers between devices with their start and end apart: 172 -> 84, of which waited for: 55 -> 33; matrix products, arithmetic and copies ran while one was open for 30% -> 19% of each run, Pallas kernels for 9% -> 21%
where the time goes in v2:
time: 954 us; the launch traced here: 945 us
  waiting for transfers between devices  351 us (37%)
  Pallas kernels  235 us (25%)
  starting transfers between devices  114 us (12%)
  local copies, waits for them, and re-layouts  103 us (11%)
  other arithmetic  76.2 us (8%)
  matrix products  49.4 us (5%)
  between operations  15.6 us (2%)
    ppermute x74, waiting for transfers between devices, send(): sent = lax.ppermute(after(value, *last.get(lane, ())), axis, pairs)  300 us
    pallas_call x8, Pallas kernels, kernel_call(): pl.pallas_call(kernel, grid_spec=pltpu.PrefetchScalarGridSpec(num_scalar_...  135 us
    ppermute x74, starting transfers between devices, send(): sent = lax.ppermute(after(value, *last.get(lane, ())), axis, pairs)  113 us
    pallas_call x4, Pallas kernels, mixer_backward(): pl.pallas_call(partial(backward_kernel, cfg, at), grid_spec=pltpu.Prefetc...  64.7 us
    dot_general x5, matrix products, dot(): return lax.dot_general(left, right, dims, preferred_element_type=F32)  49.4 us
    all_gather x2, waiting for transfers between devices, gather_whole(): return lax.all_gather(piece, 'fsdp', axis=0, tiled=True)  44.3 us
    unnamed x188, local copies, waits for them, and re-layouts  43.7 us
    pallas_call x4, Pallas kernels, mixer_forward(): pl.pallas_call(partial(forward_kernel, cfg, at), grid_spec=pltpu.Prefetch...  35.4 us
  transfers between devices with their start and end apart: 84, of which 33 were waited for; matrix products, arithmetic and copies ran while one was open for 19% of the time, Pallas kernels for 21%

profile of v2, /device:TPU:1, one launch (start us, length us, event | category | flops | bytes accessed | tf_op | source)
XLA Modules:
  0.0 945.4 jit_solution(2106221119819272664)
XLA Ops:
  28.1 4.0 collective-permute-start.16
  33.4 17.7 %collective-permute-done.refs_0_ = bf16[272,2048]{1,0:T(8,128)(2,1)} collective-permute-done((bf16[272,2048]{1,0:T(8,128)(2,1)}, bf16[272,2048]{1,0:T(8,128)(2,1)}, u32[]{:S(2)}, u32[]{:S(2)}) %collective-permute-start) | collective-permute-done | bytes 1114144 | tf_op jit(solution)/shard_map/ppermute | solution.py:419
  52.4 16.8 %collective-permute-done.17 = bf16[176,2048]{1,0:T(8,128)(2,1)} collective-permute-done((bf16[176,2048]{1,0:T(8,128)(2,1)}, bf16[176,2048]{1,0:T(8,128)(2,1)}, u32[]{:S(2)}, u32[]{:S(2)}) %collective-permute-start.17) | collective-permute-done | bytes 720928 | tf_op jit(solution)/shard_map/ppermute | solution.py:419
  74.9 4.1 collective-permute-start.4
  78.9 5.6 collective-permute-done.18.refs_16_.refs_5_
  86.9 21.8 %collective-permute-done.20 = bf16[176,2048]{1,0:T(8,128)(2,1)} collective-permute-done((bf16[176,2048]{1,0:T(8,128)(2,1)}, bf16[176,2048]{1,0:T(8,128)(2,1)}, u32[]{:S(2)}, u32[]{:S(2)}) %collective-permute-start.20) | collective-permute-done | bytes 720928 | tf_op jit(solution)/shard_map/ppermute | solution.py:419
  111.4 3.5 collective-permute-start.5
  114.8 59.1 %collective-permute-done.22 = bf16[176,2048]{1,0:T(8,128)(2,1)} collective-permute-done((bf16[176,2048]{1,0:T(8,128)(2,1)}, bf16[176,2048]{1,0:T(8,128)(2,1)}, u32[]{:S(2)}, u32[]{:S(2)}) %collective-permute-start.22) | collective-permute-done | bytes 720928 | tf_op jit(solution)/shard_map/ppermute | solution.py:419
  175.2 4.0 collective-permute-start.24
  179.2 4.6 copy.90
  183.8 4.5 copy.91
  192.3 20.9 %all-gather.3.cloned.1.call-done.refs_2_.refs_6_.refs_14_.refs_1_ = bf16[2048,2688]{1,0:T(8,128)(2,1)} async-done(((bf16[256,2688]{1,0:T(8,128)(2,1)}), bf16[2048,2688]{1,0:T(8,128)(2,1)}) %all-gather.3.cloned.1.call-update) | async-done | bytes 11010064 | tf_op jit(solution)/shard_map/all_gather | solution.py:451
  216.5 13.7 %enter.2 = (f32[1024,2176]{1,0:T(8,128)}, bf16[1024,2048]{1,0:T(8,128)(2,1)}, bf16[1024,512]{1,0:T(8,128)(2,1)}, f32[16,2048]{1,0:T(8,128)}) custom-call(s32[3]{0:T(128)} %pad.70.info_ref, bf16[272,2048]{1,0:T(8,128)(2,1)} %fusion.22.refs_0_, bf16[272,2048]{1,0:T(8,128)(2,1)} %collective-permute-done.1.refs_1_, ...), custom_call_target="tpu_custom_call" | custom-call | flops 11000000 | bytes 1024 | tf_op jit(solution)/shard_map/enter/pallas_call | solution.py:383
  231.5 8.7 mixer_forward.4
  240.2 9.2 mixer_forward.5
  249.3 13.5 %enter.3 = (f32[1024,2176]{1,0:T(8,128)}, bf16[1024,2048]{1,0:T(8,128)(2,1)}, bf16[1024,512]{1,0:T(8,128)(2,1)}, f32[16,2048]{1,0:T(8,128)}) custom-call(s32[3]{0:T(128)} %pad_add_fusion.info_ref, bf16[272,2048]{1,0:T(8,128)(2,1)} %collective-permute-done.refs_0_, ...), custom_call_target="tpu_custom_call", output_to_operand_aliasing={{0}: (4, {}), {1}: (5, {}), {2}: (6, {})} | custom-call | flops 11000000 | bytes 1024 | tf_op jit(solution)/shard_map/enter/pallas_call | solution.py:383
  262.8 8.7 mixer_forward.6
  271.5 8.9 mixer_forward.7
  281.5 6.5 collective-permute-start.7
  288.0 23.5 %collective-permute-done.7.refs_2_ = bf16[1024,512]{1,0:T(8,128)(2,1)S(1)} collective-permute-done((bf16[1024,512]{1,0:T(8,128)(2,1)S(1)}, bf16[1024,512]{1,0:T(8,128)(2,1)S(1)}, u32[]{:S(2)}, u32[]{:S(2)}) %collective-permute-start.7) | collective-permute-done | bytes 1048608 | tf_op jit(solution)/shard_map/ppermute | solution.py:419
  315.4 10.1 %leave.1 = (bf16[1024,2048]{1,0:T(8,128)(2,1)}, f32[1024,512]{1,0:T(8,128)}, f32[1024,512]{1,0:T(8,128)}, bf16[1024,512]{1,0:T(8,128)(2,1)}, f32[4,1,256]{2,1,0:T(1,128)}) custom-call(s32[2]{0:T(128)} %pad_add_fusion.1.info_ref, bf16[1024,512]{1,0:T(8,128)(2,1)} %copy-done.5, bf16[1024,512]{1,0:T(8,128)(2,1)} %copy-done.52, bf16[1024,512]{1,0:T(8,128)(2,1)} %copy-done.53, ...), custom_call_target="tpu_custom_call" | custom-call | flops 9000000 | bytes 1024 | tf_op jit(solution)/shard_map/leave/pallas_call | solution.py:383
  331.7 23.2 %collective-permute-done.13.refs_2_ = bf16[1024,512]{1,0:T(8,128)(2,1)S(1)} collective-permute-done((bf16[1024,512]{1,0:T(8,128)(2,1)}, bf16[1024,512]{1,0:T(8,128)(2,1)S(1)}, u32[]{:S(2)}, u32[]{:S(2)}) %collective-permute-start.13) | collective-permute-done | bytes 1048608 | tf_op jit(solution)/shard_map/ppermute | solution.py:419
  358.1 23.4 %all-gather.5.cloned.1.call-done.refs_12_.refs_1_ = bf16[2048,2816]{1,0:T(8,128)(2,1)} async-done(((bf16[256,2816]{1,0:T(8,128)(2,1)}), bf16[2048,2816]{1,0:T(8,128)(2,1)}) %all-gather.5.cloned.1.call-update) | async-done | bytes 11534352 | tf_op jit(solution)/shard_map/all_gather | solution.py:451
  381.4 34.5 %hidden.1 = (bf16[1024,2048]{1,0:T(8,128)(2,1)}, bf16[1024,1408]{1,0:T(8,128)(2,1)}, bf16[1024,2816]{1,0:T(8,128)(2,1)}, f32[4,1,256]{2,1,0:T(1,128)}, bf16[1024...) custom-call(s32[10]{0:T(128)} %stack.112.info_ref, bf16[1024,512]{1,0:T(8,128)(2,1)} %get-tuple-element.205.refs_0_, ...), custom_call_target="tpu_custom_call" | custom-call | flops 33000000 | bytes 1024 | tf_op jit(solution)/shard_map/hidden/pallas_call | solution.py:383
  415.9 18.3 %convolution_convert_fusion = bf16[2048,2816]{1,0:T(8,128)(2,1)} fusion(bf16[1024,2048]{1,0:T(8,128)(2,1)} %get-tuple-element.220, bf16[1024,2816]{1,0:T(8,128)(2,1)} %get-tuple-element.221.refs_0_), kind=kOutput, calls=%fused_computation | convolution fusion | flops 11816927232 | bytes 21495808 | tf_op jit(solution)/shard_map/dot_general | solution.py:319
  439.7 20.4 %back.1 = (bf16[1024,512]{1,0:T(8,128)(2,1)}, bf16[1024,512]{1,0:T(8,128)(2,1)}, bf16[1024,512]{1,0:T(8,128)(2,1)}, bf16[1024,512]{1,0:T(8,128)(2,1)}) custom-call(s32[2]{0:T(128)} %pad_add_fusion.1.info_ref, bf16[1024,2816]{1,0:T(8,128)(2,1)} %get-tuple-element.221.refs_0_, bf16[2048,2816]{1,0:T(8,128)(2,1)} %all-gather.5.cloned.1.call-done.refs_12_.refs_1_), custom_call_target="tpu_custom_call" | custom-call | flops 19000000 | bytes 1024 | tf_op jit(solution)/shard_map/back/pallas_call | solution.py:383
  466.2 10.7 %convolution_convert_fusion.2 = bf16[1408,2048]{1,0:T(8,128)(2,1)} fusion(bf16[1024,1408]{1,0:T(8,128)(2,1)S(1)} %copy-done.37, bf16[1024,2048]{1,0:T(8,128)(2,1)} %get-tuple-element.235), kind=kOutput, calls=%fused_computation.2 | convolution fusion | flops 5908463616 | bytes 12845056 | tf_op jit(solution)/shard_map/dot_general | solution.py:319
  476.9 12.3 %collective-permute-done.30.refs_2_ = bf16[1024,512]{1,0:T(8,128)(2,1)S(1)} collective-permute-done((bf16[1024,512]{1,0:T(8,128)(2,1)S(1)}, bf16[1024,512]{1,0:T(8,128)(2,1)S(1)}, u32[]{:S(2)}, u32[]{:S(2)}) %collective-permute-start.30) | collective-permute-done | bytes 1048608 | tf_op jit(solution)/shard_map/ppermute | solution.py:419
  490.2 9.4 turn.1
  505.2 14.9 %down.1 = (bf16[256,2048]{1,0:T(8,128)(2,1)}, bf16[256,2048]{1,0:T(8,128)(2,1)}, bf16[256,2048]{1,0:T(8,128)(2,1)}, bf16[256,2048]{1,0:T(8,128)(2,1)}) custom-call(s32[9]{0:T(128)} %stack.113.info_ref, bf16[1024,1408]{1,0:T(8,128)(2,1)} %get-tuple-element.234.refs_0_, f32[1024,512]{1,0:T(8,128)} %get-tuple-element.239.refs_1_, ...), custom_call_target="tpu_custom_call" | custom-call | flops 14000000 | bytes 1024 | tf_op jit(solution)/shard_map/down/pallas_call | solution.py:383
  522.0 4.6 constant_dynamic-slice_fusion.8
  531.5 13.7 %collective-permute-done.34.far_ref = bf16[1024,512]{1,0:T(8,128)(2,1)S(1)} collective-permute-done((bf16[1024,512]{1,0:T(8,128)(2,1)S(1)}, bf16[1024,512]{1,0:T(8,128)(2,1)S(1)}, u32[]{:S(2)}, u32[]{:S(2)}) %collective-permute-start.34) | collective-permute-done | bytes 1048608 | tf_op jit(solution)/shard_map/ppermute | solution.py:419
  547.5 6.3 convolution_convert_fusion.4
  555.3 16.1 %mixer_backward.4 = (bf16[1024,2176]{1,0:T(8,128)(2,1)}, f32[4,1536]{1,0:T(4,128)S(1)}, f32[1,128]{1,0:T(1,128)S(1)}, f32[8,128]{1,0:T(8,128)S(1)}) custom-call(s32[1]{0:T(128)} %bitcast.rank_ref, s32[4,2]{1,0:T(4,128)S(1)} %maximum_convert_fusion.9.len_ref, f32[16]{0:T(128)S(1)} %copy-done.6, f32[16]{0:T(128)S(1)} %copy-done.7, ...), custom_call_target="tpu_custom_call" | custom-call | flops 12000000 | bytes 1024 | tf_op jit(solution)/shard_map/mixer_backward/pallas_call | solution.py:298
  571.4 16.1 %mixer_backward.5 = (bf16[1024,2176]{1,0:T(8,128)(2,1)}, f32[4,1536]{1,0:T(4,128)S(1)}, f32[1,128]{1,0:T(1,128)S(1)}, f32[8,128]{1,0:T(8,128)S(1)}) custom-call(s32[1]{0:T(128)} %bitcast.rank_ref, s32[4,2]{1,0:T(4,128)S(1)} %maximum_convert_fusion.9.len_ref, f32[16]{0:T(128)S(1)} %copy-done.6, f32[16]{0:T(128)S(1)} %copy-done.7, ...), custom_call_target="tpu_custom_call", output_to_operand_aliasing={{0}: (11, {})} | custom-call | flops 12000000 | bytes 1024 | tf_op jit(solution)/shard_map/mixer_backward/pallas_call | solution.py:298
  588.9 16.3 %mixer_backward.6 = (bf16[1024,2176]{1,0:T(8,128)(2,1)}, f32[4,1536]{1,0:T(4,128)S(1)}, f32[1,128]{1,0:T(1,128)S(1)}, f32[8,128]{1,0:T(8,128)S(1)}) custom-call(s32[1]{0:T(128)} %bitcast.rank_ref, s32[4,2]{1,0:T(4,128)S(1)} %maximum_convert_fusion.9.len_ref, f32[16]{0:T(128)S(1)} %copy-done.6, f32[16]{0:T(128)S(1)} %copy-done.7, ...), custom_call_target="tpu_custom_call", output_to_operand_aliasing={{0}: (11, {})} | custom-call | flops 12000000 | bytes 1024 | tf_op jit(solution)/shard_map/mixer_backward/pallas_call | solution.py:298
  605.2 16.2 %mixer_backward.7 = (bf16[1024,2176]{1,0:T(8,128)(2,1)}, f32[4,1536]{1,0:T(4,128)S(1)}, f32[1,128]{1,0:T(1,128)S(1)}, f32[8,128]{1,0:T(8,128)S(1)}) custom-call(s32[1]{0:T(128)} %bitcast.rank_ref, s32[4,2]{1,0:T(4,128)S(1)} %maximum_convert_fusion.9.len_ref, f32[16]{0:T(128)S(1)} %copy-done.6, f32[16]{0:T(128)S(1)} %copy-done.7, ...), custom_call_target="tpu_custom_call", output_to_operand_aliasing={{0}: (11, {})} | custom-call | flops 12000000 | bytes 1024 | tf_op jit(solution)/shard_map/mixer_backward/pallas_call | solution.py:298
  621.4 6.7 convolution_convert_fusion.3
  630.7 5.5 collective-permute-done.40
  636.7 7.4 convolution_convert_fusion.1
  644.0 18.8 %first.1 = (bf16[256,2048]{1,0:T(8,128)(2,1)}, bf16[256,2048]{1,0:T(8,128)(2,1)}, bf16[256,2048]{1,0:T(8,128)(2,1)}, bf16[256,2048]{1,0:T(8,128)(2,1)}) custom-call(s32[2]{0:T(128)} %pad_add_fusion.1.info_ref, bf16[1024,2176]{1,0:T(8,128)(2,1)} %get-tuple-element.280.refs_0_, bf16[2048,2688]{1,0:T(8,128)(2,1)} %all-gather.3.cloned.1.call-done.refs_2_.refs_6_.refs_14_.refs_1_), custom_call_target="tpu_custom_call" | custom-call | flops 19000000 | bytes 1024 | tf_op jit(solution)/shard_map/first/pallas_call | solution.py:383
  669.8 3.3 dynamic-slice_bitcast_fusion
  673.1 9.7 %collective-permute-done.41 = bf16[4,256,1024]{2,1,0:T(8,128)(2,1)} collective-permute-done((bf16[4,256,1024]{2,1,0:T(8,128)(2,1)}, bf16[4,256,1024]{2,1,0:T(8,128)(2,1)}, u32[]{:S(2)}, u32[]{:S(2)}) %collective-permute-start.41) | collective-permute-done | bytes 2097184 | tf_op jit(solution)/shard_map/ppermute | solution.py:419
  693.4 5.5 collective-permute-done.37
  709.3 4.8 collective-permute-start.51
  714.1 10.6 %collective-permute-done.44 = bf16[256,2048]{1,0:T(8,128)(2,1)} collective-permute-done((bf16[256,2048]{1,0:T(8,128)(2,1)}, bf16[256,2048]{1,0:T(8,128)(2,1)}, u32[]{:S(2)}, u32[]{:S(2)}) %collective-permute-start.44) | collective-permute-done | bytes 1048608 | tf_op jit(solution)/shard_map/ppermute | solution.py:419
  729.5 4.6 collective-permute-done.42
  742.3 14.0 %collective-permute-done.58 = bf16[4,256,512]{2,1,0:T(8,128)(2,1)S(1)} collective-permute-done((bf16[4,256,512]{2,1,0:T(8,128)(2,1)}, bf16[4,256,512]{2,1,0:T(8,128)(2,1)S(1)}, u32[]{:S(2)}, u32[]{:S(2)}) %collective-permute-start.58) | collective-permute-done | bytes 1048608 | tf_op jit(solution)/shard_map/ppermute | solution.py:419
  761.8 4.6 collective-permute-start.60
  766.4 3.9 fusion.1
  770.8 6.5 collective-permute-start.47
  781.1 4.7 fusion.12
  788.3 9.6 %collective-permute-done.45 = bf16[256,2816]{1,0:T(8,128)(2,1)} collective-permute-done((bf16[256,2816]{1,0:T(8,128)(2,1)}, bf16[256,2816]{1,0:T(8,128)(2,1)}, u32[]{:S(2)}, u32[]{:S(2)}) %collective-permute-start.45) | collective-permute-done | bytes 1441824 | tf_op jit(solution)/shard_map/ppermute | solution.py:419
  797.9 7.0 collective-permute-start.48
  815.3 6.7 collective-permute-done.61
  821.9 9.8 %collective-permute-done.64 = bf16[256,512]{1,0:T(8,128)(2,1)S(1)} collective-permute-done((bf16[256,512]{1,0:T(8,128)(2,1)S(1)}, bf16[256,512]{1,0:T(8,128)(2,1)S(1)}, u32[]{:S(2)}, u32[]{:S(2)}) %collective-permute-start.64) | collective-permute-done | bytes 262176 | tf_op jit(solution)/shard_map/ppermute | solution.py:419
  835.3 4.0 broadcast_select_fusion.7
  854.0 4.7 maximum_convert_fusion
  860.7 5.8 copy.99
  876.1 7.2 collective-permute-done.73
  890.6 5.5 reduce-scatter.8.cloned.1.call-done
  898.4 11.9 %collective-permute-done.76 = bf16[256,1152]{0,1:T(8,128)(2,1)S(1)} collective-permute-done((bf16[256,1152]{0,1:T(8,128)(2,1)}, bf16[256,1152]{0,1:T(8,128)(2,1)S(1)}, u32[]{:S(2)}, u32[]{:S(2)}) %collective-permute-start.76) | collective-permute-done | bytes 589856 | tf_op jit(solution)/shard_map/ppermute | solution.py:419
  915.9 6.2 copy.109
  922.2 6.3 copy.110
  (439 shorter events, 208.7 us)
Async XLA Ops:
  7.2 206.1 %all-gather.3.cloned.1.call-start = ((), (), s32[]{:S(2)}) async-start(), calls=%async_computation.3 | async-start | bytes 12386304 | tf_op jit(solution)/shard_map/all_gather | solution.py:451
  20.1 361.3 %all-gather.5.cloned.1.call-start = ((), (), s32[]{:S(2)}) async-start(), calls=%async_computation.4 | async-start | bytes 12976128 | tf_op jit(solution)/shard_map/all_gather | solution.py:451
  23.2 10.3 %collective-permute-start.1 = (bf16[272,2048]{1,0:T(8,128)(2,1)}, bf16[272,2048]{1,0:T(8,128)(2,1)}, u32[]{:S(2)}, u32[]{:S(2)}) collective-permute-start(bf16[272,2048]{1,0:T(8,128)(2,1)} %fusion.22.refs_0_), channel_id=1, source_target_pairs={{0,8},{8,0},{16,24},{24,16},{1,9},{9,1},{17,25},{25,17},{2,10},{10... | collective-permute-start | bytes 3342344 | tf_op jit(solution)/shard_map/ppermute | solution.py:419
  23.2 27.9 %collective-permute-start = (bf16[272,2048]{1,0:T(8,128)(2,1)}, bf16[272,2048]{1,0:T(8,128)(2,1)}, u32[]{:S(2)}, u32[]{:S(2)}) collective-permute-start(bf16[272,2048]{1,0:T(8,128)(2,1)} %fusion.22.refs_0_), channel_id=1, source_target_pairs={{0,16},{8,24},{16,0},{24,8},{1,17},{9,25},{17,1},{25,9},{2,18},{10... | collective-permute-start | bytes 3342344 | tf_op jit(solution)/shard_map/ppermute | solution.py:419
  26.8 42.4 %collective-permute-start.17 = (bf16[176,2048]{1,0:T(8,128)(2,1)}, bf16[176,2048]{1,0:T(8,128)(2,1)}, u32[]{:S(2)}, u32[]{:S(2)}) collective-permute-start(bf16[176,2048]{1,0:T(8,128)(2,1)} %constant_dynamic-slice_fusion.12.refs_13_.refs_2_), channel_id=1, source_target_pairs={{2,0},{3,1},{4,2},{5,3},{6,4},{7,5},{10,8},{11,9},{12,10},{13,11},... | collective-permute-start | bytes 2162696 | tf_op jit(solution)/shard_map/ppermute | solution.py:419
  28.1 41.1 %collective-permute-start.16 = (bf16[176,2048]{1,0:T(8,128)(2,1)}, bf16[176,2048]{1,0:T(8,128)(2,1)S(1)}, u32[]{:S(2)}, u32[]{:S(2)}) collective-permute-start(bf16[176,2048]{1,0:T(8,128)(2,1)} %constant_dynamic-slice_fusion.12.refs_13_.refs_2_), channel_id=1, source_target_pairs={{0,2},{1,3},{2,4},{3,5},{4,6},{5,7},{8,10},{9,11},{10,12},{11,13},... | collective-permute-start | bytes 2162696 | tf_op jit(solution)/shard_map/ppermute | solution.py:419
  32.1 38.3 %collective-permute-start.15 = (bf16[176,2048]{1,0:T(8,128)(2,1)}, bf16[176,2048]{1,0:T(8,128)(2,1)S(1)}, u32[]{:S(2)}, u32[]{:S(2)}) collective-permute-start(bf16[176,2048]{1,0:T(8,128)(2,1)} %constant_dynamic-slice_fusion.12.refs_13_.refs_2_), channel_id=1, source_target_pairs={{0,1},{1,0},{2,3},{3,2},{4,5},{5,4},{6,7},{7,6},{8,9},{9,8},{10,11... | collective-permute-start | bytes 2162696 | tf_op jit(solution)/shard_map/ppermute | solution.py:419
  51.1 23.7 %collective-permute-start.2 = (bf16[272,2048]{1,0:T(8,128)(2,1)}, bf16[272,2048]{1,0:T(8,128)(2,1)S(1)}, u32[]{:S(2)}, u32[]{:S(2)}) collective-permute-start(bf16[272,2048]{1,0:T(8,128)(2,1)} %collective-permute-done.refs_0_), channel_id=1, source_target_pairs={{0,8},{8,0},{16,24},{24,16},{1,9},{9,1},{17,25},{25,17},{2,10},{10... | collective-permute-start | bytes 3342344 | tf_op jit(solution)/shard_map/ppermute | solution.py:419
  70.4 14.1 %collective-permute-start.18 = (bf16[176,2048]{1,0:T(8,128)(2,1)S(1)}, bf16[176,2048]{1,0:T(8,128)(2,1)S(1)}, u32[]{:S(2)}, u32[]{:S(2)}) collective-permute-start(bf16[176,2048]{1,0:T(8,128)(2,1)S(1)} %broadcast_select_fusion.17.refs_15_.refs_4_), channel_id=1, source_target_pairs={{0,1},{1,0},{2,3},{3,2},{4,5},{5,4},{6,7},{7,6},{8,9},{9,8},{10,11... | collective-permute-start | bytes 2162696 | tf_op jit(solution)/shard_map/ppermute | solution.py:419
  71.8 12.7 %collective-permute-start.19 = (bf16[176,2048]{1,0:T(8,128)(2,1)S(1)}, bf16[176,2048]{1,0:T(8,128)(2,1)}, u32[]{:S(2)}, u32[]{:S(2)}) collective-permute-start(bf16[176,2048]{1,0:T(8,128)(2,1)S(1)} %collective-permute-done.16), channel_id=1, source_target_pairs={{2,4},{3,5},{4,6},{5,7},{10,12},{11,13},{12,14},{13,15},{18,20},{1... | collective-permute-start | bytes 2162696 | tf_op jit(solution)/shard_map/ppermute | solution.py:419
  73.3 35.4 %collective-permute-start.20 = (bf16[176,2048]{1,0:T(8,128)(2,1)}, bf16[176,2048]{1,0:T(8,128)(2,1)}, u32[]{:S(2)}, u32[]{:S(2)}) collective-permute-start(bf16[176,2048]{1,0:T(8,128)(2,1)} %collective-permute-done.17), channel_id=1, source_target_pairs={{2,0},{3,1},{4,2},{5,3},{10,8},{11,9},{12,10},{13,11},{18,16},{19,... | collective-permute-start | bytes 2162696 | tf_op jit(solution)/shard_map/ppermute | solution.py:419
  74.8 36.6 %collective-permute-start.3 = (bf16[256,2048]{1,0:T(8,128)(2,1)S(1)}, bf16[256,2048]{1,0:T(8,128)(2,1)}, u32[]{:S(2)}, u32[]{:S(2)}) collective-permute-start(bf16[256,2048]{1,0:T(8,128)(2,1)S(1)} %broadcast_multiply_fusion.refs_8_), channel_id=1, source_target_pairs={{0,16},{8,24},{16,0},{24,8},{1,17},{9,25},{17,1},{25,9},{2,18},{10... | collective-permute-start | bytes 3145736 | tf_op jit(solution)/shard_map/ppermute | solution.py:419
  74.9 36.5 %collective-permute-start.4 = (bf16[256,2048]{1,0:T(8,128)(2,1)S(1)}, bf16[256,2048]{1,0:T(8,128)(2,1)}, u32[]{:S(2)}, u32[]{:S(2)}) collective-permute-start(bf16[256,2048]{1,0:T(8,128)(2,1)S(1)} %broadcast_multiply_fusion.refs_8_), channel_id=1, source_target_pairs={{0,8},{8,0},{16,24},{24,16},{1,9},{9,1},{17,25},{25,17},{2,10},{10... | collective-permute-start | bytes 3145736 | tf_op jit(solution)/shard_map/ppermute | solution.py:419
  85.4 29.4 %collective-permute-start.23 = (bf16[176,2048]{1,0:T(8,128)(2,1)}, bf16[176,2048]{1,0:T(8,128)(2,1)}, u32[]{:S(2)}, u32[]{:S(2)}) collective-permute-start(bf16[176,2048]{1,0:T(8,128)(2,1)} %collective-permute-done.19), channel_id=1, source_target_pairs={{4,6},{5,7},{12,14},{13,15},{20,22},{21,23},{28,30},{29,31}} | collective-permute-start | bytes 2162696 | tf_op jit(solution)/shard_map/ppermute | solution.py:419
  108.7 65.2 %collective-permute-start.22 = (bf16[176,2048]{1,0:T(8,128)(2,1)}, bf16[176,2048]{1,0:T(8,128)(2,1)}, u32[]{:S(2)}, u32[]{:S(2)}) collective-permute-start(bf16[176,2048]{1,0:T(8,128)(2,1)} %collective-permute-done.20), channel_id=1, source_target_pairs={{2,0},{3,1},{10,8},{11,9},{18,16},{19,17},{26,24},{27,25}} | collective-permute-start | bytes 2162696 | tf_op jit(solution)/shard_map/ppermute | solution.py:419
  111.3 63.9 %collective-permute-start.21 = (bf16[176,2048]{1,0:T(8,128)(2,1)S(1)}, bf16[176,2048]{1,0:T(8,128)(2,1)}, u32[]{:S(2)}, u32[]{:S(2)}) collective-permute-start(bf16[176,2048]{1,0:T(8,128)(2,1)S(1)} %broadcast_select_fusion.16.refs_17_.refs_6_), channel_id=1, source_target_pairs={{0,1},{1,0},{2,3},{3,2},{4,5},{5,4},{6,7},{7,6},{8,9},{9,8},{10,11... | collective-permute-start | bytes 2162696 | tf_op jit(solution)/shard_map/ppermute | solution.py:419
  111.4 81.0 %collective-permute-start.5 = (bf16[256,2048]{1,0:T(8,128)(2,1)}, bf16[256,2048]{1,0:T(8,128)(2,1)}, u32[]{:S(2)}, u32[]{:S(2)}) collective-permute-start(bf16[256,2048]{1,0:T(8,128)(2,1)} %collective-permute-done.3.refs_10_), channel_id=1, source_target_pairs={{0,8},{8,0},{16,24},{24,16},{1,9},{9,1},{17,25},{25,17},{2,10},{10... | collective-permute-start | bytes 3145736 | tf_op jit(solution)/shard_map/ppermute | solution.py:419
  175.2 17.1 %collective-permute-start.24 = (bf16[176,2048]{1,0:T(8,128)(2,1)S(1)}, bf16[176,2048]{1,0:T(8,128)(2,1)}, u32[]{:S(2)}, u32[]{:S(2)}) collective-permute-start(bf16[176,2048]{1,0:T(8,128)(2,1)S(1)} %select_select_fusion.refs_19_.refs_8_), channel_id=1, source_target_pairs={{0,1},{1,0},{2,3},{3,2},{4,5},{5,4},{6,7},{7,6},{8,9},{9,8},{10,11... | collective-permute-start | bytes 2162696 | tf_op jit(solution)/shard_map/ppermute | solution.py:419
  213.3 557.1 %reduce-scatter.4.cloned.1.call-start = ((), (), s32[]{:S(2)}) async-start(), calls=%async_computation.5 | async-start | bytes 12976128 | tf_op jit(solution)/shard_map/reduce_scatter | solution.py:467
  281.5 30.1 %collective-permute-start.7 = (bf16[1024,512]{1,0:T(8,128)(2,1)S(1)}, bf16[1024,512]{1,0:T(8,128)(2,1)S(1)}, u32[]{:S(2)}, u32[]{:S(2)}) collective-permute-start(bf16[1024,512]{1,0:T(8,128)(2,1)S(1)} %get-tuple-element.196.refs_0_), channel_id=1, source_target_pairs={{0,16},{8,24},{16,0},{24,8},{1,17},{9,25},{17,1},{25,9},{2,18},{10... | collective-permute-start | bytes 3145736 | tf_op jit(solution)/shard_map/ppermute | solution.py:419
  329.8 25.1 %collective-permute-start.13 = (bf16[1024,512]{1,0:T(8,128)(2,1)}, bf16[1024,512]{1,0:T(8,128)(2,1)S(1)}, u32[]{:S(2)}, u32[]{:S(2)}) collective-permute-start(bf16[1024,512]{1,0:T(8,128)(2,1)} %get-tuple-element.205.refs_0_), channel_id=1, source_target_pairs={{0,16},{8,24},{16,0},{24,8},{1,17},{9,25},{17,1},{25,9},{2,18},{10... | collective-permute-start | bytes 3145736 | tf_op jit(solution)/shard_map/ppermute | solution.py:419
  331.3 23.6 %collective-permute-start.12 = (bf16[1024,512]{1,0:T(8,128)(2,1)}, bf16[1024,512]{1,0:T(8,128)(2,1)}, u32[]{:S(2)}, u32[]{:S(2)}) collective-permute-start(bf16[1024,512]{1,0:T(8,128)(2,1)} %get-tuple-element.205.refs_0_), channel_id=1, source_target_pairs={{0,8},{8,0},{16,24},{24,16},{1,9},{9,1},{17,25},{25,17},{2,10},{10... | collective-permute-start | bytes 3145736 | tf_op jit(solution)/shard_map/ppermute | solution.py:419
  434.2 408.4 %reduce-scatter.6.cloned.1.call-start = ((), (), s32[]{:S(2)}) async-start(), calls=%async_computation.6 | async-start | bytes 2621440 | tf_op jit(solution)/shard_map/reduce_scatter | solution.py:479
  438.3 21.9 %collective-permute-start.27 = (f32[4,1,256]{2,1,0:T(1,128)S(1)}, f32[4,1,256]{2,1,0:T(1,128)S(1)}, u32[]{:S(2)}, u32[]{:S(2)}) collective-permute-start(f32[4,1,256]{2,1,0:T(1,128)S(1)} %collective-permute-done.25.refs_12_), channel_id=1, source_target_pairs={{0,8},{8,0},{16,24},{24,16},{1,9},{9,1},{17,25},{25,17},{2,10},{10... | collective-permute-start | bytes 12296 | tf_op jit(solution)/shard_map/ppermute | solution.py:419
  464.7 12.3 %collective-permute-start.29 = (bf16[1024,512]{1,0:T(8,128)(2,1)}, bf16[1024,512]{1,0:T(8,128)(2,1)S(1)}, u32[]{:S(2)}, u32[]{:S(2)}) collective-permute-start(bf16[1024,512]{1,0:T(8,128)(2,1)} %get-tuple-element.230), channel_id=1, source_target_pairs={{0,8},{8,0},{16,24},{24,16},{1,9},{9,1},{17,25},{25,17},{2,10},{10... | collective-permute-start | bytes 3145736 | tf_op jit(solution)/shard_map/ppermute | solution.py:419
  464.8 24.4 %collective-permute-start.30 = (bf16[1024,512]{1,0:T(8,128)(2,1)S(1)}, bf16[1024,512]{1,0:T(8,128)(2,1)S(1)}, u32[]{:S(2)}, u32[]{:S(2)}) collective-permute-start(bf16[1024,512]{1,0:T(8,128)(2,1)S(1)} %add_convert_fusion.3), channel_id=1, source_target_pairs={{0,16},{8,24},{16,0},{24,8},{1,17},{9,25},{17,1},{25,9},{2,18},{10... | collective-permute-start | bytes 3145736 | tf_op jit(solution)/shard_map/ppermute | solution.py:419
  504.3 15.8 %collective-permute-start.32 = (bf16[1024,512]{1,0:T(8,128)(2,1)}, bf16[1024,512]{1,0:T(8,128)(2,1)S(1)}, u32[]{:S(2)}, u32[]{:S(2)}) collective-permute-start(bf16[1024,512]{1,0:T(8,128)(2,1)} %get-tuple-element.245), channel_id=1, source_target_pairs={{0,8},{8,0},{16,24},{24,16},{1,9},{9,1},{17,25},{25,17},{2,10},{10... | collective-permute-start | bytes 3145736 | tf_op jit(solution)/shard_map/ppermute | solution.py:419
  520.1 9.1 collective-permute-start.33
  520.7 24.6 %collective-permute-start.34 = (bf16[1024,512]{1,0:T(8,128)(2,1)S(1)}, bf16[1024,512]{1,0:T(8,128)(2,1)S(1)}, u32[]{:S(2)}, u32[]{:S(2)}) collective-permute-start(bf16[1024,512]{1,0:T(8,128)(2,1)S(1)} %add_convert_fusion.1), channel_id=1, source_target_pairs={{0,16},{8,24},{16,0},{24,8},{1,17},{9,25},{17,1},{25,9},{2,18},{10... | collective-permute-start | bytes 3145736 | tf_op jit(solution)/shard_map/ppermute | solution.py:419
  528.7 107.5 %collective-permute-start.40 = (bf16[4,176,2048]{2,1,0:T(8,128)(2,1)}, bf16[4,176,2048]{2,1,0:T(8,128)(2,1)}, u32[]{:S(2)}, u32[]{:S(2)}) collective-permute-start(bf16[4,176,2048]{2,1,0:T(8,128)(2,1)} %pad_maximum_fusion), channel_id=1, source_target_pairs={{0,1},{1,0},{2,3},{3,2},{4,5},{5,4},{6,7},{7,6},{8,9},{9,8},{10,11... | collective-permute-start | bytes 8650760 | tf_op jit(solution)/shard_map/ppermute | solution.py:419
  529.2 58.3 %collective-permute-start.38 = (bf16[256,2048]{1,0:T(8,128)(2,1)}, bf16[256,2048]{1,0:T(8,128)(2,1)}, u32[]{:S(2)}, u32[]{:S(2)}) collective-permute-start(bf16[256,2048]{1,0:T(8,128)(2,1)} %get-tuple-element.253), channel_id=1, source_target_pairs={{0,8},{8,0},{16,24},{24,16},{1,9},{9,1},{17,25},{25,17},{2,10},{10... | collective-permute-start | bytes 3145736 | tf_op jit(solution)/shard_map/ppermute | solution.py:419
  546.2 42.6 %collective-permute-start.35 = (bf16[256,2048]{1,0:T(8,128)(2,1)}, bf16[256,2048]{1,0:T(8,128)(2,1)}, u32[]{:S(2)}, u32[]{:S(2)}) collective-permute-start(bf16[256,2048]{1,0:T(8,128)(2,1)} %add_convert_fusion.2), channel_id=1, source_target_pairs={{0,16},{8,24},{16,0},{24,8},{1,17},{9,25},{17,1},{25,9},{2,18},{10... | collective-permute-start | bytes 3145736 | tf_op jit(solution)/shard_map/ppermute | solution.py:419
  587.5 79.3 %collective-permute-start.39 = (bf16[256,512]{1,0:T(8,128)(2,1)}, bf16[256,512]{1,0:T(8,128)(2,1)S(1)}, u32[]{:S(2)}, u32[]{:S(2)}) collective-permute-start(bf16[256,512]{1,0:T(8,128)(2,1)} %get-tuple-element.254), channel_id=1, source_target_pairs={{0,8},{8,0},{16,24},{24,16},{1,9},{9,1},{17,25},{25,17},{2,10},{10... | collective-permute-start | bytes 786440 | tf_op jit(solution)/shard_map/ppermute | solution.py:419
  636.2 46.6 %collective-permute-start.41 = (bf16[4,256,1024]{2,1,0:T(8,128)(2,1)}, bf16[4,256,1024]{2,1,0:T(8,128)(2,1)}, u32[]{:S(2)}, u32[]{:S(2)}) collective-permute-start(bf16[4,256,1024]{2,1,0:T(8,128)(2,1)} %dynamic-slice_bitcast_fusion.1), channel_id=1, source_target_pairs={{0,1},{1,0},{2,3},{3,2},{4,5},{5,4},{6,7},{7,6},{8,9},{9,8},{10,11... | collective-permute-start | bytes 6291464 | tf_op jit(solution)/shard_map/ppermute | solution.py:419
  664.3 19.2 %collective-permute-start.49 = (bf16[176,2048]{1,0:T(8,128)(2,1)S(1)}, bf16[176,2048]{1,0:T(8,128)(2,1)}, u32[]{:S(2)}, u32[]{:S(2)}) collective-permute-start(bf16[176,2048]{1,0:T(8,128)(2,1)S(1)} %fusion.18), channel_id=1, source_target_pairs={{0,2},{1,3},{8,10},{9,11},{16,18},{17,19},{24,26},{25,27}} | collective-permute-start | bytes 2162696 | tf_op jit(solution)/shard_map/ppermute | solution.py:419
  666.9 25.2 %collective-permute-start.43 = (bf16[256,2048]{1,0:T(8,128)(2,1)}, bf16[256,2048]{1,0:T(8,128)(2,1)S(1)}, u32[]{:S(2)}, u32[]{:S(2)}) collective-permute-start(bf16[256,2048]{1,0:T(8,128)(2,1)} %get-tuple-element.283), channel_id=1, source_target_pairs={{0,8},{8,0},{16,24},{24,16},{1,9},{9,1},{17,25},{25,17},{2,10},{10... | collective-permute-start | bytes 3145736 | tf_op jit(solution)/shard_map/ppermute | solution.py:419
  668.6 20.9 %collective-permute-start.36 = (bf16[256,512]{1,0:T(8,128)(2,1)}, bf16[256,512]{1,0:T(8,128)(2,1)S(1)}, u32[]{:S(2)}, u32[]{:S(2)}) collective-permute-start(bf16[256,512]{1,0:T(8,128)(2,1)} %get-tuple-element.250), channel_id=1, source_target_pairs={{0,16},{8,24},{16,0},{24,8},{1,17},{9,25},{17,1},{25,9},{2,18},{10... | collective-permute-start | bytes 786440 | tf_op jit(solution)/shard_map/ppermute | solution.py:419
  682.8 51.3 %collective-permute-start.42 = (bf16[4,256,1152]{2,1,0:T(8,128)(2,1)}, bf16[4,256,1152]{2,1,0:T(8,128)(2,1)}, u32[]{:S(2)}, u32[]{:S(2)}) collective-permute-start(bf16[4,256,1152]{2,1,0:T(8,128)(2,1)} %dynamic-slice_bitcast_fusion), channel_id=1, source_target_pairs={{0,1},{1,0},{2,3},{3,2},{4,5},{5,4},{6,7},{7,6},{8,9},{9,8},{10,11... | collective-permute-start | bytes 7077896 | tf_op jit(solution)/shard_map/ppermute | solution.py:419
  686.1 15.7 %collective-permute-start.50 = (bf16[176,2048]{1,0:T(8,128)(2,1)}, bf16[176,2048]{1,0:T(8,128)(2,1)}, u32[]{:S(2)}, u32[]{:S(2)}) collective-permute-start(bf16[176,2048]{1,0:T(8,128)(2,1)} %fusion.16), channel_id=1, source_target_pairs={{0,2},{1,3},{2,4},{3,5},{8,10},{9,11},{10,12},{11,13},{16,18},{17,... | collective-permute-start | bytes 2162696 | tf_op jit(solution)/shard_map/ppermute | solution.py:419
  689.5 9.4 collective-permute-start.37
  698.9 15.2 %collective-permute-start.46 = (bf16[256,2048]{1,0:T(8,128)(2,1)}, bf16[256,2048]{1,0:T(8,128)(2,1)}, u32[]{:S(2)}, u32[]{:S(2)}) collective-permute-start(bf16[256,2048]{1,0:T(8,128)(2,1)} %get-tuple-element.287), channel_id=1, source_target_pairs={{0,8},{8,0},{16,24},{24,16},{1,9},{9,1},{17,25},{25,17},{2,10},{10... | collective-permute-start | bytes 3145736 | tf_op jit(solution)/shard_map/ppermute | solution.py:419
  699.6 25.1 %collective-permute-start.44 = (bf16[256,2048]{1,0:T(8,128)(2,1)}, bf16[256,2048]{1,0:T(8,128)(2,1)}, u32[]{:S(2)}, u32[]{:S(2)}) collective-permute-start(bf16[256,2048]{1,0:T(8,128)(2,1)} %add_convert_fusion), channel_id=1, source_target_pairs={{0,16},{8,24},{16,0},{24,8},{1,17},{9,25},{17,1},{25,9},{2,18},{10... | collective-permute-start | bytes 3145736 | tf_op jit(solution)/shard_map/ppermute | solution.py:419
  704.9 30.1 %collective-permute-start.52 = (bf16[176,2048]{1,0:T(8,128)(2,1)}, bf16[176,2048]{1,0:T(8,128)(2,1)}, u32[]{:S(2)}, u32[]{:S(2)}) collective-permute-start(bf16[176,2048]{1,0:T(8,128)(2,1)} %get-tuple-element.298), channel_id=1, source_target_pairs={{6,4},{7,5},{14,12},{15,13},{22,20},{23,21},{30,28},{31,29}} | collective-permute-start | bytes 2162696 | tf_op jit(solution)/shard_map/ppermute | solution.py:419
  709.3 47.0 %collective-permute-start.51 = (bf16[176,2048]{1,0:T(8,128)(2,1)}, bf16[176,2048]{1,0:T(8,128)(2,1)}, u32[]{:S(2)}, u32[]{:S(2)}) collective-permute-start(bf16[176,2048]{1,0:T(8,128)(2,1)} %get-tuple-element.297), channel_id=1, source_target_pairs={{0,2},{1,3},{2,4},{3,5},{4,6},{5,7},{8,10},{9,11},{10,12},{11,13},... | collective-permute-start | bytes 2162696 | tf_op jit(solution)/shard_map/ppermute | solution.py:419
  734.1 22.2 %collective-permute-start.58 = (bf16[4,256,512]{2,1,0:T(8,128)(2,1)}, bf16[4,256,512]{2,1,0:T(8,128)(2,1)S(1)}, u32[]{:S(2)}, u32[]{:S(2)}) collective-permute-start(bf16[4,256,512]{2,1,0:T(8,128)(2,1)} %pad_maximum_fusion.2), channel_id=1, source_target_pairs={{0,1},{1,0},{2,3},{3,2},{4,5},{5,4},{6,7},{7,6},{8,9},{9,8},{10,11... | collective-permute-start | bytes 3145736 | tf_op jit(solution)/shard_map/ppermute | solution.py:419
  736.7 21.0 %collective-permute-start.53 = (bf16[176,2048]{1,0:T(8,128)(2,1)S(1)}, bf16[176,2048]{1,0:T(8,128)(2,1)S(1)}, u32[]{:S(2)}, u32[]{:S(2)}) collective-permute-start(bf16[176,2048]{1,0:T(8,128)(2,1)S(1)} %fusion.17), channel_id=1, source_target_pairs={{4,2},{5,3},{6,4},{7,5},{12,10},{13,11},{14,12},{15,13},{20,18},{2... | collective-permute-start | bytes 2162696 | tf_op jit(solution)/shard_map/ppermute | solution.py:419
  741.6 28.7 %collective-permute-start.70 = (f32[232,128]{1,0:T(8,128)S(1)}, f32[232,128]{1,0:T(8,128)S(1)}, u32[]{:S(2)}, u32[]{:S(2)}) collective-permute-start(f32[232,128]{1,0:T(8,128)S(1)} %fusion.59), channel_id=1, source_target_pairs={{0,1},{1,0},{2,3},{3,2},{4,5},{5,4},{6,7},{7,6},{8,9},{9,8},{10,11... | collective-permute-start | bytes 356360 | tf_op jit(solution)/shard_map/ppermute | solution.py:836
  758.8 21.5 %collective-permute-start.54 = (bf16[176,2048]{1,0:T(8,128)(2,1)}, bf16[176,2048]{1,0:T(8,128)(2,1)}, u32[]{:S(2)}, u32[]{:S(2)}) collective-permute-start(bf16[176,2048]{1,0:T(8,128)(2,1)} %add_convert_fusion.5), channel_id=1, source_target_pairs={{2,0},{3,1},{4,2},{5,3},{6,4},{7,5},{10,8},{11,9},{12,10},{13,11},... | collective-permute-start | bytes 2162696 | tf_op jit(solution)/shard_map/ppermute | solution.py:419
  761.8 16.6 %collective-permute-start.60 = (bf16[256,512]{1,0:T(8,128)(2,1)}, bf16[256,512]{1,0:T(8,128)(2,1)}, u32[]{:S(2)}, u32[]{:S(2)}) collective-permute-start(bf16[256,512]{1,0:T(8,128)(2,1)} %fusion.23), channel_id=1, source_target_pairs={{0,2},{1,3},{2,4},{3,5},{8,10},{9,11},{10,12},{11,13},{16,18},{17,... | collective-permute-start | bytes 786440 | tf_op jit(solution)/shard_map/ppermute | solution.py:419
  770.4 27.4 %collective-permute-start.45 = (bf16[256,2816]{1,0:T(8,128)(2,1)}, bf16[256,2816]{1,0:T(8,128)(2,1)}, u32[]{:S(2)}, u32[]{:S(2)}) collective-permute-start(bf16[256,2816]{1,0:T(8,128)(2,1)} %reduce-scatter.4.cloned.1.call-done), channel_id=1, source_target_pairs={{0,16},{8,24},{16,0},{24,8},{1,17},{9,25},{17,1},{25,9},{2,18},{10... | collective-permute-start | bytes 4325384 | tf_op jit(solution)/shard_map/ppermute | solution.py:419
  770.8 27.1 %collective-permute-start.47 = (bf16[256,2816]{1,0:T(8,128)(2,1)}, bf16[256,2816]{1,0:T(8,128)(2,1)}, u32[]{:S(2)}, u32[]{:S(2)}) collective-permute-start(bf16[256,2816]{1,0:T(8,128)(2,1)} %reduce-scatter.4.cloned.1.call-done), channel_id=1, source_target_pairs={{0,8},{8,0},{16,24},{24,16},{1,9},{9,1},{17,25},{25,17},{2,10},{10... | collective-permute-start | bytes 4325384 | tf_op jit(solution)/shard_map/ppermute | solution.py:419
  781.0 115.1 %reduce-scatter.8.cloned.1.call-start = ((), (), s32[]{:S(2)}) async-start(), calls=%async_computation.7 | async-start | bytes 2949120 | tf_op jit(solution)/shard_map/reduce_scatter | solution.py:479
  787.6 22.6 %collective-permute-start.63 = (bf16[256,512]{1,0:T(8,128)(2,1)S(1)}, bf16[256,512]{1,0:T(8,128)(2,1)S(1)}, u32[]{:S(2)}, u32[]{:S(2)}) collective-permute-start(bf16[256,512]{1,0:T(8,128)(2,1)S(1)} %fusion.24), channel_id=1, source_target_pairs={{4,2},{5,3},{6,4},{7,5},{12,10},{13,11},{14,12},{15,13},{20,18},{2... | collective-permute-start | bytes 786440 | tf_op jit(solution)/shard_map/ppermute | solution.py:419
  797.9 35.1 %collective-permute-start.48 = (bf16[256,2816]{1,0:T(8,128)(2,1)}, bf16[256,2816]{1,0:T(8,128)(2,1)S(1)}, u32[]{:S(2)}, u32[]{:S(2)}) collective-permute-start(bf16[256,2816]{1,0:T(8,128)(2,1)} %collective-permute-done.45), channel_id=1, source_target_pairs={{0,8},{8,0},{16,24},{24,16},{1,9},{9,1},{17,25},{25,17},{2,10},{10... | collective-permute-start | bytes 4325384 | tf_op jit(solution)/shard_map/ppermute | solution.py:419
  806.9 15.1 %collective-permute-start.61 = (bf16[256,512]{1,0:T(8,128)(2,1)S(1)}, bf16[256,512]{1,0:T(8,128)(2,1)S(1)}, u32[]{:S(2)}, u32[]{:S(2)}) collective-permute-start(bf16[256,512]{1,0:T(8,128)(2,1)S(1)} %copy-done.76), channel_id=1, source_target_pairs={{0,2},{1,3},{2,4},{3,5},{4,6},{5,7},{8,10},{9,11},{10,12},{11,13},... | collective-permute-start | bytes 786440 | tf_op jit(solution)/shard_map/ppermute | solution.py:419
  810.3 21.5 %collective-permute-start.64 = (bf16[256,512]{1,0:T(8,128)(2,1)S(1)}, bf16[256,512]{1,0:T(8,128)(2,1)S(1)}, u32[]{:S(2)}, u32[]{:S(2)}) collective-permute-start(bf16[256,512]{1,0:T(8,128)(2,1)S(1)} %add_convert_fusion.8), channel_id=1, source_target_pairs={{2,0},{3,1},{4,2},{5,3},{6,4},{7,5},{10,8},{11,9},{12,10},{13,11},... | collective-permute-start | bytes 786440 | tf_op jit(solution)/shard_map/ppermute | solution.py:419
  811.8 21.0 %collective-permute-start.55 = (bf16[176,2048]{1,0:T(8,128)(2,1)S(1)}, bf16[176,2048]{1,0:T(8,128)(2,1)}, u32[]{:S(2)}, u32[]{:S(2)}) collective-permute-start(bf16[176,2048]{1,0:T(8,128)(2,1)S(1)} %add_convert_fusion.4), channel_id=1, source_target_pairs={{0,16},{8,24},{16,0},{24,8},{1,17},{9,25},{17,1},{25,9},{2,18},{10... | collective-permute-start | bytes 2162696 | tf_op jit(solution)/shard_map/ppermute | solution.py:419
  832.9 21.1 %collective-permute-start.65 = (bf16[256,512]{1,0:T(8,128)(2,1)S(1)}, bf16[256,512]{1,0:T(8,128)(2,1)S(1)}, u32[]{:S(2)}, u32[]{:S(2)}) collective-permute-start(bf16[256,512]{1,0:T(8,128)(2,1)S(1)} %add_convert_fusion.7), channel_id=1, source_target_pairs={{0,16},{8,24},{16,0},{24,8},{1,17},{9,25},{17,1},{25,9},{2,18},{10... | collective-permute-start | bytes 786440 | tf_op jit(solution)/shard_map/ppermute | solution.py:419
  853.9 16.8 %collective-permute-start.67 = (bf16[256,512]{1,0:T(8,128)(2,1)S(1)}, bf16[256,512]{1,0:T(8,128)(2,1)}, u32[]{:S(2)}, u32[]{:S(2)}) collective-permute-start(bf16[256,512]{1,0:T(8,128)(2,1)S(1)} %collective-permute-done.65), channel_id=1, source_target_pairs={{0,8},{8,0},{16,24},{24,16},{1,9},{9,1},{17,25},{25,17},{2,10},{10... | collective-permute-start | bytes 786440 | tf_op jit(solution)/shard_map/ppermute | solution.py:419
  870.1 13.2 %collective-permute-start.73 = (bf16[256,1024]{1,0:T(8,128)(2,1)S(1)}, bf16[256,1024]{1,0:T(8,128)(2,1)S(1)}, u32[]{:S(2)}, u32[]{:S(2)}) collective-permute-start(bf16[256,1024]{1,0:T(8,128)(2,1)S(1)} %copy-done.67), channel_id=1, source_target_pairs={{0,16},{8,24},{16,0},{24,8},{1,17},{9,25},{17,1},{25,9},{2,18},{10... | collective-permute-start | bytes 1572872 | tf_op jit(solution)/shard_map/ppermute | solution.py:419
  870.8 12.5 %collective-permute-start.74 = (bf16[256,1024]{1,0:T(8,128)(2,1)S(1)}, bf16[256,1024]{1,0:T(8,128)(2,1)S(1)}, u32[]{:S(2)}, u32[]{:S(2)}) collective-permute-start(bf16[256,1024]{1,0:T(8,128)(2,1)S(1)} %copy-done.67), channel_id=1, source_target_pairs={{0,8},{8,0},{16,24},{24,16},{1,9},{9,1},{17,25},{25,17},{2,10},{10... | collective-permute-start | bytes 1572872 | tf_op jit(solution)/shard_map/ppermute | solution.py:419
  896.1 14.2 %collective-permute-start.76 = (bf16[256,1152]{0,1:T(8,128)(2,1)}, bf16[256,1152]{0,1:T(8,128)(2,1)S(1)}, u32[]{:S(2)}, u32[]{:S(2)}) collective-permute-start(bf16[256,1152]{0,1:T(8,128)(2,1)} %reduce-scatter.8.cloned.1.call-done), channel_id=1, source_target_pairs={{0,16},{8,24},{16,0},{24,8},{1,17},{9,25},{17,1},{25,9},{2,18},{10... | collective-permute-start | bytes 1769480 | tf_op jit(solution)/shard_map/ppermute | solution.py:419
  897.3 13.0 %collective-permute-start.77 = (bf16[256,1152]{0,1:T(8,128)(2,1)}, bf16[256,1152]{0,1:T(8,128)(2,1)S(1)}, u32[]{:S(2)}, u32[]{:S(2)}) collective-permute-start(bf16[256,1152]{0,1:T(8,128)(2,1)} %reduce-scatter.8.cloned.1.call-done), channel_id=1, source_target_pairs={{0,8},{8,0},{16,24},{24,16},{1,9},{9,1},{17,25},{25,17},{2,10},{10... | collective-permute-start | bytes 1769480 | tf_op jit(solution)/shard_map/ppermute | solution.py:419
  910.3 18.1 %collective-permute-start.78 = (bf16[256,1152]{0,1:T(8,128)(2,1)S(1)}, bf16[256,1152]{0,1:T(8,128)(2,1)S(1)}, u32[]{:S(2)}, u32[]{:S(2)}) collective-permute-start(bf16[256,1152]{0,1:T(8,128)(2,1)S(1)} %collective-permute-done.76), channel_id=1, source_target_pairs={{0,8},{8,0},{16,24},{24,16},{1,9},{9,1},{17,25},{25,17},{2,10},{10... | collective-permute-start | bytes 1769480 | tf_op jit(solution)/shard_map/ppermute | solution.py:419
  (106 other events, 1347.1 us)
Sparse Core Ops, SparseCore 0:
  20.3 192.9 all-gather.2
  216.0 165.3 all-gather.4
  434.4 225.6 reduce-scatter.3
  781.1 59.3 reduce-scatter.5
  845.2 50.8 reduce-scatter.7

commit v3 on v2

--- a/solution.py
+++ b/solution.py
@@ -140,9 +140,12 @@
     ]
 
 
-def solve(lower, inverse, right, dims=NN):
-    result = one_pass(inverse, right, dims)
-    return result + one_pass(inverse, right - result - three_pass(lower, result, dims), dims)
+def solve_all(lowers, inverses, rights, dims=NN):
+    results = [one_pass(inverse, right, dims) for inverse, right in zip(inverses, rights)]
+    lefts = [
+        right - result - three_pass(lower, result, dims) for lower, right, result in zip(lowers, rights, results)
+    ]
+    return [result + one_pass(inverse, left, dims) for result, inverse, left in zip(results, inverses, lefts)]
 
 
 def forward_kernel(cfg, step, rank_ref, len_ref, log_ref, bias_ref, pre_ref, taps_ref, gain_ref, *refs):
@@ -159,10 +162,10 @@
         parts.append(head_parts(pre_ref, taps_ref, small, head, local, heads_local, head_size, heads_all, log_ref[head], bias_ref[head], geo))
     lowers = [p["beta"] * p["fall_strict"] * p["keys"] for p in parts]
     inverses = unit_inverses(lowers)
-    for local, (p, lower, inverse) in enumerate(zip(parts, lowers, inverses)):
+    updates = solve_all(lowers, inverses, [p["beta"] * p["value"].astype(F32) for p in parts])
+    mixeds = [dot_use(p["scores"] * p["fall"], update) for p, update in zip(parts, updates)]
+    for local, (p, inverse, mixed) in enumerate(zip(parts, inverses, mixeds)):
         inv_ref[0, local] = inverse
-        update = solve(lower, inverse, p["beta"] * p["value"].astype(F32))
-        mixed = dot_use(p["scores"] * p["fall"], update)
         scale = lax.rsqrt(jnp.mean(mixed * mixed, axis=1, keepdims=True) + EPS)
         gate = p["gate"]
         out = mixed * scale * gain_ref[...] * (gate * jax.nn.sigmoid(gate))
@@ -184,42 +187,53 @@
     dsmall = jnp.zeros_like(small)
     lanes = lax.broadcasted_iota(jnp.int32, small.shape, 1)
     row_lanes = lax.broadcasted_iota(jnp.int32, (1, ddecay_ref.shape[1]), 1)
-    for local in range(heads_local):
-        head = rank_ref[0] * heads_local + local
-        p = head_parts(pre_ref, taps_ref, small, head, local, heads_local, head_size, heads_all, log_ref[head], bias_ref[head], geo)
-        at = lambda part: slice(part * width + local * head_size, part * width + (local + 1) * head_size)
-        query, key, value, beta = p["query"], p["key"], p["value"], p["beta"]
-        value_f = value.astype(F32)
-        inverse = inv_ref[0, local]
-        spread_keys = p["fall_strict"] * p["keys"]
-        lower = beta * spread_keys
-        update = solve(lower, inverse, beta * value_f)
-        attn = p["scores"] * p["fall"]
-        mixed = dot_use(attn, update)
+    everyone = range(heads_local)
+    heads = [rank_ref[0] * heads_local + local for local in everyone]
+    at = lambda part, local: slice(part * width + local * head_size, part * width + (local + 1) * head_size)
+    ps = [
+        head_parts(pre_ref, taps_ref, small, head, local, heads_local, head_size, heads_all, log_ref[head], bias_ref[head], geo)
+        for local, head in zip(everyone, heads)
+    ]
+    gain = gain_ref[...]
+    betas = [p["beta"] for p in ps]
+    values = [p["value"].astype(F32) for p in ps]
+    inverses = [inv_ref[0, local] for local in everyone]
+    spreads = [p["fall_strict"] * p["keys"] for p in ps]
+    lowers = [beta * spread for beta, spread in zip(betas, spreads)]
+    attns = [p["scores"] * p["fall"] for p in ps]
+    updates = solve_all(lowers, inverses, [beta * value for beta, value in zip(betas, values)])
+    mixeds = [dot_use(attn, update) for attn, update in zip(attns, updates)]
+    dmixeds = []
+    for local, (p, mixed) in enumerate(zip(ps, mixeds)):
         lanes_of = slice(local * head_size, (local + 1) * head_size)
         grad = own_ref[:, lanes_of].astype(F32) + near_ref[:, lanes_of].astype(F32) + far_ref[:, lanes_of].astype(F32)
-        gate, gain = p["gate"], gain_ref[...]
+        gate = p["gate"]
         sig = jax.nn.sigmoid(gate)
         opened = gate * sig
         scale = lax.rsqrt(jnp.mean(mixed * mixed, axis=1, keepdims=True) + EPS)
         normed = mixed * scale
-        dgate = grad * normed * gain * (sig * (1.0 + gate * (1.0 - sig)))
+        dpre_ref[:, at(3, local)] = (grad * normed * gain * (sig * (1.0 + gate * (1.0 - sig)))).astype(BF)
         dgain_ref[...] += jnp.sum(grad * opened * normed, axis=0, keepdims=True)
         dnormed = grad * opened * gain
-        dmixed = scale * (dnormed - normed * jnp.mean(dnormed * normed, axis=1, keepdims=True))
-        dupdate = dot_use(attn, dmixed, TN)
-        dattn = jnp.where(within, dot_use(dmixed, update, NT), 0.0)
-        dright = solve(lower, inverse, dupdate, TN)
-        dlower = jnp.where(strict, -dot_use(dright, update, NT), 0.0)
-        dvalue = beta * dright
-        dbeta = jnp.sum(dright * value_f, axis=1, keepdims=True) + jnp.sum(dlower * spread_keys, axis=1, keepdims=True)
-        dscores = dattn * p["fall"]
-        dkeys = dlower * beta * p["fall_strict"]
-        dquery = two_pass(dscores, key)
-        dkey = two_pass(dscores, query, TN) + two_pass(dkeys, key) + two_pass(dkeys, key, TN)
-        pairs = dattn * attn + dlower * lower
+        dmixeds.append(scale * (dnormed - normed * jnp.mean(dnormed * normed, axis=1, keepdims=True)))
+    dupdates = [dot_use(attn, dmixed, TN) for attn, dmixed in zip(attns, dmixeds)]
+    dattns = [jnp.where(within, dot_use(dmixed, update, NT), 0.0) for dmixed, update in zip(dmixeds, updates)]
+    drights = solve_all(lowers, inverses, dupdates, TN)
+    dlowers = [jnp.where(strict, -dot_use(dright, update, NT), 0.0) for dright, update in zip(drights, updates)]
+    dscores = [dattn * p["fall"] for dattn, p in zip(dattns, ps)]
+    dkeys = [dlower * beta * p["fall_strict"] for dlower, beta, p in zip(dlowers, betas, ps)]
+    dqueries = [two_pass(dscore, p["key"]) for dscore, p in zip(dscores, ps)]
+    dkey_rows = [
+        two_pass(dscore, p["query"], TN) + two_pass(dkey, p["key"]) + two_pass(dkey, p["key"], TN)
+        for dscore, dkey, p in zip(dscores, dkeys, ps)
+    ]
+    later = (col <= row) & (col - offset == row_start(row, len_ref, step))
+    for local, (head, p) in enumerate(zip(heads, ps)):
+        beta, dright, dlower, dattn = betas[local], drights[local], dlowers[local], dattns[local]
+        dbeta = jnp.sum(dright * values[local], axis=1, keepdims=True)
+        dbeta = dbeta + jnp.sum(dlower * spreads[local], axis=1, keepdims=True)
+        pairs = dattn * attns[local] + dlower * lowers[local]
         dtotal_row = to_row(jnp.sum(pairs, axis=1, keepdims=True), eye) - jnp.sum(pairs, axis=0, keepdims=True)
-        later = (col <= row) & (col - offset == row_start(row, len_ref, step))
         ddecay = jnp.sum(jnp.where(later, dtotal_row, 0.0), axis=1, keepdims=True)
         dshifted = ddecay * p["rate"] * jax.nn.sigmoid(p["shifted"])
         dlog = jnp.sum(ddecay * p["decay"], axis=0, keepdims=True)
@@ -228,7 +242,7 @@
         ddecay_ref[1:2] += jnp.where(row_lanes == head, dbias, 0.0)
         dsmall = dsmall + jnp.where(lanes == head, dshifted, 0.0)
         dsmall = dsmall + jnp.where(lanes == heads_all + head, dbeta * beta * (1.0 - beta), 0.0)
-        rounded = [g.astype(BF).astype(F32) for g in (dquery, dkey, dvalue)]
+        rounded = [g.astype(BF).astype(F32) for g in (dqueries[local], dkey_rows[local], beta * dright)]
         cq, ck = p["convs"][0], p["convs"][1]
         gq = rounded[0] * head_size**-0.5
         dconvs = [
@@ -240,13 +254,12 @@
             sig_c, total, taps, pre = p["sigs"][part], p["sums"][part], p["taps"][part], p["pres"][part]
             dsum = dconvs[part] * (sig_c * (1.0 + total * (1.0 - sig_c)))
             dpre = dsum * taps[0:1]
-            dtaps_ref[0:1, at(part)] += jnp.sum(dsum * pre, axis=0, keepdims=True)
+            dtaps_ref[0:1, at(part, local)] += jnp.sum(dsum * pre, axis=0, keepdims=True)
             for by in range(1, taps.shape[0]):
                 kept = jnp.where(offset >= by, dsum, 0.0)
-                dtaps_ref[by : by + 1, at(part)] += jnp.sum(kept * pltpu.roll(pre, by, 0), axis=0, keepdims=True)
+                dtaps_ref[by : by + 1, at(part, local)] += jnp.sum(kept * pltpu.roll(pre, by, 0), axis=0, keepdims=True)
                 dpre = dpre + pltpu.roll(kept, rows - by, 0) * taps[by : by + 1]
-            dpre_ref[:, at(part)] = dpre.astype(BF)
-        dpre_ref[:, at(3)] = dgate.astype(BF)
+            dpre_ref[:, at(part, local)] = dpre.astype(BF)
     dpre_ref[:, 4 * width :] = dsmall.astype(BF)
 
 
@@ -413,15 +426,15 @@
     def after(value, *others):
         return lax.optimization_barrier((value,) + others)[0] if others else value
 
-    last = {}
+    last, leaving = {}, {}
 
     def send(lane, value, axis, pairs):
         sent = lax.ppermute(after(value, *last.get(lane, ())), axis, pairs)
         last[lane] = (sent,)
         return sent
 
-    def pair(value):
-        return send("pair", value, "fsdp", [(f, f ^ 1) for f in range(shards)])
+    def pair(value, lane="pair"):
+        return send(lane, value, "fsdp", [(f, f ^ 1) for f in range(shards)])
 
     def across(value, bits):
         return send(("rank", min(bits, 2)), value, "replica", [(r, r ^ bits) for r in range(ranks)])
@@ -456,22 +469,8 @@
             total = total + term.astype(F32)
         return total.astype(BF)
 
-    def line_sum(part):
-        up = down = None
-        for k in range(1, 4):
-            up = hop(plus(part(4 - k), *([] if up is None else [up])), 1, range(k))
-            down = hop(plus(part(k), *([] if down is None else [down])), -1, range(4 - k, 4))
-        return [up, down]
-
     def scatter_whole(value):
         return lax.psum_scatter(value, "fsdp", scatter_dimension=0, tiled=True)
-
-    def scatter(part):
-        given = pair(jnp.stack([part(dz, 1) for dz in range(4)]))
-        return lambda *events: finish([plus(after(part(dz, 0), *events), given[dz]) for dz in range(4)])
-
-    def finish(summed):
-        return plus(summed[0], *line_sum(lambda dz: summed[dz]))
 
     def scatter_along(value):
         lines = [[2 * at + y for at in range(ring)] for y in range(2)]
@@ -483,7 +482,8 @@
         return [value, across(value, 1), two, across(two, 1)]
 
     def scatter_group(parts):
-        far = across(plus(parts[2], across(parts[3], 1)), 2)
+        leaving["far"] = plus(parts[2], across(parts[3], 1))
+        far = across(leaving["far"], 2)
         return parts[0], across(parts[1], 1), far
 
     def by_rank(pieces, rank):
@@ -549,19 +549,31 @@
         full_gu = Pieces([(whole_gu, 0)], model)
         full_down = Pieces(got_d, hidden_cols)
 
-        info = [rank]
+        info = [rank, y]
         by_slot = lambda cols: pl.BlockSpec((rows, cols), lambda i, info: (i ^ info[0], 0))
         by_row = lambda cols: pl.BlockSpec((rows, cols), lambda i, info: (i, 0))
         a_row = pl.BlockSpec((1, 1, rows), lambda i, info: (i, 0, 0))
         lanes_of = lambda info, j: pl.ds(pl.multiple_of((info[0] ^ j) * width, 128), width)
         own_lanes = lambda info: lanes_of(info, 0)
         gain_rows = 16
+        split = 2 if by_line else 1
+        kept_cols = model // split
+
+        def write_split(info, value_ref, refs):
+            if not by_line:
+                refs[0][...] = value_ref[...]
+                return
+            for other, ref in enumerate(refs):
+                for at in range(ring):
+                    first = (2 * at + (info[1] ^ other)) * piece_rows
+                    ref[:, at * piece_rows : (at + 1) * piece_rows] = value_ref[:, pl.ds(pl.multiple_of(first, 128), piece_rows)]
+
 
         def enter_body(info, ins, weights, outs, extra):
             (w_ref,) = weights
             x_refs = ins
-            pre_ref, normed_ref, x_own_ref, lane_ref = outs
-            (x_ref,) = extra
+            pre_ref, x_own_ref, lane_ref = outs[0], outs[1 + split], outs[2 + split]
+            x_ref, normed_ref = extra
             step = pl.program_id(0)
 
             @pl.when(step == 0)
@@ -582,24 +594,25 @@
             scale = lax.rsqrt(jnp.mean(x * x, axis=1, keepdims=True) + EPS)
             normed = (x * scale * lane_ref[0:1]).astype(BF)
             normed_ref[...] = normed
+            write_split(info, normed_ref, outs[1 : 1 + split])
             pre_ref[...] = dot(normed, w_ref[...])
 
         slot = pl.BlockSpec((rows, model), lambda i, info: (0, 0))
         entered = []
         for first in (0, 2):
-            some = lambda cols: pl.BlockSpec((rows, cols), lambda i, info: ((i + info[1]) ^ info[0], 0))
+            some = lambda cols: pl.BlockSpec((rows, cols), lambda i, info: ((i + info[2]) ^ info[0], 0))
             entered.append(kernel_call(
-                enter_body, "enter", 11, (2,), [rank, first],
+                enter_body, "enter", 11, (2,), [rank, y, first],
                 [(x, whole(x)) for x in token_slots[first : first + 2]], [full_in],
                 [
-                    ((group, in_cols), F32, some(in_cols)), ((group, model), BF, some(model)),
+                    ((group, in_cols), F32, some(in_cols)), *[((group, kept_cols), BF, some(kept_cols))] * split,
                     ((group, width), BF, some(width)),
                     ((gain_rows, model), F32, pl.BlockSpec((gain_rows, model), lambda i, info: (0, 0))),
                 ],
-                [pltpu.VMEM((rows, model), BF)], entered[0][:3] if entered else (),
+                [pltpu.VMEM((rows, model), BF)] * 2, entered[0][: 2 + split] if entered else (),
             ))
-        pre, normed, x_cols = entered[1][:3]
-        lanes = entered[0][3]
+        pre, normed, x_cols = entered[1][0], entered[1][1 : 1 + split], entered[1][1 + split]
+        lanes = entered[0][2 + split]
         gain_one = lanes[0]
         own_gain = pl.BlockSpec((1, width), lambda i, info: (0, 0))
         gain_two = lax.dynamic_slice_in_dim(lanes[1:2], rank * width, width, axis=1)
@@ -621,9 +634,11 @@
         def leave_body(info, ins, weights, outs, extra):
             (w_ref,) = weights
             x_ref, gain_ref = ins[ranks:]
-            all_ref, resid_ref, branch_ref, scaled_ref, square_ref = outs
+            resid_ref, branch_ref, scaled_ref, square_ref = outs[split:]
+            (all_ref,) = extra
             for j in range(ranks):
                 all_ref[:, lanes_of(info, j)] = ins[j][...]
+            write_split(info, all_ref, outs[:split])
             branch = dot(all_ref[...], w_ref[...])
             resid = x_ref[...].astype(F32) + branch
             resid_ref[...] = resid
@@ -631,15 +646,16 @@
             scaled_ref[...] = (resid * gain_ref[...]).astype(BF)
             square_ref[0] = to_row(jnp.sum(resid * resid, axis=1, keepdims=True), diagonal(rows))
 
-        gated_all, resid, branch, scaled, square = kernel_call(
+        *gated_all, resid, branch, scaled, square = kernel_call(
             leave_body, "leave", 9, (buffers,), info,
             [(g, by_row(width)) for g in gather_group(gated)] + [(x_cols, by_row(width)), (gain_two, own_gain)],
             [full_out],
             [
-                ((group, model), BF, by_row(model)), ((group, width), F32, by_row(width)),
+                *[((group, kept_cols), BF, by_row(kept_cols))] * split, ((group, width), F32, by_row(width)),
                 ((group, width), F32, by_row(width)), ((group, width), BF, by_row(width)),
                 ((buffers, 1, rows), F32, a_row),
             ],
+            [pltpu.VMEM((rows, model), BF)],
         )
         squares = gather_group(square)
 
@@ -651,7 +667,8 @@
 
         def hidden_body(info, ins, weights, outs, extra):
             w_ref, d_ref = weights
-            all_ref, hidden_ref, grad_ref, stat_ref, u_ref, u_own_ref = outs
+            hidden_ref, grad_ref, stat_ref, u_ref, u_own_ref = outs[split:]
+            (all_ref,) = extra
             for j in range(ranks):
                 @pl.when(pl.program_id(0) ^ info[0] == j)
                 def _():
@@ -660,6 +677,7 @@
             u_own_ref[...] = u_ref[:, own_lanes(info)]
             for j in range(ranks):
                 all_ref[:, lanes_of(info, j)] = ins[j][...]
+            write_split(info, all_ref, outs[:split])
             inv = inverse_scale(ins[ranks : 2 * ranks])
             raw_gate = dot(all_ref[...], w_ref[:, :hidden_cols])
             raw_up = dot(all_ref[...], w_ref[:, hidden_cols:])
@@ -676,16 +694,17 @@
             stat = jnp.sum(raw_gate * grad_gate.astype(F32) + raw_up * grad_up.astype(F32), axis=1, keepdims=True)
             stat_ref[0] = to_row(stat, diagonal(rows))
 
-        scaled_all, hidden_b, grad_gu, stat, upstream, u_cols = kernel_call(
+        *scaled_all, hidden_b, grad_gu, stat, upstream, u_cols = kernel_call(
             hidden_body, "hidden", 33, (buffers,), info,
             [(s, by_row(width)) for s in gather_group(scaled)] + [(s, a_row) for s in squares]
             + [(u, slot) for u in upstream_slots],
             [full_gu, full_down],
             [
-                ((group, model), BF, by_row(model)), ((group, hidden_cols), BF, by_row(hidden_cols)),
+                *[((group, kept_cols), BF, by_row(kept_cols))] * split, ((group, hidden_cols), BF, by_row(hidden_cols)),
                 ((group, 2 * hidden_cols), BF, by_row(2 * hidden_cols)), ((buffers, 1, rows), F32, a_row),
                 ((group, model), BF, by_row(model)), ((group, width), BF, by_row(width)),
             ],
+            [pltpu.VMEM((rows, model), BF)],
         )
         stats = gather_group(stat)
 
@@ -693,21 +712,31 @@
             for j in range(ranks):
                 outs[j][...] = dot(ins[0][...], weights[0][lanes_of(info, j)], NT).astype(BF)
 
-        d_gu = dot(scaled_all, grad_gu, TN).astype(BF)
-        share_gu = scatter_whole(d_gu)
+        def scattered(lefts, right, piece, *begin):
+            if not by_line:
+                value = dot(lefts[0], right, TN).astype(BF)
+                return value, lambda *events: (scatter_whole(value), value)
+            kept, sent = (dot(left, right, TN).astype(BF) for left in lefts)
+            return exchanged(kept, sent, piece, *begin)
+
+        def exchanged(kept, sent, piece, *begin):
+            given = lax.ppermute(after(sent, *begin), "fsdp", [(f, f ^ 1) for f in range(shards)])
+
+            def end(*events):
+                total = plus(after(kept, *events), given)
+                return scatter_along(total.reshape(ring, piece, -1)), total
+
+            return sent, end
+
+        sent_gate, end_gate = scattered(scaled_all, grad_gu[:, :hidden_cols], piece_rows)
         parts = kernel_call(
-            back_body, "back", 19, (buffers,), info, [(after(grad_gu, d_gu), by_row(2 * hidden_cols))], [full_gu],
+            back_body, "back", 19, (buffers,), info, [(after(grad_gu, sent_gate), by_row(2 * hidden_cols))], [full_gu],
             [((group, width), BF, by_row(width))] * ranks,
         )
         terms_two = scatter_group(parts)
 
-        def scattered(value, piece):
-            if not by_line:
-                return lambda *events: scatter_whole(value)
-            return scatter(lambda dz, dy: lax.dynamic_slice_in_dim(value, owner(dz, dy) * piece, piece, axis=0))
-
+        sent_up, end_up = scattered(scaled_all, grad_gu[:, hidden_cols:], piece_rows, parts[0])
         d_down = dot(hidden_b, upstream, TN).astype(BF)
-        end_d = scattered(d_down, hidden_piece)
 
         def turn_body(info, ins, weights, outs, extra):
             (w_ref,) = weights
@@ -735,14 +764,19 @@
         turned = kernel_call(
             turn_body, "turn", 9, (buffers,), info,
             [(t, by_row(width)) for t in terms_two]
-            + [(after(resid, d_down), by_row(width)), (u_cols, by_row(width)), (gain_two, own_gain)]
+            + [(after(resid, d_down, sent_up), by_row(width)), (u_cols, by_row(width)), (gain_two, own_gain)]
             + [(s, a_row) for s in squares] + [(s, a_row) for s in stats],
             [full_out],
             [((group, width), BF, by_row(width))] * (1 + ranks) + [((1, width), F32, own_gain)],
         )
         grad_branch, grad_mlp_gain = turned[0], turned[1 + ranks][0]
         terms_gated = scatter_group(turned[1 : 1 + ranks])
-        d_out = dot(gated_all, grad_branch, TN).astype(BF)
+        if by_line:
+            placed = d_down.reshape(ring, 2, hidden_piece, model)
+            side = lambda at: lax.dynamic_index_in_dim(placed, at, 1, keepdims=False).reshape(ring * hidden_piece, model)
+            _, end_down = exchanged(side(y), side(1 - y), hidden_piece, grad_branch)
+        else:
+            end_down = lambda *events: (scatter_whole(d_down), d_down)
         own_block = lambda value, j: lax.dynamic_slice_in_dim(value, (rank ^ j) * rows, rows, axis=0)
 
         def to_tokens(value):
@@ -759,7 +793,7 @@
                     outs[j][...] = full[...].astype(BF)
 
         down = kernel_call(
-            down_body, "down", 14, (ranks,), info, [(hidden_b, by_slot(hidden_cols)), (branch, by_slot(width))], [full_down],
+            down_body, "down", 14, (ranks,), info, [(after(hidden_b, leaving["far"]), by_slot(hidden_cols)), (branch, by_slot(width))], [full_down],
             [((rows, model), BF, slot)] * ranks, [pltpu.VMEM((rows, model), F32)],
         )
         down_terms = scatter_group(down)
@@ -770,27 +804,22 @@
         grad_resid_own = to_tokens(grad_branch)
 
         made = ()
-        ahead = [(d_out, *down), (), (down_terms[2],), (grad_resid_own,)]
+        share_gate, _ = end_gate(down[0])
+        ahead = [tuple(down), (), (), (down_terms[2],)]
         for at in range(buffers):
             made = mixer_backward(
                 at, rank_arr, lengths, decay_log, decay_bias, after(pre, *ahead[at]), taps, head_gain[None], inverse,
                 terms_gated, heads_local, made,
             )
+            if at == 0:
+                _, end_out = scattered(gated_all, grad_branch, piece_rows, made[1])
+            if at == 1:
+                share_up, _ = end_up(made[1])
         d_pre, d_taps, d_head_gain, d_decay = made
         cuts = ((0, 2 * width), (2 * width, 2 * width + 128))
-        d_in = [dot(normed, d_pre[:, first : first + count], TN).astype(BF) for first, count in cuts]
-        in_sums = []
-        for value in d_in:
-            if by_line:
-                placed = value.reshape(ring, 2, piece_rows, value.shape[1])
-                given = pair(lax.dynamic_index_in_dim(placed, 1 - y, 1, keepdims=False))
-                in_sums.append(plus(lax.dynamic_index_in_dim(placed, y, 1, keepdims=False), given))
-            else:
-                in_sums.append(value)
-        along = scatter_along if by_line else scatter_whole
-        share_a = along(after(in_sums[0], share_gu))
-        share_b = along(after(in_sums[1], share_a))
-        end_o = scattered(d_out, piece_rows)
+        ends_in = [scattered(normed, d_pre[:, first : first + count], piece_rows) for first, count in cuts]
+        d_in = [sent for sent, _ in ends_in]
+        share_d, _ = end_down(*d_in)
 
         def first_body(info, ins, weights, outs, extra):
             result = dot(ins[0][...], weights[0][...], NT).astype(BF)
@@ -803,17 +832,51 @@
             first_body, "first", 19, (ranks,), info, [(after(d_pre, *d_in), by_slot(in_cols))], [full_in],
             [((rows, model), BF, slot)] * ranks,
         )
-        grad_one = sum(t.astype(F32) for t in scatter_group(grad_slots))
-        gu_slots = gather_group(share_gu)
-        share_d = end_d(grad_slots[0], down[0])
-        share_o = end_o(grad_slots[0], down[0])
-        d_slots, o_slots = gather_group(share_d), gather_group(share_o)
+        first_terms = scatter_group(grad_slots)
+        grad_one = sum(t.astype(F32) for t in first_terms)
+        share_o, sum_o = end_out(grad_slots[0])
+        share_a, sum_a = ends_in[0][1](sum_o, first_terms[2])
+        share_b, sum_b = ends_in[1][1](sum_a)
         x_own = tokens.astype(F32)
         inv_one = lax.rsqrt(jnp.mean(x_own * x_own, axis=-1, keepdims=True) + EPS)
         grad_attn_gain = jnp.sum(grad_one * x_own * inv_one, axis=0)
         pulled = gain_one * grad_one
         grad_x = inv_one * pulled - x_own * (inv_one**3 * jnp.mean(pulled * x_own, axis=-1, keepdims=True))
         grad_tokens = (grad_resid_own + grad_x).astype(BF)
+
+        def finish_body(info, ins, weights, outs, extra):
+            for j in range(ranks):
+                for at, out in enumerate(outs):
+                    out[:, lanes_of(info, j)] = ins[j][:, at * width : (at + 1) * width].astype(F32)
+
+        def finish(slots, count):
+            tile = piece_rows // 4
+            tiled = lambda cols: pl.BlockSpec((tile, cols), lambda i, info: (i, 0))
+            return kernel_call(
+                finish_body, "finish", 5, (4,), info, [(v, tiled(v.shape[1])) for v in slots], [],
+                [((piece_rows, model), F32, tiled(model))] * count,
+            )
+
+        def unhide_body(info, ins, weights, outs, extra):
+            (held,) = extra
+            for j in range(ranks):
+                held[info[0] ^ j] = ins[j][...]
+            for out in outs:
+                for f in range(shards):
+                    first = f * hidden_piece
+                    out[:, f * ranks * hidden_piece : (f + 1) * ranks * hidden_piece] = jnp.concatenate(
+                        [held[b, :, first : first + hidden_piece].astype(F32) for b in range(ranks)], axis=1
+                    )
+
+        def unhide(slots):
+            tile = piece_rows // 4
+            tiled = lambda cols: pl.BlockSpec((tile, cols), lambda i, info: (i, 0))
+            full = shards * ranks * hidden_piece
+            [result] = kernel_call(
+                unhide_body, "unhide", 8, (4,), info, [(v, tiled(v.shape[1])) for v in slots], [],
+                [((piece_rows, full), F32, tiled(full))], [pltpu.VMEM((ranks, tile, hidden_cols), BF)],
+            )
+            return result
 
         own_cols = lambda value: lax.dynamic_update_slice_in_dim(
             jnp.zeros(value.shape[:-1] + (model,), F32), value, rank * width, axis=value.ndim - 1
@@ -847,27 +910,20 @@
         at += head_gain.size
         sum_log, sum_bias = total[at : at + heads], total[at + heads : at + 2 * heads]
 
-        gu_all = by_rank(gu_slots, rank)
-        unhide = lambda first: (
-            jnp.stack([p[:, first : first + hidden_cols].reshape(piece_rows, shards, hidden_piece) for p in gu_all], axis=2)
-            .reshape(piece_rows, shards * ranks * hidden_piece)
-            .astype(F32)
-        )
-        out_gate, out_up = unhide(0), unhide(hidden_cols)
+        gate_slots, up_slots = gather_group(share_gate), gather_group(share_up)
+        out_gate = unhide(gate_slots)
+        d_slots = gather_group(after(share_d, out_gate))
+        out_up = unhide(up_slots)
+        o_slots = gather_group(after(share_o, out_up))
         out_down = jnp.concatenate(by_rank(d_slots, rank), axis=0).astype(F32)
-        out_output = jnp.concatenate(by_rank(o_slots, rank), axis=1).astype(F32)
-        a_all = by_rank(gather_group(share_a), rank)
-        out_query, out_key = (
-            jnp.concatenate([p[:, at * width : (at + 1) * width] for p in a_all], axis=1).astype(F32) for at in range(2)
-        )
+        a_slots = gather_group(after(share_a, out_down))
+        [out_output] = finish(o_slots, 1)
+        out_query, out_key = finish(a_slots, 2)
         finished = (out_gate, out_up, out_down, out_output, output, grad_tokens, sum_conv, out_query, out_key)
         share_b, *finished = lax.optimization_barrier((share_b, *finished))
         out_gate, out_up, out_down, out_output, output, grad_tokens, sum_conv, out_query, out_key = finished
         b_slots = gather_group(share_b)
-        b_all = by_rank(b_slots, rank)
-        out_value, out_outgate = (
-            jnp.concatenate([p[:, at * width : (at + 1) * width] for p in b_all], axis=1).astype(F32) for at in range(2)
-        )
+        out_value, out_outgate = finish(b_slots, 2)
         low = [p[:, 2 * width :].astype(F32) for p in b_slots]
         low = (low[0] + low[1]) + (low[2] + low[3])
         out_alpha, out_beta = low[:, :heads], low[:, heads : 2 * heads]

time: 954 us -> 917 us (0.961)
  waiting for transfers between devices: 351 us -> 418 us
  local copies, waits for them, and re-layouts: 103 us -> 48.7 us
  starting transfers between devices: 114 us -> 70.9 us
  other arithmetic: 76.2 us -> 52.2 us
  matrix products: 49.4 us -> 59.6 us
    ppermute x74 -> x61, starting transfers between devices: 113 us -> 63.9 us  [send(): sent = lax.ppermute(after(value, *last.get(lane, ())), axis, pairs)]
    ppermute x0 -> x6, waiting for transfers between devices: none -> 41.3 us  [exchanged(): lax.ppermute(after(sent, *begin), 'fsdp', [(f, f ^ 1) for f in range(shar...]
    pallas_call x8 -> x13, Pallas kernels: 135 us -> 166 us  [kernel_call(): pl.pallas_call(kernel, grid_spec=pltpu.PrefetchScalarGridSpec(num_scalar_...]
    ppermute x74 -> x61, waiting for transfers between devices: 300 us -> 327 us  [send(): sent = lax.ppermute(after(value, *last.get(lane, ())), axis, pairs)]
    unnamed x188 -> x128, local copies, waits for them, and re-layouts: 43.7 us -> 24.3 us
    pallas_call x4, Pallas kernels: 64.7 us -> 49.2 us  [mixer_backward(): pl.pallas_call(partial(backward_kernel, cfg, at), grid_spec=pltpu.Prefetc...]
    slice x20 -> x0, local copies, waits for them, and re-layouts: 13.1 us -> none  [the longest x12 11.4 us: on_device(): p[:, first:first + hidden_cols].reshape(piece_rows, shards, hidden_piece)]
    convert_element_type x7 -> x0, other arithmetic: 12.7 us -> none  [the longest x2 5.18 us: on_device(): unhide = lambda first: jnp.stack([p[:, first:first + hidden_cols].reshape...]
  transfers between devices with their start and end apart: 84 -> 80, of which waited for: 33 -> 43; matrix products, arithmetic and copies ran while one was open for 19% -> 15% of each run, Pallas kernels for 21% -> 22%
where the time goes in v3:
time: 917 us; the launch traced here: 909 us
  waiting for transfers between devices  418 us (46%)
  Pallas kernels  244 us (27%)
  starting transfers between devices  70.9 us (8%)
  matrix products  59.6 us (6%)
  other arithmetic  52.2 us (6%)
  local copies, waits for them, and re-layouts  48.7 us (5%)
  between operations  15.3 us (2%)
    ppermute x61, waiting for transfers between devices, send(): sent = lax.ppermute(after(value, *last.get(lane, ())), axis, pairs)  327 us
    pallas_call x13, Pallas kernels, kernel_call(): pl.pallas_call(kernel, grid_spec=pltpu.PrefetchScalarGridSpec(num_scalar_...  166 us
    ppermute x61, starting transfers between devices, send(): sent = lax.ppermute(after(value, *last.get(lane, ())), axis, pairs)  63.9 us
    dot_general x11, matrix products, dot(): return lax.dot_general(left, right, dims, preferred_element_type=F32)  59.6 us
    pallas_call x4, Pallas kernels, mixer_backward(): pl.pallas_call(partial(backward_kernel, cfg, at), grid_spec=pltpu.Prefetc...  49.2 us
    ppermute x6, waiting for transfers between devices, exchanged(): lax.ppermute(after(sent, *begin), 'fsdp', [(f, f ^ 1) for f in range(shar...  41.3 us
    all_gather x2, waiting for transfers between devices, gather_whole(): return lax.all_gather(piece, 'fsdp', axis=0, tiled=True)  41 us
    pallas_call x4, Pallas kernels, mixer_forward(): pl.pallas_call(partial(forward_kernel, cfg, at), grid_spec=pltpu.Prefetch...  28.7 us
  transfers between devices with their start and end apart: 80, of which 43 were waited for; matrix products, arithmetic and copies ran while one was open for 15% of the time, Pallas kernels for 22%

profile of v3, /device:TPU:1, one launch (start us, length us, event | category | flops | bytes accessed | tf_op | source)
XLA Modules:
  0.0 908.7 jit_solution(1147564326547563057)
XLA Ops:
  27.1 3.2 collective-permute-start.16
  32.9 16.9 %collective-permute-done.refs_0_ = bf16[272,2048]{1,0:T(8,128)(2,1)} collective-permute-done((bf16[272,2048]{1,0:T(8,128)(2,1)}, bf16[272,2048]{1,0:T(8,128)(2,1)}, u32[]{:S(2)}, u32[]{:S(2)}) %collective-permute-start) | collective-permute-done | bytes 1114144 | tf_op jit(solution)/shard_map/ppermute | solution.py:432
  51.6 8.1 collective-permute-done.16
  59.7 20.9 %collective-permute-done.17 = bf16[176,2048]{1,0:T(8,128)(2,1)} collective-permute-done((bf16[176,2048]{1,0:T(8,128)(2,1)}, bf16[176,2048]{1,0:T(8,128)(2,1)}, u32[]{:S(2)}, u32[]{:S(2)}) %collective-permute-start.17) | collective-permute-done | bytes 720928 | tf_op jit(solution)/shard_map/ppermute | solution.py:432
  88.0 10.1 %collective-permute-done.18.refs_16_.refs_5_ = bf16[176,2048]{1,0:T(8,128)(2,1)S(1)} collective-permute-done((bf16[176,2048]{1,0:T(8,128)(2,1)S(1)}, bf16[176,2048]{1,0:T(8,128)(2,1)S(1)}, u32[]{:S(2)}, u32[]{:S(2)}) %collective-permute-start.18) | collective-permute-done | bytes 720928 | tf_op jit(solution)/shard_map/ppermute | solution.py:432
  98.0 18.6 %collective-permute-done.20 = bf16[176,2048]{1,0:T(8,128)(2,1)} collective-permute-done((bf16[176,2048]{1,0:T(8,128)(2,1)}, bf16[176,2048]{1,0:T(8,128)(2,1)}, u32[]{:S(2)}, u32[]{:S(2)}) %collective-permute-start.20) | collective-permute-done | bytes 720928 | tf_op jit(solution)/shard_map/ppermute | solution.py:432
  123.8 60.7 %collective-permute-done.22 = bf16[176,2048]{1,0:T(8,128)(2,1)} collective-permute-done((bf16[176,2048]{1,0:T(8,128)(2,1)}, bf16[176,2048]{1,0:T(8,128)(2,1)}, u32[]{:S(2)}, u32[]{:S(2)}) %collective-permute-start.22) | collective-permute-done | bytes 720928 | tf_op jit(solution)/shard_map/ppermute | solution.py:432
  187.6 4.5 copy.76
  192.1 4.5 copy.75
  202.0 12.2 %all-gather.3.cloned.1.call-done.refs_2_.refs_6_.refs_14_.refs_1_ = bf16[2048,2688]{1,0:T(8,128)(2,1)} async-done(((bf16[256,2688]{1,0:T(8,128)(2,1)}), bf16[2048,2688]{1,0:T(8,128)(2,1)}) %all-gather.3.cloned.1.call-update) | async-done | bytes 11010064 | tf_op jit(solution)/shard_map/all_gather | solution.py:464
  217.5 14.8 %enter.2 = (f32[1024,2176]{1,0:T(8,128)}, bf16[1024,1024]{1,0:T(8,128)(2,1)}, bf16[1024,1024]{1,0:T(8,128)(2,1)}, bf16[1024,512]{1,0:T(8,128)(2,1)}, f32[16,2048]{1,0:T(8,128)}) custom-call(s32[4]{0:T(128)} %pad_add_fusion.2.info_ref, bf16[272,2048]{1,0:T(8,128)(2,1)} %fusion.20.refs_0_, bf16[272,2048]{1,0:T(8,128)(2,1)} %collective-permute-done.1.refs_1_, ...), custom_call_target="tpu_custom_call" | custom-call | flops 11000000 | bytes 1024 | tf_op jit(solution)/shard_map/enter/pallas_call | solution.py:396
  233.6 7.2 mixer_forward.4
  240.8 7.2 mixer_forward.5
  247.9 14.1 %enter.3 = (f32[1024,2176]{1,0:T(8,128)}, bf16[1024,1024]{1,0:T(8,128)(2,1)}, bf16[1024,1024]{1,0:T(8,128)(2,1)}, bf16[1024,512]{1,0:T(8,128)(2,1)}, f32[16,2048]{1,0:T(8,128)}) custom-call(s32[4]{0:T(128)} %pad_add_fusion.info_ref, ...), custom_call_target="tpu_custom_call", output_to_operand_aliasing={{0}: (4, {}), {1}: (5, {}), {2}: (6, {}), {3}: (7, {})} | custom-call | flops 11000000 | bytes 1024 | tf_op jit(solution)/shard_map/enter/pallas_call | solution.py:396
  262.1 7.2 mixer_forward.6
  269.3 7.2 mixer_forward.7
  279.3 22.6 %collective-permute-done.7.refs_2_ = bf16[1024,512]{1,0:T(8,128)(2,1)S(1)} collective-permute-done((bf16[1024,512]{1,0:T(8,128)(2,1)S(1)}, bf16[1024,512]{1,0:T(8,128)(2,1)S(1)}, u32[]{:S(2)}, u32[]{:S(2)}) %collective-permute-start.7) | collective-permute-done | bytes 1048608 | tf_op jit(solution)/shard_map/ppermute | solution.py:432
  305.9 10.5 %leave.1 = (bf16[1024,1024]{1,0:T(8,128)(2,1)}, bf16[1024,1024]{1,0:T(8,128)(2,1)}, f32[1024,512]{1,0:T(8,128)}, f32[1024,512]{1,0:T(8,128)}, bf16[1024,512]{1,0:T(8,128)(2,1)}, /*index=5*/f32[4,1,256]{2,1,0:T(1,128)}) custom-call(s32[3]{0:T(128)} %pad_add_fusion.3.info_ref, bf16[1024,512]{1,0:T(8,128)(2,1)} %copy-done.7, bf16[1024,512]{1,0:T(8,128)(2,1)} %copy-done.28, ...), custom_call_target="tpu_custom_call" | custom-call | flops 9000000 | bytes 1024 | tf_op jit(solution)/shard_map/leave/pallas_call | solution.py:396
  321.8 23.8 %collective-permute-done.13.refs_2_ = bf16[1024,512]{1,0:T(8,128)(2,1)S(1)} collective-permute-done((bf16[1024,512]{1,0:T(8,128)(2,1)}, bf16[1024,512]{1,0:T(8,128)(2,1)S(1)}, u32[]{:S(2)}, u32[]{:S(2)}) %collective-permute-start.13) | collective-permute-done | bytes 1048608 | tf_op jit(solution)/shard_map/ppermute | solution.py:432
  348.9 28.8 %all-gather.5.cloned.1.call-done.refs_12_.refs_1_ = bf16[2048,2816]{1,0:T(8,128)(2,1)} async-done(((bf16[256,2816]{1,0:T(8,128)(2,1)}), bf16[2048,2816]{1,0:T(8,128)(2,1)}) %all-gather.5.cloned.1.call-update) | async-done | bytes 11534352 | tf_op jit(solution)/shard_map/all_gather | solution.py:464
  377.7 35.4 %hidden.1 = (bf16[1024,1024]{1,0:T(8,128)(2,1)}, bf16[1024,1024]{1,0:T(8,128)(2,1)}, bf16[1024,1408]{1,0:T(8,128)(2,1)}, bf16[1024,2816]{1,0:T(8,128)(2,1)}, f32...) custom-call(s32[11]{0:T(128)} %stack.48.info_ref, ...), custom_call_target="tpu_custom_call" | custom-call | flops 33000000 | bytes 1024 | tf_op jit(solution)/shard_map/hidden/pallas_call | solution.py:396
  418.1 7.5 convolution_convert_fusion.6
  425.6 20.2 %back.1 = (bf16[1024,512]{1,0:T(8,128)(2,1)}, bf16[1024,512]{1,0:T(8,128)(2,1)}, bf16[1024,512]{1,0:T(8,128)(2,1)}, bf16[1024,512]{1,0:T(8,128)(2,1)}) custom-call(s32[3]{0:T(128)} %pad_add_fusion.3.info_ref, bf16[1024,2816]{1,0:T(8,128)(2,1)} %get-tuple-element.220.refs_0_, bf16[2048,2816]{1,0:T(8,128)(2,1)} %all-gather.5.cloned.1.call-done.refs_12_.refs_1_), custom_call_target="tpu_custom_call" | custom-call | flops 19000000 | bytes 1024 | tf_op jit(solution)/shard_map/back/pallas_call | solution.py:396
  451.8 10.9 %convolution_convert_fusion = bf16[1408,2048]{1,0:T(8,128)(2,1)} fusion(bf16[1024,1408]{1,0:T(8,128)(2,1)S(1)} %copy-done.18, bf16[1024,2048]{1,0:T(8,128)(2,1)} %get-tuple-element.233), kind=kOutput, calls=%fused_computation | convolution fusion | flops 5908463616 | bytes 12845056 | tf_op jit(solution)/shard_map/dot_general | solution.py:332
  462.7 4.9 convolution_convert_fusion.5
  467.5 7.5 collective-permute-done.30.refs_2_
  476.1 9.1 turn.1
  486.9 6.0 convolution_convert_fusion.4
  495.4 14.7 %down.1 = (bf16[256,2048]{1,0:T(8,128)(2,1)}, bf16[256,2048]{1,0:T(8,128)(2,1)}, bf16[256,2048]{1,0:T(8,128)(2,1)}, bf16[256,2048]{1,0:T(8,128)(2,1)}) custom-call(s32[10]{0:T(128)} %stack.47.info_ref, bf16[1024,1408]{1,0:T(8,128)(2,1)} %get-tuple-element.239.refs_0_, f32[1024,512]{1,0:T(8,128)} %get-tuple-element.240.refs_1_, ...), custom_call_target="tpu_custom_call" | custom-call | flops 14000000 | bytes 1024 | tf_op jit(solution)/shard_map/down/pallas_call | solution.py:396
  510.2 4.1 add_convert_fusion.2
  517.5 6.4 convolution_convert_fusion.3
  524.0 17.5 %collective-permute-done.34.far_ref = bf16[1024,512]{1,0:T(8,128)(2,1)S(1)} collective-permute-done((bf16[1024,512]{1,0:T(8,128)(2,1)}, bf16[1024,512]{1,0:T(8,128)(2,1)S(1)}, u32[]{:S(2)}, u32[]{:S(2)}) %collective-permute-start.34) | collective-permute-done | bytes 1048608 | tf_op jit(solution)/shard_map/ppermute | solution.py:432
  541.5 12.6 %mixer_backward.4 = (bf16[1024,2176]{1,0:T(8,128)(2,1)}, f32[4,1536]{1,0:T(4,128)S(1)}, f32[1,128]{1,0:T(1,128)S(1)}, f32[8,128]{1,0:T(8,128)S(1)}) custom-call(s32[1]{0:T(128)} %bitcast.rank_ref, s32[4,2]{1,0:T(4,128)S(1)} %maximum_convert_fusion.1.len_ref, f32[16]{0:T(128)S(1)} %copy-done.8, f32[16]{0:T(128)S(1)} %copy-done.9, ...), custom_call_target="tpu_custom_call" | custom-call | flops 12000000 | bytes 1024 | tf_op jit(solution)/shard_map/mixer_backward/pallas_call | solution.py:311
  554.1 12.0 %mixer_backward.5 = (bf16[1024,2176]{1,0:T(8,128)(2,1)}, f32[4,1536]{1,0:T(4,128)S(1)}, f32[1,128]{1,0:T(1,128)S(1)}, f32[8,128]{1,0:T(8,128)S(1)}) custom-call(s32[1]{0:T(128)} %bitcast.rank_ref, s32[4,2]{1,0:T(4,128)S(1)} %maximum_convert_fusion.1.len_ref, f32[16]{0:T(128)S(1)} %copy-done.8, f32[16]{0:T(128)S(1)} %copy-done.9, ...), custom_call_target="tpu_custom_call", output_to_operand_aliasing={{0}: (11, {})} | custom-call | flops 12000000 | bytes 1024 | tf_op jit(solution)/shard_map/mixer_backward/pallas_call | solution.py:311
  566.1 11.9 %collective-permute-done.50 = bf16[1024,1408]{1,0:T(8,128)(2,1)S(1)} collective-permute-done((bf16[1024,1408]{1,0:T(8,128)(2,1)}, bf16[1024,1408]{1,0:T(8,128)(2,1)S(1)}, u32[]{:S(2)}, u32[]{:S(2)}) %collective-permute-start.50) | collective-permute-done | bytes 2883616 | tf_op jit(solution)/shard_map/ppermute | solution.py:723
  582.7 3.3 constant_dynamic-slice_fusion.2
  589.9 12.0 %mixer_backward.6 = (bf16[1024,2176]{1,0:T(8,128)(2,1)}, f32[4,1536]{1,0:T(4,128)S(1)}, f32[1,128]{1,0:T(1,128)S(1)}, f32[8,128]{1,0:T(8,128)S(1)}) custom-call(s32[1]{0:T(128)} %bitcast.rank_ref, s32[4,2]{1,0:T(4,128)S(1)} %maximum_convert_fusion.1.len_ref, f32[16]{0:T(128)S(1)} %copy-done.8, f32[16]{0:T(128)S(1)} %copy-done.9, ...), custom_call_target="tpu_custom_call", output_to_operand_aliasing={{0}: (11, {})} | custom-call | flops 12000000 | bytes 1024 | tf_op jit(solution)/shard_map/mixer_backward/pallas_call | solution.py:311
  601.9 11.4 %collective-permute-done.35 = bf16[256,2048]{1,0:T(8,128)(2,1)S(1)} collective-permute-done((bf16[256,2048]{1,0:T(8,128)(2,1)S(1)}, bf16[256,2048]{1,0:T(8,128)(2,1)S(1)}, u32[]{:S(2)}, u32[]{:S(2)}) %collective-permute-start.35) | collective-permute-done | bytes 1048608 | tf_op jit(solution)/shard_map/ppermute | solution.py:432
  614.3 12.6 %mixer_backward.7 = (bf16[1024,2176]{1,0:T(8,128)(2,1)}, f32[4,1536]{1,0:T(4,128)S(1)}, f32[1,128]{1,0:T(1,128)S(1)}, f32[8,128]{1,0:T(8,128)S(1)}) custom-call(s32[1]{0:T(128)} %bitcast.rank_ref, s32[4,2]{1,0:T(4,128)S(1)} %maximum_convert_fusion.1.len_ref, f32[16]{0:T(128)S(1)} %copy-done.8, f32[16]{0:T(128)S(1)} %copy-done.9, ...), custom_call_target="tpu_custom_call", output_to_operand_aliasing={{0}: (11, {})} | custom-call | flops 12000000 | bytes 1024 | tf_op jit(solution)/shard_map/mixer_backward/pallas_call | solution.py:311
  626.9 5.5 convolution_convert_fusion.7
  632.4 4.4 convolution_convert_fusion.1
  636.8 13.4 %collective-permute-done.54 = bf16[704,2048]{1,0:T(8,128)(2,1)S(1)} collective-permute-done((bf16[704,2048]{1,0:T(8,128)(2,1)S(1)}, bf16[704,2048]{1,0:T(8,128)(2,1)S(1)}, u32[]{:S(2)}, u32[]{:S(2)}) %collective-permute-start.54) | collective-permute-done | bytes 2883616 | tf_op jit(solution)/shard_map/ppermute | solution.py:723
  654.2 4.0 convolution_convert_fusion.9
  660.5 18.8 %first.1 = (bf16[256,2048]{1,0:T(8,128)(2,1)}, bf16[256,2048]{1,0:T(8,128)(2,1)}, bf16[256,2048]{1,0:T(8,128)(2,1)}, bf16[256,2048]{1,0:T(8,128)(2,1)}) custom-call(s32[3]{0:T(128)} %pad_add_fusion.3.info_ref, bf16[1024,2176]{1,0:T(8,128)(2,1)} %get-tuple-element.270.refs_0_, bf16[2048,2688]{1,0:T(8,128)(2,1)} %all-gather.3.cloned.1.call-done.refs_2_.refs_6_.refs_14_.refs_1_), custom_call_target="tpu_custom_call" | custom-call | flops 19000000 | bytes 1024 | tf_op jit(solution)/shard_map/first/pallas_call | solution.py:396
  684.9 5.3 collective-permute-done.40
  694.3 5.5 collective-permute-done.41
  700.3 4.0 convolution_convert_fusion.8
  704.4 19.9 %collective-permute-done.42 = bf16[256,2048]{1,0:T(8,128)(2,1)S(1)} collective-permute-done((bf16[256,2048]{1,0:T(8,128)(2,1)S(1)}, bf16[256,2048]{1,0:T(8,128)(2,1)S(1)}, u32[]{:S(2)}, u32[]{:S(2)}) %collective-permute-start.42) | collective-permute-done | bytes 1048608 | tf_op jit(solution)/shard_map/ppermute | solution.py:432
  724.3 3.6 collective-permute-done.43
  736.7 15.8 %collective-permute-done.48.refs_2_ = bf16[256,1408]{1,0:T(8,128)(2,1)} collective-permute-done((bf16[256,1408]{1,0:T(8,128)(2,1)}, bf16[256,1408]{1,0:T(8,128)(2,1)}, u32[]{:S(2)}, u32[]{:S(2)}) %collective-permute-start.48) | collective-permute-done | bytes 720928 | tf_op jit(solution)/shard_map/ppermute | solution.py:432
  755.9 4.9 convolution_convert_fusion.2
  760.8 10.7 %collective-permute-done.52.refs_2_ = bf16[256,1408]{1,0:T(8,128)(2,1)} collective-permute-done((bf16[256,1408]{1,0:T(8,128)(2,1)}, bf16[256,1408]{1,0:T(8,128)(2,1)}, u32[]{:S(2)}, u32[]{:S(2)}) %collective-permute-start.52) | collective-permute-done | bytes 720928 | tf_op jit(solution)/shard_map/ppermute | solution.py:432
  772.2 12.4 %collective-permute-done.44 = bf16[1024,1152]{1,0:T(8,128)(2,1)} collective-permute-done((bf16[1024,1152]{1,0:T(8,128)(2,1)}, bf16[1024,1152]{1,0:T(8,128)(2,1)}, u32[]{:S(2)}, u32[]{:S(2)}) %collective-permute-start.44) | collective-permute-done | bytes 2359328 | tf_op jit(solution)/shard_map/ppermute | solution.py:723
  784.6 3.6 add_convert_fusion.3
  789.0 7.3 unhide.2
  799.4 14.0 %collective-permute-done.55 = bf16[176,2048]{1,0:T(8,128)(2,1)} collective-permute-done((bf16[176,2048]{1,0:T(8,128)(2,1)}, bf16[176,2048]{1,0:T(8,128)(2,1)}, u32[]{:S(2)}, u32[]{:S(2)}) %collective-permute-start.55) | collective-permute-done | bytes 720928 | tf_op jit(solution)/shard_map/ppermute | solution.py:432
  821.9 7.1 unhide.3
  832.1 4.7 collective-permute-done.59.refs_2_
  847.9 4.1 collective-permute-done.64
  855.6 4.0 fusion.13
  861.7 4.2 finish.3
  866.0 5.1 finish.4
  873.7 13.3 %collective-permute-done.70.refs_2_ = bf16[256,1152]{1,0:T(8,128)(2,1)} collective-permute-done((bf16[256,1152]{1,0:T(8,128)(2,1)}, bf16[256,1152]{1,0:T(8,128)(2,1)}, u32[]{:S(2)}, u32[]{:S(2)}) %collective-permute-start.70) | collective-permute-done | bytes 589856 | tf_op jit(solution)/shard_map/ppermute | solution.py:432
  896.7 5.0 finish.5
  (341 shorter events, 170.3 us)
Async XLA Ops:
  7.2 207.0 %all-gather.3.cloned.1.call-start = ((), (), s32[]{:S(2)}) async-start(), calls=%async_computation.6 | async-start | bytes 12386304 | tf_op jit(solution)/shard_map/all_gather | solution.py:464
  20.1 357.6 %all-gather.5.cloned.1.call-start = ((), (), s32[]{:S(2)}) async-start(), calls=%async_computation.7 | async-start | bytes 12976128 | tf_op jit(solution)/shard_map/all_gather | solution.py:464
  23.1 26.6 %collective-permute-start = (bf16[272,2048]{1,0:T(8,128)(2,1)}, bf16[272,2048]{1,0:T(8,128)(2,1)}, u32[]{:S(2)}, u32[]{:S(2)}) collective-permute-start(bf16[272,2048]{1,0:T(8,128)(2,1)} %fusion.20.refs_0_), channel_id=1, source_target_pairs={{0,16},{8,24},{16,0},{24,8},{1,17},{9,25},{17,1},{25,9},{2,18},{10... | collective-permute-start | bytes 3342344 | tf_op jit(solution)/shard_map/ppermute | solution.py:432
  25.2 24.6 %collective-permute-start.1 = (bf16[272,2048]{1,0:T(8,128)(2,1)}, bf16[272,2048]{1,0:T(8,128)(2,1)}, u32[]{:S(2)}, u32[]{:S(2)}) collective-permute-start(bf16[272,2048]{1,0:T(8,128)(2,1)} %fusion.20.refs_0_), channel_id=1, source_target_pairs={{0,8},{8,0},{16,24},{24,16},{1,9},{9,1},{17,25},{25,17},{2,10},{10... | collective-permute-start | bytes 3342344 | tf_op jit(solution)/shard_map/ppermute | solution.py:432
  27.1 32.6 %collective-permute-start.16 = (bf16[176,2048]{1,0:T(8,128)(2,1)}, bf16[176,2048]{1,0:T(8,128)(2,1)S(1)}, u32[]{:S(2)}, u32[]{:S(2)}) collective-permute-start(bf16[176,2048]{1,0:T(8,128)(2,1)} %constant_dynamic-slice_fusion.6.refs_13_.refs_2_), channel_id=1, source_target_pairs={{0,2},{1,3},{2,4},{3,5},{4,6},{5,7},{8,10},{9,11},{10,12},{11,13},... | collective-permute-start | bytes 2162696 | tf_op jit(solution)/shard_map/ppermute | solution.py:432
  30.3 50.2 %collective-permute-start.17 = (bf16[176,2048]{1,0:T(8,128)(2,1)}, bf16[176,2048]{1,0:T(8,128)(2,1)}, u32[]{:S(2)}, u32[]{:S(2)}) collective-permute-start(bf16[176,2048]{1,0:T(8,128)(2,1)} %constant_dynamic-slice_fusion.6.refs_13_.refs_2_), channel_id=1, source_target_pairs={{2,0},{3,1},{4,2},{5,3},{6,4},{7,5},{10,8},{11,9},{12,10},{13,11},... | collective-permute-start | bytes 2162696 | tf_op jit(solution)/shard_map/ppermute | solution.py:432
  31.6 50.1 %collective-permute-start.15 = (bf16[176,2048]{1,0:T(8,128)(2,1)}, bf16[176,2048]{1,0:T(8,128)(2,1)S(1)}, u32[]{:S(2)}, u32[]{:S(2)}) collective-permute-start(bf16[176,2048]{1,0:T(8,128)(2,1)} %constant_dynamic-slice_fusion.6.refs_13_.refs_2_), channel_id=1, source_target_pairs={{0,1},{1,0},{2,3},{3,2},{4,5},{5,4},{6,7},{7,6},{8,9},{9,8},{10,11... | collective-permute-start | bytes 2162696 | tf_op jit(solution)/shard_map/ppermute | solution.py:432
  49.8 36.2 %collective-permute-start.2 = (bf16[272,2048]{1,0:T(8,128)(2,1)}, bf16[272,2048]{1,0:T(8,128)(2,1)S(1)}, u32[]{:S(2)}, u32[]{:S(2)}) collective-permute-start(bf16[272,2048]{1,0:T(8,128)(2,1)} %collective-permute-done.refs_0_), channel_id=1, source_target_pairs={{0,8},{8,0},{16,24},{24,16},{1,9},{9,1},{17,25},{25,17},{2,10},{10... | collective-permute-start | bytes 3342344 | tf_op jit(solution)/shard_map/ppermute | solution.py:432
  81.7 16.3 %collective-permute-start.18 = (bf16[176,2048]{1,0:T(8,128)(2,1)S(1)}, bf16[176,2048]{1,0:T(8,128)(2,1)S(1)}, u32[]{:S(2)}, u32[]{:S(2)}) collective-permute-start(bf16[176,2048]{1,0:T(8,128)(2,1)S(1)} %broadcast_select_fusion.9.refs_15_.refs_4_), channel_id=1, source_target_pairs={{0,1},{1,0},{2,3},{3,2},{4,5},{5,4},{6,7},{7,6},{8,9},{9,8},{10,11... | collective-permute-start | bytes 2162696 | tf_op jit(solution)/shard_map/ppermute | solution.py:432
  83.0 35.0 %collective-permute-start.19 = (bf16[176,2048]{1,0:T(8,128)(2,1)S(1)}, bf16[176,2048]{1,0:T(8,128)(2,1)}, u32[]{:S(2)}, u32[]{:S(2)}) collective-permute-start(bf16[176,2048]{1,0:T(8,128)(2,1)S(1)} %collective-permute-done.16), channel_id=1, source_target_pairs={{2,4},{3,5},{4,6},{5,7},{10,12},{11,13},{12,14},{13,15},{18,20},{1... | collective-permute-start | bytes 2162696 | tf_op jit(solution)/shard_map/ppermute | solution.py:432
  84.5 32.2 %collective-permute-start.20 = (bf16[176,2048]{1,0:T(8,128)(2,1)}, bf16[176,2048]{1,0:T(8,128)(2,1)}, u32[]{:S(2)}, u32[]{:S(2)}) collective-permute-start(bf16[176,2048]{1,0:T(8,128)(2,1)} %collective-permute-done.17), channel_id=1, source_target_pairs={{2,0},{3,1},{4,2},{5,3},{10,8},{11,9},{12,10},{13,11},{18,16},{19,... | collective-permute-start | bytes 2162696 | tf_op jit(solution)/shard_map/ppermute | solution.py:432
  85.9 35.9 %collective-permute-start.3 = (bf16[256,2048]{1,0:T(8,128)(2,1)S(1)}, bf16[256,2048]{1,0:T(8,128)(2,1)}, u32[]{:S(2)}, u32[]{:S(2)}) collective-permute-start(bf16[256,2048]{1,0:T(8,128)(2,1)S(1)} %broadcast_multiply_fusion.refs_8_), channel_id=1, source_target_pairs={{0,16},{8,24},{16,0},{24,8},{1,17},{9,25},{17,1},{25,9},{2,18},{10... | collective-permute-start | bytes 3145736 | tf_op jit(solution)/shard_map/ppermute | solution.py:432
  86.0 35.8 %collective-permute-start.4 = (bf16[256,2048]{1,0:T(8,128)(2,1)S(1)}, bf16[256,2048]{1,0:T(8,128)(2,1)}, u32[]{:S(2)}, u32[]{:S(2)}) collective-permute-start(bf16[256,2048]{1,0:T(8,128)(2,1)S(1)} %broadcast_multiply_fusion.refs_8_), channel_id=1, source_target_pairs={{0,8},{8,0},{16,24},{24,16},{1,9},{9,1},{17,25},{25,17},{2,10},{10... | collective-permute-start | bytes 3145736 | tf_op jit(solution)/shard_map/ppermute | solution.py:432
  116.7 67.8 %collective-permute-start.22 = (bf16[176,2048]{1,0:T(8,128)(2,1)}, bf16[176,2048]{1,0:T(8,128)(2,1)}, u32[]{:S(2)}, u32[]{:S(2)}) collective-permute-start(bf16[176,2048]{1,0:T(8,128)(2,1)} %collective-permute-done.20), channel_id=1, source_target_pairs={{2,0},{3,1},{10,8},{11,9},{18,16},{19,17},{26,24},{27,25}} | collective-permute-start | bytes 2162696 | tf_op jit(solution)/shard_map/ppermute | solution.py:432
  118.0 66.5 %collective-permute-start.23 = (bf16[176,2048]{1,0:T(8,128)(2,1)}, bf16[176,2048]{1,0:T(8,128)(2,1)}, u32[]{:S(2)}, u32[]{:S(2)}) collective-permute-start(bf16[176,2048]{1,0:T(8,128)(2,1)} %collective-permute-done.19), channel_id=1, source_target_pairs={{4,6},{5,7},{12,14},{13,15},{20,22},{21,23},{28,30},{29,31}} | collective-permute-start | bytes 2162696 | tf_op jit(solution)/shard_map/ppermute | solution.py:432
  120.8 65.0 %collective-permute-start.21 = (bf16[176,2048]{1,0:T(8,128)(2,1)S(1)}, bf16[176,2048]{1,0:T(8,128)(2,1)}, u32[]{:S(2)}, u32[]{:S(2)}) collective-permute-start(bf16[176,2048]{1,0:T(8,128)(2,1)S(1)} %broadcast_select_fusion.8.refs_17_.refs_6_), channel_id=1, source_target_pairs={{0,1},{1,0},{2,3},{3,2},{4,5},{5,4},{6,7},{7,6},{8,9},{9,8},{10,11... | collective-permute-start | bytes 2162696 | tf_op jit(solution)/shard_map/ppermute | solution.py:432
  121.8 80.2 %collective-permute-start.5 = (bf16[256,2048]{1,0:T(8,128)(2,1)}, bf16[256,2048]{1,0:T(8,128)(2,1)}, u32[]{:S(2)}, u32[]{:S(2)}) collective-permute-start(bf16[256,2048]{1,0:T(8,128)(2,1)} %collective-permute-done.3.refs_10_), channel_id=1, source_target_pairs={{0,8},{8,0},{16,24},{24,16},{1,9},{9,1},{17,25},{25,17},{2,10},{10... | collective-permute-start | bytes 3145736 | tf_op jit(solution)/shard_map/ppermute | solution.py:432
  185.8 16.2 %collective-permute-start.24 = (bf16[176,2048]{1,0:T(8,128)(2,1)S(1)}, bf16[176,2048]{1,0:T(8,128)(2,1)}, u32[]{:S(2)}, u32[]{:S(2)}) collective-permute-start(bf16[176,2048]{1,0:T(8,128)(2,1)S(1)} %select_select_fusion.refs_19_.refs_8_), channel_id=1, source_target_pairs={{0,1},{1,0},{2,3},{3,2},{4,5},{5,4},{6,7},{7,6},{8,9},{9,8},{10,11... | collective-permute-start | bytes 2162696 | tf_op jit(solution)/shard_map/ppermute | solution.py:432
  214.2 519.9 %reduce-scatter.9.cloned.1.call-start = ((), (), s32[]{:S(2)}) async-start(), calls=%async_computation.9 | async-start | bytes 3604480 | tf_op jit(solution)/shard_map/reduce_scatter | solution.py:478
  277.0 24.8 %collective-permute-start.7 = (bf16[1024,512]{1,0:T(8,128)(2,1)S(1)}, bf16[1024,512]{1,0:T(8,128)(2,1)S(1)}, u32[]{:S(2)}, u32[]{:S(2)}) collective-permute-start(bf16[1024,512]{1,0:T(8,128)(2,1)S(1)} %get-tuple-element.194.refs_0_), channel_id=1, source_target_pairs={{0,16},{8,24},{16,0},{24,8},{1,17},{9,25},{17,1},{25,9},{2,18},{10... | collective-permute-start | bytes 3145736 | tf_op jit(solution)/shard_map/ppermute | solution.py:432
  320.7 24.9 %collective-permute-start.13 = (bf16[1024,512]{1,0:T(8,128)(2,1)}, bf16[1024,512]{1,0:T(8,128)(2,1)S(1)}, u32[]{:S(2)}, u32[]{:S(2)}) collective-permute-start(bf16[1024,512]{1,0:T(8,128)(2,1)} %get-tuple-element.203.refs_0_), channel_id=1, source_target_pairs={{0,16},{8,24},{16,0},{24,8},{1,17},{9,25},{17,1},{25,9},{2,18},{10... | collective-permute-start | bytes 3145736 | tf_op jit(solution)/shard_map/ppermute | solution.py:432
  321.5 24.1 %collective-permute-start.12 = (bf16[1024,512]{1,0:T(8,128)(2,1)}, bf16[1024,512]{1,0:T(8,128)(2,1)}, u32[]{:S(2)}, u32[]{:S(2)}) collective-permute-start(bf16[1024,512]{1,0:T(8,128)(2,1)} %get-tuple-element.203.refs_0_), channel_id=1, source_target_pairs={{0,8},{8,0},{16,24},{24,16},{1,9},{9,1},{17,25},{25,17},{2,10},{10... | collective-permute-start | bytes 3145736 | tf_op jit(solution)/shard_map/ppermute | solution.py:432
  416.7 29.0 %collective-permute-start.27 = (f32[4,1,256]{2,1,0:T(1,128)S(1)}, f32[4,1,256]{2,1,0:T(1,128)S(1)}, u32[]{:S(2)}, u32[]{:S(2)}) collective-permute-start(f32[4,1,256]{2,1,0:T(1,128)S(1)} %collective-permute-done.25.refs_12_), channel_id=1, source_target_pairs={{0,8},{8,0},{16,24},{24,16},{1,9},{9,1},{17,25},{25,17},{2,10},{10... | collective-permute-start | bytes 12296 | tf_op jit(solution)/shard_map/ppermute | solution.py:432
  445.9 64.3 %collective-permute-start.45 = (bf16[1024,1408]{1,0:T(8,128)(2,1)}, bf16[1024,1408]{1,0:T(8,128)(2,1)}, u32[]{:S(2)}, u32[]{:S(2)}) collective-permute-start(bf16[1024,1408]{1,0:T(8,128)(2,1)} %convolution_convert_fusion.6), channel_id=1, source_target_pairs={{0,1},{1,0},{2,3},{3,2},{4,5},{5,4},{6,7},{7,6},{8,9},{9,8},{10,11... | collective-permute-start | bytes 8650760 | tf_op jit(solution)/shard_map/ppermute | solution.py:723
  448.7 18.8 %collective-permute-start.29 = (bf16[1024,512]{1,0:T(8,128)(2,1)}, bf16[1024,512]{1,0:T(8,128)(2,1)S(1)}, u32[]{:S(2)}, u32[]{:S(2)}) collective-permute-start(bf16[1024,512]{1,0:T(8,128)(2,1)} %get-tuple-element.229), channel_id=1, source_target_pairs={{0,8},{8,0},{16,24},{24,16},{1,9},{9,1},{17,25},{25,17},{2,10},{10... | collective-permute-start | bytes 3145736 | tf_op jit(solution)/shard_map/ppermute | solution.py:432
  450.5 24.5 %collective-permute-start.30 = (bf16[1024,512]{1,0:T(8,128)(2,1)S(1)}, bf16[1024,512]{1,0:T(8,128)(2,1)S(1)}, u32[]{:S(2)}, u32[]{:S(2)}) collective-permute-start(bf16[1024,512]{1,0:T(8,128)(2,1)S(1)} %add_convert_fusion.9), channel_id=1, source_target_pairs={{0,16},{8,24},{16,0},{24,8},{1,17},{9,25},{17,1},{25,9},{2,18},{10... | collective-permute-start | bytes 3145736 | tf_op jit(solution)/shard_map/ppermute | solution.py:432
  485.1 7.8 collective-permute-start.31
  514.3 239.1 %reduce-scatter.11.cloned.1.call-start = ((), (), s32[]{:S(2)}) async-start(), calls=%async_computation.10 | async-start | bytes 3604480 | tf_op jit(solution)/shard_map/reduce_scatter | solution.py:478
  514.7 63.3 %collective-permute-start.50 = (bf16[1024,1408]{1,0:T(8,128)(2,1)}, bf16[1024,1408]{1,0:T(8,128)(2,1)S(1)}, u32[]{:S(2)}, u32[]{:S(2)}) collective-permute-start(bf16[1024,1408]{1,0:T(8,128)(2,1)} %convolution_convert_fusion.5), channel_id=1, source_target_pairs={{0,1},{1,0},{2,3},{3,2},{4,5},{5,4},{6,7},{7,6},{8,9},{9,8},{10,11... | collective-permute-start | bytes 8650760 | tf_op jit(solution)/shard_map/ppermute | solution.py:723
  515.1 8.9 collective-permute-start.32
  516.4 25.1 %collective-permute-start.34 = (bf16[1024,512]{1,0:T(8,128)(2,1)}, bf16[1024,512]{1,0:T(8,128)(2,1)S(1)}, u32[]{:S(2)}, u32[]{:S(2)}) collective-permute-start(bf16[1024,512]{1,0:T(8,128)(2,1)} %add_convert_fusion.8), channel_id=1, source_target_pairs={{0,16},{8,24},{16,0},{24,8},{1,17},{9,25},{17,1},{25,9},{2,18},{10... | collective-permute-start | bytes 3145736 | tf_op jit(solution)/shard_map/ppermute | solution.py:432
  580.4 215.8 %reduce-scatter.13.cloned.1.call-start = ((), (), s32[]{:S(2)}) async-start(), calls=%async_computation.11 | async-start | bytes 3604480 | tf_op jit(solution)/shard_map/reduce_scatter | solution.py:478
  580.7 5.6 collective-permute-start.33
  586.0 64.1 %collective-permute-start.54 = (bf16[704,2048]{1,0:T(8,128)(2,1)S(1)}, bf16[704,2048]{1,0:T(8,128)(2,1)S(1)}, u32[]{:S(2)}, u32[]{:S(2)}) collective-permute-start(bf16[704,2048]{1,0:T(8,128)(2,1)S(1)} %bitcast.95), channel_id=1, source_target_pairs={{0,1},{1,0},{2,3},{3,2},{4,5},{5,4},{6,7},{7,6},{8,9},{9,8},{10,11... | collective-permute-start | bytes 8650760 | tf_op jit(solution)/shard_map/ppermute | solution.py:723
  588.5 24.8 %collective-permute-start.35 = (bf16[256,2048]{1,0:T(8,128)(2,1)S(1)}, bf16[256,2048]{1,0:T(8,128)(2,1)S(1)}, u32[]{:S(2)}, u32[]{:S(2)}) collective-permute-start(bf16[256,2048]{1,0:T(8,128)(2,1)S(1)} %add_convert_fusion.7), channel_id=1, source_target_pairs={{0,16},{8,24},{16,0},{24,8},{1,17},{9,25},{17,1},{25,9},{2,18},{10... | collective-permute-start | bytes 3145736 | tf_op jit(solution)/shard_map/ppermute | solution.py:432
  653.0 176.0 %reduce-scatter.15.cloned.1.call-start = ((), (), s32[]{:S(2)}) async-start(), calls=%async_computation.12 | async-start | bytes 1310720 | tf_op jit(solution)/shard_map/reduce_scatter | solution.py:478
  653.0 6.3 collective-permute-start.37
  658.1 25.4 %collective-permute-start.36 = (bf16[1024,512]{1,0:T(8,128)(2,1)}, bf16[1024,512]{1,0:T(8,128)(2,1)S(1)}, u32[]{:S(2)}, u32[]{:S(2)}) collective-permute-start(bf16[1024,512]{1,0:T(8,128)(2,1)} %convolution_convert_fusion.9), channel_id=1, source_target_pairs={{0,1},{1,0},{2,3},{3,2},{4,5},{5,4},{6,7},{7,6},{8,9},{9,8},{10,11... | collective-permute-start | bytes 3145736 | tf_op jit(solution)/shard_map/ppermute | solution.py:723
  659.3 20.0 %collective-permute-start.38 = (bf16[256,512]{1,0:T(8,128)(2,1)S(1)}, bf16[256,512]{1,0:T(8,128)(2,1)S(1)}, u32[]{:S(2)}, u32[]{:S(2)}) collective-permute-start(bf16[256,512]{1,0:T(8,128)(2,1)S(1)} %get-tuple-element.278), channel_id=1, source_target_pairs={{0,8},{8,0},{16,24},{24,16},{1,9},{9,1},{17,25},{25,17},{2,10},{10... | collective-permute-start | bytes 786440 | tf_op jit(solution)/shard_map/ppermute | solution.py:432
  679.3 13.1 %collective-permute-start.39 = (bf16[256,2048]{1,0:T(8,128)(2,1)}, bf16[256,2048]{1,0:T(8,128)(2,1)}, u32[]{:S(2)}, u32[]{:S(2)}) collective-permute-start(bf16[256,2048]{1,0:T(8,128)(2,1)} %get-tuple-element.279), channel_id=1, source_target_pairs={{0,8},{8,0},{16,24},{24,16},{1,9},{9,1},{17,25},{25,17},{2,10},{10... | collective-permute-start | bytes 3145736 | tf_op jit(solution)/shard_map/ppermute | solution.py:432
  679.8 48.0 %collective-permute-start.43 = (bf16[1024,1024]{1,0:T(8,128)(2,1)}, bf16[1024,1024]{1,0:T(8,128)(2,1)S(1)}, u32[]{:S(2)}, u32[]{:S(2)}) collective-permute-start(bf16[1024,1024]{1,0:T(8,128)(2,1)} %convolution_convert_fusion.7), channel_id=1, source_target_pairs={{0,1},{1,0},{2,3},{3,2},{4,5},{5,4},{6,7},{7,6},{8,9},{9,8},{10,11... | collective-permute-start | bytes 6291464 | tf_op jit(solution)/shard_map/ppermute | solution.py:723
  682.3 7.9 collective-permute-start.40
  684.9 156.0 %reduce-scatter.17.cloned.1.call-start = ((), (), s32[]{:S(2)}) async-start(), calls=%async_computation.13 | async-start | bytes 2621440 | tf_op jit(solution)/shard_map/reduce_scatter | solution.py:478
  690.2 9.6 %collective-permute-start.41 = (bf16[256,512]{1,0:T(8,128)(2,1)}, bf16[256,512]{1,0:T(8,128)(2,1)}, u32[]{:S(2)}, u32[]{:S(2)}) collective-permute-start(bf16[256,512]{1,0:T(8,128)(2,1)} %get-tuple-element.281), channel_id=1, source_target_pairs={{0,24},{8,16},{16,8},{24,0},{1,25},{9,17},{17,9},{25,1},{2,26},{10... | collective-permute-start | bytes 786440 | tf_op jit(solution)/shard_map/ppermute | solution.py:432
  699.8 24.5 %collective-permute-start.42 = (bf16[256,2048]{1,0:T(8,128)(2,1)S(1)}, bf16[256,2048]{1,0:T(8,128)(2,1)S(1)}, u32[]{:S(2)}, u32[]{:S(2)}) collective-permute-start(bf16[256,2048]{1,0:T(8,128)(2,1)S(1)} %add_convert_fusion.5), channel_id=1, source_target_pairs={{0,16},{8,24},{16,0},{24,8},{1,17},{9,25},{17,1},{25,9},{2,18},{10... | collective-permute-start | bytes 3145736 | tf_op jit(solution)/shard_map/ppermute | solution.py:432
  730.2 140.8 %reduce-scatter.7.cloned.1.call-start = ((), (), s32[]{:S(2)}) async-start(), calls=%async_computation.8 | async-start | bytes 2949120 | tf_op jit(solution)/shard_map/reduce_scatter | solution.py:478
  731.5 53.1 %collective-permute-start.44 = (bf16[1024,1152]{1,0:T(8,128)(2,1)}, bf16[1024,1152]{1,0:T(8,128)(2,1)}, u32[]{:S(2)}, u32[]{:S(2)}) collective-permute-start(bf16[1024,1152]{1,0:T(8,128)(2,1)} %convolution_convert_fusion.1), channel_id=1, source_target_pairs={{0,1},{1,0},{2,3},{3,2},{4,5},{5,4},{6,7},{7,6},{8,9},{9,8},{10,11... | collective-permute-start | bytes 7077896 | tf_op jit(solution)/shard_map/ppermute | solution.py:723
  734.5 17.9 %collective-permute-start.48 = (bf16[256,1408]{1,0:T(8,128)(2,1)}, bf16[256,1408]{1,0:T(8,128)(2,1)}, u32[]{:S(2)}, u32[]{:S(2)}) collective-permute-start(bf16[256,1408]{1,0:T(8,128)(2,1)} %reduce-scatter.9.cloned.1.call-done.refs_0_), channel_id=1, source_target_pairs={{0,16},{8,24},{16,0},{24,8},{1,17},{9,25},{17,1},{25,9},{2,18},{10... | collective-permute-start | bytes 2162696 | tf_op jit(solution)/shard_map/ppermute | solution.py:432
  753.4 18.1 %collective-permute-start.52 = (bf16[256,1408]{1,0:T(8,128)(2,1)}, bf16[256,1408]{1,0:T(8,128)(2,1)}, u32[]{:S(2)}, u32[]{:S(2)}) collective-permute-start(bf16[256,1408]{1,0:T(8,128)(2,1)} %reduce-scatter.11.cloned.1.call-done.refs_0_), channel_id=1, source_target_pairs={{0,16},{8,24},{16,0},{24,8},{1,17},{9,25},{17,1},{25,9},{2,18},{10... | collective-permute-start | bytes 2162696 | tf_op jit(solution)/shard_map/ppermute | solution.py:432
  755.5 15.9 %collective-permute-start.51 = (bf16[256,1408]{1,0:T(8,128)(2,1)}, bf16[256,1408]{1,0:T(8,128)(2,1)}, u32[]{:S(2)}, u32[]{:S(2)}) collective-permute-start(bf16[256,1408]{1,0:T(8,128)(2,1)} %reduce-scatter.11.cloned.1.call-done.refs_0_), channel_id=1, source_target_pairs={{0,8},{8,0},{16,24},{24,16},{1,9},{9,1},{17,25},{25,17},{2,10},{10... | collective-permute-start | bytes 2162696 | tf_op jit(solution)/shard_map/ppermute | solution.py:432
  771.5 26.0 %collective-permute-start.53 = (bf16[256,1408]{1,0:T(8,128)(2,1)}, bf16[256,1408]{1,0:T(8,128)(2,1)}, u32[]{:S(2)}, u32[]{:S(2)}) collective-permute-start(bf16[256,1408]{1,0:T(8,128)(2,1)} %collective-permute-done.52.refs_2_), channel_id=1, source_target_pairs={{0,8},{8,0},{16,24},{24,16},{1,9},{9,1},{17,25},{25,17},{2,10},{10... | collective-permute-start | bytes 2162696 | tf_op jit(solution)/shard_map/ppermute | solution.py:432
  796.2 17.2 %collective-permute-start.55 = (bf16[176,2048]{1,0:T(8,128)(2,1)}, bf16[176,2048]{1,0:T(8,128)(2,1)}, u32[]{:S(2)}, u32[]{:S(2)}) collective-permute-start(bf16[176,2048]{1,0:T(8,128)(2,1)} %reduce-scatter.13.cloned.1.call-done), channel_id=1, source_target_pairs={{0,16},{8,24},{16,0},{24,8},{1,17},{9,25},{17,1},{25,9},{2,18},{10... | collective-permute-start | bytes 2162696 | tf_op jit(solution)/shard_map/ppermute | solution.py:432
  797.4 16.0 %collective-permute-start.56 = (bf16[176,2048]{1,0:T(8,128)(2,1)}, bf16[176,2048]{1,0:T(8,128)(2,1)}, u32[]{:S(2)}, u32[]{:S(2)}) collective-permute-start(bf16[176,2048]{1,0:T(8,128)(2,1)} %reduce-scatter.13.cloned.1.call-done), channel_id=1, source_target_pairs={{0,8},{8,0},{16,24},{24,16},{1,9},{9,1},{17,25},{25,17},{2,10},{10... | collective-permute-start | bytes 2162696 | tf_op jit(solution)/shard_map/ppermute | solution.py:432
  813.4 15.9 %collective-permute-start.57 = (bf16[176,2048]{1,0:T(8,128)(2,1)}, bf16[176,2048]{1,0:T(8,128)(2,1)}, u32[]{:S(2)}, u32[]{:S(2)}) collective-permute-start(bf16[176,2048]{1,0:T(8,128)(2,1)} %collective-permute-done.55), channel_id=1, source_target_pairs={{0,8},{8,0},{16,24},{24,16},{1,9},{9,1},{17,25},{25,17},{2,10},{10... | collective-permute-start | bytes 2162696 | tf_op jit(solution)/shard_map/ppermute | solution.py:432
  820.8 20.8 %collective-permute-start.62 = (f32[232,128]{1,0:T(8,128)}, f32[232,128]{1,0:T(8,128)}, u32[]{:S(2)}, u32[]{:S(2)}) collective-permute-start(f32[232,128]{1,0:T(8,128)} %fusion.23), channel_id=1, source_target_pairs={{0,16},{8,24},{16,0},{24,8},{1,17},{9,25},{17,1},{25,9},{2,18},{10... | collective-permute-start | bytes 356360 | tf_op jit(solution)/shard_map/ppermute | solution.py:896
  829.0 7.7 collective-permute-start.59
  829.3 7.4 collective-permute-start.58
  840.9 13.9 %collective-permute-start.67 = (bf16[256,1024]{1,0:T(8,128)(2,1)}, bf16[256,1024]{1,0:T(8,128)(2,1)}, u32[]{:S(2)}, u32[]{:S(2)}) collective-permute-start(bf16[256,1024]{1,0:T(8,128)(2,1)} %reduce-scatter.17.cloned.1.call-done.refs_0_), channel_id=1, source_target_pairs={{0,16},{8,24},{16,0},{24,8},{1,17},{9,25},{17,1},{25,9},{2,18},{10... | collective-permute-start | bytes 1572872 | tf_op jit(solution)/shard_map/ppermute | solution.py:432
  841.3 13.5 %collective-permute-start.66 = (bf16[256,1024]{1,0:T(8,128)(2,1)}, bf16[256,1024]{1,0:T(8,128)(2,1)}, u32[]{:S(2)}, u32[]{:S(2)}) collective-permute-start(bf16[256,1024]{1,0:T(8,128)(2,1)} %reduce-scatter.17.cloned.1.call-done.refs_0_), channel_id=1, source_target_pairs={{0,8},{8,0},{16,24},{24,16},{1,9},{9,1},{17,25},{25,17},{2,10},{10... | collective-permute-start | bytes 1572872 | tf_op jit(solution)/shard_map/ppermute | solution.py:432
  842.8 5.0 collective-permute-start.63
  852.1 8.3 collective-permute-start.65
  854.8 11.1 %collective-permute-start.68 = (bf16[256,1024]{1,0:T(8,128)(2,1)}, bf16[256,1024]{1,0:T(8,128)(2,1)}, u32[]{:S(2)}, u32[]{:S(2)}) collective-permute-start(bf16[256,1024]{1,0:T(8,128)(2,1)} %collective-permute-done.67.refs_2_), channel_id=1, source_target_pairs={{0,8},{8,0},{16,24},{24,16},{1,9},{9,1},{17,25},{25,17},{2,10},{10... | collective-permute-start | bytes 1572872 | tf_op jit(solution)/shard_map/ppermute | solution.py:432
  871.9 15.2 %collective-permute-start.70 = (bf16[256,1152]{1,0:T(8,128)(2,1)}, bf16[256,1152]{1,0:T(8,128)(2,1)}, u32[]{:S(2)}, u32[]{:S(2)}) collective-permute-start(bf16[256,1152]{1,0:T(8,128)(2,1)} %reduce-scatter.7.cloned.1.call-done.refs_0_), channel_id=1, source_target_pairs={{0,16},{8,24},{16,0},{24,8},{1,17},{9,25},{17,1},{25,9},{2,18},{10... | collective-permute-start | bytes 1769480 | tf_op jit(solution)/shard_map/ppermute | solution.py:432
  887.1 4.8 collective-permute-start.71
  (73 other events, 1202.1 us)
Sparse Core Ops, SparseCore 0:
  20.3 193.8 all-gather.2
  216.9 160.7 all-gather.4
  514.4 54.5 reduce-scatter.8
  580.6 55.4 reduce-scatter.10
  653.1 54.3 reduce-scatter.12
  710.2 26.9 reduce-scatter.14
  740.2 42.4 reduce-scatter.16
  788.4 46.2 reduce-scatter.6

commit v4 on v3

--- a/solution.py
+++ b/solution.py
@@ -832,6 +832,7 @@
             first_body, "first", 19, (ranks,), info, [(after(d_pre, *d_in), by_slot(in_cols))], [full_in],
             [((rows, model), BF, slot)] * ranks,
         )
+        gate_slots = gather_group(share_gate)
         first_terms = scatter_group(grad_slots)
         grad_one = sum(t.astype(F32) for t in first_terms)
         share_o, sum_o = end_out(grad_slots[0])
@@ -910,7 +911,7 @@
         at += head_gain.size
         sum_log, sum_bias = total[at : at + heads], total[at + heads : at + 2 * heads]
 
-        gate_slots, up_slots = gather_group(share_gate), gather_group(share_up)
+        up_slots = gather_group(share_up)
         out_gate = unhide(gate_slots)
         d_slots = gather_group(after(share_d, out_gate))
         out_up = unhide(up_slots)

time: 917 us -> 949 us (1.035)
  waiting for transfers between devices: 418 us -> 451 us
    ppermute x6, waiting for transfers between devices: 41.3 us -> 75 us  [exchanged(): lax.ppermute(after(sent, *begin), 'fsdp', [(f, f ^ 1) for f in range(shar...]
    unnamed x128 -> x138, local copies, waits for them, and re-layouts: 24.3 us -> 25.7 us
  transfers between devices with their start and end apart: 80 -> 80, of which waited for: 43 -> 41; matrix products, arithmetic and copies ran while one was open for 15% -> 14% of each run, Pallas kernels for 22% -> 22%
where the time goes in v4:
time: 949 us; the launch traced here: 941 us
  waiting for transfers between devices  451 us (48%)
  Pallas kernels  244 us (26%)
  starting transfers between devices  71 us (7%)
  matrix products  59.8 us (6%)
  other arithmetic  51.8 us (5%)
  local copies, waits for them, and re-layouts  49.1 us (5%)
  between operations  15.4 us (2%)
    ppermute x61, waiting for transfers between devices, send(): sent = lax.ppermute(after(value, *last.get(lane, ())), axis, pairs)  325 us
    pallas_call x13, Pallas kernels, kernel_call(): pl.pallas_call(kernel, grid_spec=pltpu.PrefetchScalarGridSpec(num_scalar_...  166 us
    ppermute x6, waiting for transfers between devices, exchanged(): lax.ppermute(after(sent, *begin), 'fsdp', [(f, f ^ 1) for f in range(shar...  75 us
    ppermute x61, starting transfers between devices, send(): sent = lax.ppermute(after(value, *last.get(lane, ())), axis, pairs)  65.2 us
    dot_general x11, matrix products, dot(): return lax.dot_general(left, right, dims, preferred_element_type=F32)  59.8 us
    pallas_call x4, Pallas kernels, mixer_backward(): pl.pallas_call(partial(backward_kernel, cfg, at), grid_spec=pltpu.Prefetc...  49.2 us
    all_gather x2, waiting for transfers between devices, gather_whole(): return lax.all_gather(piece, 'fsdp', axis=0, tiled=True)  42.6 us
    pallas_call x4, Pallas kernels, mixer_forward(): pl.pallas_call(partial(forward_kernel, cfg, at), grid_spec=pltpu.Prefetch...  28.7 us
  transfers between devices with their start and end apart: 80, of which 41 were waited for; matrix products, arithmetic and copies ran while one was open for 14% of the time, Pallas kernels for 22%

profile of v4, /device:TPU:1, one launch (start us, length us, event | category | flops | bytes accessed | tf_op | source)
XLA Modules:
  0.0 941.3 jit_solution(7708555390520546240)
XLA Ops:
  27.1 3.2 collective-permute-start.16
  32.9 16.9 %collective-permute-done.refs_0_ = bf16[272,2048]{1,0:T(8,128)(2,1)} collective-permute-done((bf16[272,2048]{1,0:T(8,128)(2,1)}, bf16[272,2048]{1,0:T(8,128)(2,1)}, u32[]{:S(2)}, u32[]{:S(2)}) %collective-permute-start) | collective-permute-done | bytes 1114144 | tf_op jit(solution)/shard_map/ppermute | solution.py:432
  51.6 8.1 collective-permute-done.16
  59.7 20.8 %collective-permute-done.17 = bf16[176,2048]{1,0:T(8,128)(2,1)} collective-permute-done((bf16[176,2048]{1,0:T(8,128)(2,1)}, bf16[176,2048]{1,0:T(8,128)(2,1)}, u32[]{:S(2)}, u32[]{:S(2)}) %collective-permute-start.17) | collective-permute-done | bytes 720928 | tf_op jit(solution)/shard_map/ppermute | solution.py:432
  88.0 10.0 %collective-permute-done.18.refs_16_.refs_5_ = bf16[176,2048]{1,0:T(8,128)(2,1)S(1)} collective-permute-done((bf16[176,2048]{1,0:T(8,128)(2,1)S(1)}, bf16[176,2048]{1,0:T(8,128)(2,1)S(1)}, u32[]{:S(2)}, u32[]{:S(2)}) %collective-permute-start.18) | collective-permute-done | bytes 720928 | tf_op jit(solution)/shard_map/ppermute | solution.py:432
  98.0 18.4 %collective-permute-done.20 = bf16[176,2048]{1,0:T(8,128)(2,1)} collective-permute-done((bf16[176,2048]{1,0:T(8,128)(2,1)}, bf16[176,2048]{1,0:T(8,128)(2,1)}, u32[]{:S(2)}, u32[]{:S(2)}) %collective-permute-start.20) | collective-permute-done | bytes 720928 | tf_op jit(solution)/shard_map/ppermute | solution.py:432
  124.0 60.2 %collective-permute-done.22 = bf16[176,2048]{1,0:T(8,128)(2,1)} collective-permute-done((bf16[176,2048]{1,0:T(8,128)(2,1)}, bf16[176,2048]{1,0:T(8,128)(2,1)}, u32[]{:S(2)}, u32[]{:S(2)}) %collective-permute-start.22) | collective-permute-done | bytes 720928 | tf_op jit(solution)/shard_map/ppermute | solution.py:432
  186.6 4.5 copy.76
  191.2 4.5 copy.75
  200.7 13.5 %all-gather.3.cloned.1.call-done.refs_2_.refs_6_.refs_14_.refs_1_ = bf16[2048,2688]{1,0:T(8,128)(2,1)} async-done(((bf16[256,2688]{1,0:T(8,128)(2,1)}), bf16[2048,2688]{1,0:T(8,128)(2,1)}) %all-gather.3.cloned.1.call-update) | async-done | bytes 11010064 | tf_op jit(solution)/shard_map/all_gather | solution.py:464
  217.5 14.7 %enter.2 = (f32[1024,2176]{1,0:T(8,128)}, bf16[1024,1024]{1,0:T(8,128)(2,1)}, bf16[1024,1024]{1,0:T(8,128)(2,1)}, bf16[1024,512]{1,0:T(8,128)(2,1)}, f32[16,2048]{1,0:T(8,128)}) custom-call(s32[4]{0:T(128)} %pad_add_fusion.2.info_ref, bf16[272,2048]{1,0:T(8,128)(2,1)} %fusion.20.refs_0_, bf16[272,2048]{1,0:T(8,128)(2,1)} %collective-permute-done.1.refs_1_, ...), custom_call_target="tpu_custom_call" | custom-call | flops 11000000 | bytes 1024 | tf_op jit(solution)/shard_map/enter/pallas_call | solution.py:396
  233.4 7.2 mixer_forward.4
  240.6 7.2 mixer_forward.5
  247.8 14.1 %enter.3 = (f32[1024,2176]{1,0:T(8,128)}, bf16[1024,1024]{1,0:T(8,128)(2,1)}, bf16[1024,1024]{1,0:T(8,128)(2,1)}, bf16[1024,512]{1,0:T(8,128)(2,1)}, f32[16,2048]{1,0:T(8,128)}) custom-call(s32[4]{0:T(128)} %pad_add_fusion.info_ref, ...), custom_call_target="tpu_custom_call", output_to_operand_aliasing={{0}: (4, {}), {1}: (5, {}), {2}: (6, {}), {3}: (7, {})} | custom-call | flops 11000000 | bytes 1024 | tf_op jit(solution)/shard_map/enter/pallas_call | solution.py:396
  261.9 7.2 mixer_forward.6
  269.1 7.2 mixer_forward.7
  279.2 22.6 %collective-permute-done.7.refs_2_ = bf16[1024,512]{1,0:T(8,128)(2,1)S(1)} collective-permute-done((bf16[1024,512]{1,0:T(8,128)(2,1)S(1)}, bf16[1024,512]{1,0:T(8,128)(2,1)S(1)}, u32[]{:S(2)}, u32[]{:S(2)}) %collective-permute-start.7) | collective-permute-done | bytes 1048608 | tf_op jit(solution)/shard_map/ppermute | solution.py:432
  305.7 10.4 %leave.1 = (bf16[1024,1024]{1,0:T(8,128)(2,1)}, bf16[1024,1024]{1,0:T(8,128)(2,1)}, f32[1024,512]{1,0:T(8,128)}, f32[1024,512]{1,0:T(8,128)}, bf16[1024,512]{1,0:T(8,128)(2,1)}, /*index=5*/f32[4,1,256]{2,1,0:T(1,128)}) custom-call(s32[3]{0:T(128)} %pad_add_fusion.3.info_ref, bf16[1024,512]{1,0:T(8,128)(2,1)} %copy-done.7, bf16[1024,512]{1,0:T(8,128)(2,1)} %copy-done.30, ...), custom_call_target="tpu_custom_call" | custom-call | flops 9000000 | bytes 1024 | tf_op jit(solution)/shard_map/leave/pallas_call | solution.py:396
  321.6 23.8 %collective-permute-done.13.refs_2_ = bf16[1024,512]{1,0:T(8,128)(2,1)S(1)} collective-permute-done((bf16[1024,512]{1,0:T(8,128)(2,1)}, bf16[1024,512]{1,0:T(8,128)(2,1)S(1)}, u32[]{:S(2)}, u32[]{:S(2)}) %collective-permute-start.13) | collective-permute-done | bytes 1048608 | tf_op jit(solution)/shard_map/ppermute | solution.py:432
  348.7 29.1 %all-gather.5.cloned.1.call-done.refs_12_.refs_1_ = bf16[2048,2816]{1,0:T(8,128)(2,1)} async-done(((bf16[256,2816]{1,0:T(8,128)(2,1)}), bf16[2048,2816]{1,0:T(8,128)(2,1)}) %all-gather.5.cloned.1.call-update) | async-done | bytes 11534352 | tf_op jit(solution)/shard_map/all_gather | solution.py:464
  377.7 35.4 %hidden.1 = (bf16[1024,1024]{1,0:T(8,128)(2,1)}, bf16[1024,1024]{1,0:T(8,128)(2,1)}, bf16[1024,1408]{1,0:T(8,128)(2,1)}, bf16[1024,2816]{1,0:T(8,128)(2,1)}, f32...) custom-call(s32[11]{0:T(128)} %stack.48.info_ref, ...), custom_call_target="tpu_custom_call" | custom-call | flops 33000000 | bytes 1024 | tf_op jit(solution)/shard_map/hidden/pallas_call | solution.py:396
  418.1 7.5 convolution_convert_fusion.6
  425.6 20.1 %back.1 = (bf16[1024,512]{1,0:T(8,128)(2,1)}, bf16[1024,512]{1,0:T(8,128)(2,1)}, bf16[1024,512]{1,0:T(8,128)(2,1)}, bf16[1024,512]{1,0:T(8,128)(2,1)}) custom-call(s32[3]{0:T(128)} %pad_add_fusion.3.info_ref, bf16[1024,2816]{1,0:T(8,128)(2,1)} %get-tuple-element.220.refs_0_, bf16[2048,2816]{1,0:T(8,128)(2,1)} %all-gather.5.cloned.1.call-done.refs_12_.refs_1_), custom_call_target="tpu_custom_call" | custom-call | flops 19000000 | bytes 1024 | tf_op jit(solution)/shard_map/back/pallas_call | solution.py:396
  451.8 10.8 %convolution_convert_fusion = bf16[1408,2048]{1,0:T(8,128)(2,1)} fusion(bf16[1024,1408]{1,0:T(8,128)(2,1)S(1)} %copy-done.20, bf16[1024,2048]{1,0:T(8,128)(2,1)} %get-tuple-element.233), kind=kOutput, calls=%fused_computation | convolution fusion | flops 5908463616 | bytes 12845056 | tf_op jit(solution)/shard_map/dot_general | solution.py:332
  462.6 4.9 convolution_convert_fusion.5
  467.5 7.6 collective-permute-done.30.refs_2_
  476.0 9.1 turn.1
  486.9 6.0 convolution_convert_fusion.4
  495.4 14.7 %down.1 = (bf16[256,2048]{1,0:T(8,128)(2,1)}, bf16[256,2048]{1,0:T(8,128)(2,1)}, bf16[256,2048]{1,0:T(8,128)(2,1)}, bf16[256,2048]{1,0:T(8,128)(2,1)}) custom-call(s32[10]{0:T(128)} %stack.47.info_ref, bf16[1024,1408]{1,0:T(8,128)(2,1)} %get-tuple-element.239.refs_0_, f32[1024,512]{1,0:T(8,128)} %get-tuple-element.240.refs_1_, ...), custom_call_target="tpu_custom_call" | custom-call | flops 14000000 | bytes 1024 | tf_op jit(solution)/shard_map/down/pallas_call | solution.py:396
  510.1 4.1 add_convert_fusion.2
  517.5 6.4 convolution_convert_fusion.3
  524.0 17.5 %collective-permute-done.34.far_ref = bf16[1024,512]{1,0:T(8,128)(2,1)S(1)} collective-permute-done((bf16[1024,512]{1,0:T(8,128)(2,1)}, bf16[1024,512]{1,0:T(8,128)(2,1)S(1)}, u32[]{:S(2)}, u32[]{:S(2)}) %collective-permute-start.34) | collective-permute-done | bytes 1048608 | tf_op jit(solution)/shard_map/ppermute | solution.py:432
  541.5 12.6 %mixer_backward.4 = (bf16[1024,2176]{1,0:T(8,128)(2,1)}, f32[4,1536]{1,0:T(4,128)S(1)}, f32[1,128]{1,0:T(1,128)S(1)}, f32[8,128]{1,0:T(8,128)S(1)}) custom-call(s32[1]{0:T(128)} %bitcast.rank_ref, s32[4,2]{1,0:T(4,128)S(1)} %maximum_convert_fusion.1.len_ref, f32[16]{0:T(128)S(1)} %copy-done.8, f32[16]{0:T(128)S(1)} %copy-done.9, ...), custom_call_target="tpu_custom_call" | custom-call | flops 12000000 | bytes 1024 | tf_op jit(solution)/shard_map/mixer_backward/pallas_call | solution.py:311
  554.1 12.0 %mixer_backward.5 = (bf16[1024,2176]{1,0:T(8,128)(2,1)}, f32[4,1536]{1,0:T(4,128)S(1)}, f32[1,128]{1,0:T(1,128)S(1)}, f32[8,128]{1,0:T(8,128)S(1)}) custom-call(s32[1]{0:T(128)} %bitcast.rank_ref, s32[4,2]{1,0:T(4,128)S(1)} %maximum_convert_fusion.1.len_ref, f32[16]{0:T(128)S(1)} %copy-done.8, f32[16]{0:T(128)S(1)} %copy-done.9, ...), custom_call_target="tpu_custom_call", output_to_operand_aliasing={{0}: (11, {})} | custom-call | flops 12000000 | bytes 1024 | tf_op jit(solution)/shard_map/mixer_backward/pallas_call | solution.py:311
  566.1 11.8 %collective-permute-done.49 = bf16[1024,1408]{1,0:T(8,128)(2,1)S(1)} collective-permute-done((bf16[1024,1408]{1,0:T(8,128)(2,1)}, bf16[1024,1408]{1,0:T(8,128)(2,1)S(1)}, u32[]{:S(2)}, u32[]{:S(2)}) %collective-permute-start.49) | collective-permute-done | bytes 2883616 | tf_op jit(solution)/shard_map/ppermute | solution.py:723
  582.6 3.3 constant_dynamic-slice_fusion.2
  589.8 12.0 %mixer_backward.6 = (bf16[1024,2176]{1,0:T(8,128)(2,1)}, f32[4,1536]{1,0:T(4,128)S(1)}, f32[1,128]{1,0:T(1,128)S(1)}, f32[8,128]{1,0:T(8,128)S(1)}) custom-call(s32[1]{0:T(128)} %bitcast.rank_ref, s32[4,2]{1,0:T(4,128)S(1)} %maximum_convert_fusion.1.len_ref, f32[16]{0:T(128)S(1)} %copy-done.8, f32[16]{0:T(128)S(1)} %copy-done.9, ...), custom_call_target="tpu_custom_call", output_to_operand_aliasing={{0}: (11, {})} | custom-call | flops 12000000 | bytes 1024 | tf_op jit(solution)/shard_map/mixer_backward/pallas_call | solution.py:311
  601.8 11.4 %collective-permute-done.35 = bf16[256,2048]{1,0:T(8,128)(2,1)S(1)} collective-permute-done((bf16[256,2048]{1,0:T(8,128)(2,1)S(1)}, bf16[256,2048]{1,0:T(8,128)(2,1)S(1)}, u32[]{:S(2)}, u32[]{:S(2)}) %collective-permute-start.35) | collective-permute-done | bytes 1048608 | tf_op jit(solution)/shard_map/ppermute | solution.py:432
  614.2 12.6 %mixer_backward.7 = (bf16[1024,2176]{1,0:T(8,128)(2,1)}, f32[4,1536]{1,0:T(4,128)S(1)}, f32[1,128]{1,0:T(1,128)S(1)}, f32[8,128]{1,0:T(8,128)S(1)}) custom-call(s32[1]{0:T(128)} %bitcast.rank_ref, s32[4,2]{1,0:T(4,128)S(1)} %maximum_convert_fusion.1.len_ref, f32[16]{0:T(128)S(1)} %copy-done.8, f32[16]{0:T(128)S(1)} %copy-done.9, ...), custom_call_target="tpu_custom_call", output_to_operand_aliasing={{0}: (11, {})} | custom-call | flops 12000000 | bytes 1024 | tf_op jit(solution)/shard_map/mixer_backward/pallas_call | solution.py:311
  626.8 5.5 convolution_convert_fusion.7
  632.3 4.4 convolution_convert_fusion.1
  636.7 13.3 %collective-permute-done.54 = bf16[704,2048]{1,0:T(8,128)(2,1)S(1)} collective-permute-done((bf16[704,2048]{1,0:T(8,128)(2,1)S(1)}, bf16[704,2048]{1,0:T(8,128)(2,1)S(1)}, u32[]{:S(2)}, u32[]{:S(2)}) %collective-permute-start.54) | collective-permute-done | bytes 2883616 | tf_op jit(solution)/shard_map/ppermute | solution.py:723
  655.4 5.9 collective-permute-done.38
  664.0 7.2 collective-permute-done.39
  672.9 16.9 %collective-permute-done.40.refs_2_ = bf16[256,1408]{1,0:T(8,128)(2,1)S(1)} collective-permute-done((bf16[256,1408]{1,0:T(8,128)(2,1)}, bf16[256,1408]{1,0:T(8,128)(2,1)S(1)}, u32[]{:S(2)}, u32[]{:S(2)}) %collective-permute-start.40) | collective-permute-done | bytes 720928 | tf_op jit(solution)/shard_map/ppermute | solution.py:432
  690.7 3.8 convolution_convert_fusion.9
  695.0 18.8 %first.1 = (bf16[256,2048]{1,0:T(8,128)(2,1)}, bf16[256,2048]{1,0:T(8,128)(2,1)}, bf16[256,2048]{1,0:T(8,128)(2,1)}, bf16[256,2048]{1,0:T(8,128)(2,1)}) custom-call(s32[3]{0:T(128)} %pad_add_fusion.3.info_ref, bf16[1024,2176]{1,0:T(8,128)(2,1)} %get-tuple-element.270.refs_0_, bf16[2048,2688]{1,0:T(8,128)(2,1)} %all-gather.3.cloned.1.call-done.refs_2_.refs_6_.refs_14_.refs_1_), custom_call_target="tpu_custom_call" | custom-call | flops 19000000 | bytes 1024 | tf_op jit(solution)/shard_map/first/pallas_call | solution.py:396
  722.6 4.0 convolution_convert_fusion.8
  726.7 18.9 %collective-permute-done.46 = bf16[256,2048]{1,0:T(8,128)(2,1)S(1)} collective-permute-done((bf16[256,2048]{1,0:T(8,128)(2,1)S(1)}, bf16[256,2048]{1,0:T(8,128)(2,1)S(1)}, u32[]{:S(2)}, u32[]{:S(2)}) %collective-permute-start.46) | collective-permute-done | bytes 1048608 | tf_op jit(solution)/shard_map/ppermute | solution.py:432
  745.6 18.7 %collective-permute-done.47 = bf16[1024,1024]{1,0:T(8,128)(2,1)S(1)} collective-permute-done((bf16[1024,1024]{1,0:T(8,128)(2,1)}, bf16[1024,1024]{1,0:T(8,128)(2,1)S(1)}, u32[]{:S(2)}, u32[]{:S(2)}) %collective-permute-start.47) | collective-permute-done | bytes 2097184 | tf_op jit(solution)/shard_map/ppermute | solution.py:723
  771.6 5.2 convolution_convert_fusion.2
  776.8 12.6 %collective-permute-done.52.refs_2_ = bf16[256,1408]{1,0:T(8,128)(2,1)} collective-permute-done((bf16[256,1408]{1,0:T(8,128)(2,1)}, bf16[256,1408]{1,0:T(8,128)(2,1)}, u32[]{:S(2)}, u32[]{:S(2)}) %collective-permute-start.52) | collective-permute-done | bytes 720928 | tf_op jit(solution)/shard_map/ppermute | solution.py:432
  790.4 28.5 %collective-permute-done.48 = bf16[1024,1152]{1,0:T(8,128)(2,1)} collective-permute-done((bf16[1024,1152]{1,0:T(8,128)(2,1)}, bf16[1024,1152]{1,0:T(8,128)(2,1)}, u32[]{:S(2)}, u32[]{:S(2)}) %collective-permute-start.48) | collective-permute-done | bytes 2359328 | tf_op jit(solution)/shard_map/ppermute | solution.py:723
  818.9 3.7 add_convert_fusion.3
  823.2 7.2 unhide.2
  833.5 12.8 %collective-permute-done.55 = bf16[176,2048]{1,0:T(8,128)(2,1)} collective-permute-done((bf16[176,2048]{1,0:T(8,128)(2,1)}, bf16[176,2048]{1,0:T(8,128)(2,1)}, u32[]{:S(2)}, u32[]{:S(2)}) %collective-permute-start.55) | collective-permute-done | bytes 720928 | tf_op jit(solution)/shard_map/ppermute | solution.py:432
  855.0 7.1 unhide.3
  866.2 3.6 collective-permute-done.59.refs_2_
  880.8 4.1 collective-permute-done.64
  888.8 3.9 fusion.13
  894.0 4.2 finish.3
  898.3 5.1 finish.4
  906.3 13.3 %collective-permute-done.70.refs_2_ = bf16[256,1152]{1,0:T(8,128)(2,1)} collective-permute-done((bf16[256,1152]{1,0:T(8,128)(2,1)}, bf16[256,1152]{1,0:T(8,128)(2,1)}, u32[]{:S(2)}, u32[]{:S(2)}) %collective-permute-start.70) | collective-permute-done | bytes 589856 | tf_op jit(solution)/shard_map/ppermute | solution.py:432
  929.3 5.0 finish.5
  (351 shorter events, 168.9 us)
Async XLA Ops:
  7.2 207.0 %all-gather.3.cloned.1.call-start = ((), (), s32[]{:S(2)}) async-start(), calls=%async_computation.6 | async-start | bytes 12386304 | tf_op jit(solution)/shard_map/all_gather | solution.py:464
  20.1 357.6 %all-gather.5.cloned.1.call-start = ((), (), s32[]{:S(2)}) async-start(), calls=%async_computation.7 | async-start | bytes 12976128 | tf_op jit(solution)/shard_map/all_gather | solution.py:464
  23.1 26.6 %collective-permute-start = (bf16[272,2048]{1,0:T(8,128)(2,1)}, bf16[272,2048]{1,0:T(8,128)(2,1)}, u32[]{:S(2)}, u32[]{:S(2)}) collective-permute-start(bf16[272,2048]{1,0:T(8,128)(2,1)} %fusion.20.refs_0_), channel_id=1, source_target_pairs={{0,16},{8,24},{16,0},{24,8},{1,17},{9,25},{17,1},{25,9},{2,18},{10... | collective-permute-start | bytes 3342344 | tf_op jit(solution)/shard_map/ppermute | solution.py:432
  25.2 24.6 %collective-permute-start.1 = (bf16[272,2048]{1,0:T(8,128)(2,1)}, bf16[272,2048]{1,0:T(8,128)(2,1)}, u32[]{:S(2)}, u32[]{:S(2)}) collective-permute-start(bf16[272,2048]{1,0:T(8,128)(2,1)} %fusion.20.refs_0_), channel_id=1, source_target_pairs={{0,8},{8,0},{16,24},{24,16},{1,9},{9,1},{17,25},{25,17},{2,10},{10... | collective-permute-start | bytes 3342344 | tf_op jit(solution)/shard_map/ppermute | solution.py:432
  27.1 32.6 %collective-permute-start.16 = (bf16[176,2048]{1,0:T(8,128)(2,1)}, bf16[176,2048]{1,0:T(8,128)(2,1)S(1)}, u32[]{:S(2)}, u32[]{:S(2)}) collective-permute-start(bf16[176,2048]{1,0:T(8,128)(2,1)} %constant_dynamic-slice_fusion.6.refs_13_.refs_2_), channel_id=1, source_target_pairs={{0,2},{1,3},{2,4},{3,5},{4,6},{5,7},{8,10},{9,11},{10,12},{11,13},... | collective-permute-start | bytes 2162696 | tf_op jit(solution)/shard_map/ppermute | solution.py:432
  30.3 50.2 %collective-permute-start.17 = (bf16[176,2048]{1,0:T(8,128)(2,1)}, bf16[176,2048]{1,0:T(8,128)(2,1)}, u32[]{:S(2)}, u32[]{:S(2)}) collective-permute-start(bf16[176,2048]{1,0:T(8,128)(2,1)} %constant_dynamic-slice_fusion.6.refs_13_.refs_2_), channel_id=1, source_target_pairs={{2,0},{3,1},{4,2},{5,3},{6,4},{7,5},{10,8},{11,9},{12,10},{13,11},... | collective-permute-start | bytes 2162696 | tf_op jit(solution)/shard_map/ppermute | solution.py:432
  31.6 50.1 %collective-permute-start.15 = (bf16[176,2048]{1,0:T(8,128)(2,1)}, bf16[176,2048]{1,0:T(8,128)(2,1)S(1)}, u32[]{:S(2)}, u32[]{:S(2)}) collective-permute-start(bf16[176,2048]{1,0:T(8,128)(2,1)} %constant_dynamic-slice_fusion.6.refs_13_.refs_2_), channel_id=1, source_target_pairs={{0,1},{1,0},{2,3},{3,2},{4,5},{5,4},{6,7},{7,6},{8,9},{9,8},{10,11... | collective-permute-start | bytes 2162696 | tf_op jit(solution)/shard_map/ppermute | solution.py:432
  49.8 36.2 %collective-permute-start.2 = (bf16[272,2048]{1,0:T(8,128)(2,1)}, bf16[272,2048]{1,0:T(8,128)(2,1)S(1)}, u32[]{:S(2)}, u32[]{:S(2)}) collective-permute-start(bf16[272,2048]{1,0:T(8,128)(2,1)} %collective-permute-done.refs_0_), channel_id=1, source_target_pairs={{0,8},{8,0},{16,24},{24,16},{1,9},{9,1},{17,25},{25,17},{2,10},{10... | collective-permute-start | bytes 3342344 | tf_op jit(solution)/shard_map/ppermute | solution.py:432
  81.7 16.3 %collective-permute-start.18 = (bf16[176,2048]{1,0:T(8,128)(2,1)S(1)}, bf16[176,2048]{1,0:T(8,128)(2,1)S(1)}, u32[]{:S(2)}, u32[]{:S(2)}) collective-permute-start(bf16[176,2048]{1,0:T(8,128)(2,1)S(1)} %broadcast_select_fusion.9.refs_15_.refs_4_), channel_id=1, source_target_pairs={{0,1},{1,0},{2,3},{3,2},{4,5},{5,4},{6,7},{7,6},{8,9},{9,8},{10,11... | collective-permute-start | bytes 2162696 | tf_op jit(solution)/shard_map/ppermute | solution.py:432
  82.9 34.8 %collective-permute-start.19 = (bf16[176,2048]{1,0:T(8,128)(2,1)S(1)}, bf16[176,2048]{1,0:T(8,128)(2,1)}, u32[]{:S(2)}, u32[]{:S(2)}) collective-permute-start(bf16[176,2048]{1,0:T(8,128)(2,1)S(1)} %collective-permute-done.16), channel_id=1, source_target_pairs={{2,4},{3,5},{4,6},{5,7},{10,12},{11,13},{12,14},{13,15},{18,20},{1... | collective-permute-start | bytes 2162696 | tf_op jit(solution)/shard_map/ppermute | solution.py:432
  84.5 32.0 %collective-permute-start.20 = (bf16[176,2048]{1,0:T(8,128)(2,1)}, bf16[176,2048]{1,0:T(8,128)(2,1)}, u32[]{:S(2)}, u32[]{:S(2)}) collective-permute-start(bf16[176,2048]{1,0:T(8,128)(2,1)} %collective-permute-done.17), channel_id=1, source_target_pairs={{2,0},{3,1},{4,2},{5,3},{10,8},{11,9},{12,10},{13,11},{18,16},{19,... | collective-permute-start | bytes 2162696 | tf_op jit(solution)/shard_map/ppermute | solution.py:432
  85.9 35.6 %collective-permute-start.3 = (bf16[256,2048]{1,0:T(8,128)(2,1)S(1)}, bf16[256,2048]{1,0:T(8,128)(2,1)}, u32[]{:S(2)}, u32[]{:S(2)}) collective-permute-start(bf16[256,2048]{1,0:T(8,128)(2,1)S(1)} %broadcast_multiply_fusion.refs_8_), channel_id=1, source_target_pairs={{0,16},{8,24},{16,0},{24,8},{1,17},{9,25},{17,1},{25,9},{2,18},{10... | collective-permute-start | bytes 3145736 | tf_op jit(solution)/shard_map/ppermute | solution.py:432
  86.0 35.5 %collective-permute-start.4 = (bf16[256,2048]{1,0:T(8,128)(2,1)S(1)}, bf16[256,2048]{1,0:T(8,128)(2,1)}, u32[]{:S(2)}, u32[]{:S(2)}) collective-permute-start(bf16[256,2048]{1,0:T(8,128)(2,1)S(1)} %broadcast_multiply_fusion.refs_8_), channel_id=1, source_target_pairs={{0,8},{8,0},{16,24},{24,16},{1,9},{9,1},{17,25},{25,17},{2,10},{10... | collective-permute-start | bytes 3145736 | tf_op jit(solution)/shard_map/ppermute | solution.py:432
  116.4 67.8 %collective-permute-start.22 = (bf16[176,2048]{1,0:T(8,128)(2,1)}, bf16[176,2048]{1,0:T(8,128)(2,1)}, u32[]{:S(2)}, u32[]{:S(2)}) collective-permute-start(bf16[176,2048]{1,0:T(8,128)(2,1)} %collective-permute-done.20), channel_id=1, source_target_pairs={{2,0},{3,1},{10,8},{11,9},{18,16},{19,17},{26,24},{27,25}} | collective-permute-start | bytes 2162696 | tf_op jit(solution)/shard_map/ppermute | solution.py:432
  117.7 66.4 %collective-permute-start.23 = (bf16[176,2048]{1,0:T(8,128)(2,1)}, bf16[176,2048]{1,0:T(8,128)(2,1)}, u32[]{:S(2)}, u32[]{:S(2)}) collective-permute-start(bf16[176,2048]{1,0:T(8,128)(2,1)} %collective-permute-done.19), channel_id=1, source_target_pairs={{4,6},{5,7},{12,14},{13,15},{20,22},{21,23},{28,30},{29,31}} | collective-permute-start | bytes 2162696 | tf_op jit(solution)/shard_map/ppermute | solution.py:432
  120.5 64.9 %collective-permute-start.21 = (bf16[176,2048]{1,0:T(8,128)(2,1)S(1)}, bf16[176,2048]{1,0:T(8,128)(2,1)}, u32[]{:S(2)}, u32[]{:S(2)}) collective-permute-start(bf16[176,2048]{1,0:T(8,128)(2,1)S(1)} %broadcast_select_fusion.8.refs_17_.refs_6_), channel_id=1, source_target_pairs={{0,1},{1,0},{2,3},{3,2},{4,5},{5,4},{6,7},{7,6},{8,9},{9,8},{10,11... | collective-permute-start | bytes 2162696 | tf_op jit(solution)/shard_map/ppermute | solution.py:432
  121.5 79.2 %collective-permute-start.5 = (bf16[256,2048]{1,0:T(8,128)(2,1)}, bf16[256,2048]{1,0:T(8,128)(2,1)}, u32[]{:S(2)}, u32[]{:S(2)}) collective-permute-start(bf16[256,2048]{1,0:T(8,128)(2,1)} %collective-permute-done.3.refs_10_), channel_id=1, source_target_pairs={{0,8},{8,0},{16,24},{24,16},{1,9},{9,1},{17,25},{25,17},{2,10},{10... | collective-permute-start | bytes 3145736 | tf_op jit(solution)/shard_map/ppermute | solution.py:432
  185.4 15.3 %collective-permute-start.24 = (bf16[176,2048]{1,0:T(8,128)(2,1)S(1)}, bf16[176,2048]{1,0:T(8,128)(2,1)}, u32[]{:S(2)}, u32[]{:S(2)}) collective-permute-start(bf16[176,2048]{1,0:T(8,128)(2,1)S(1)} %select_select_fusion.refs_19_.refs_8_), channel_id=1, source_target_pairs={{0,1},{1,0},{2,3},{3,2},{4,5},{5,4},{6,7},{7,6},{8,9},{9,8},{10,11... | collective-permute-start | bytes 2162696 | tf_op jit(solution)/shard_map/ppermute | solution.py:432
  214.2 457.8 %reduce-scatter.7.cloned.1.call-start = ((), (), s32[]{:S(2)}) async-start(), calls=%async_computation.8 | async-start | bytes 3604480 | tf_op jit(solution)/shard_map/reduce_scatter | solution.py:478
  276.9 24.8 %collective-permute-start.7 = (bf16[1024,512]{1,0:T(8,128)(2,1)S(1)}, bf16[1024,512]{1,0:T(8,128)(2,1)S(1)}, u32[]{:S(2)}, u32[]{:S(2)}) collective-permute-start(bf16[1024,512]{1,0:T(8,128)(2,1)S(1)} %get-tuple-element.194.refs_0_), channel_id=1, source_target_pairs={{0,16},{8,24},{16,0},{24,8},{1,17},{9,25},{17,1},{25,9},{2,18},{10... | collective-permute-start | bytes 3145736 | tf_op jit(solution)/shard_map/ppermute | solution.py:432
  320.4 24.9 %collective-permute-start.13 = (bf16[1024,512]{1,0:T(8,128)(2,1)}, bf16[1024,512]{1,0:T(8,128)(2,1)S(1)}, u32[]{:S(2)}, u32[]{:S(2)}) collective-permute-start(bf16[1024,512]{1,0:T(8,128)(2,1)} %get-tuple-element.203.refs_0_), channel_id=1, source_target_pairs={{0,16},{8,24},{16,0},{24,8},{1,17},{9,25},{17,1},{25,9},{2,18},{10... | collective-permute-start | bytes 3145736 | tf_op jit(solution)/shard_map/ppermute | solution.py:432
  321.3 24.1 %collective-permute-start.12 = (bf16[1024,512]{1,0:T(8,128)(2,1)}, bf16[1024,512]{1,0:T(8,128)(2,1)}, u32[]{:S(2)}, u32[]{:S(2)}) collective-permute-start(bf16[1024,512]{1,0:T(8,128)(2,1)} %get-tuple-element.203.refs_0_), channel_id=1, source_target_pairs={{0,8},{8,0},{16,24},{24,16},{1,9},{9,1},{17,25},{25,17},{2,10},{10... | collective-permute-start | bytes 3145736 | tf_op jit(solution)/shard_map/ppermute | solution.py:432
  416.7 29.0 %collective-permute-start.27 = (f32[4,1,256]{2,1,0:T(1,128)S(1)}, f32[4,1,256]{2,1,0:T(1,128)S(1)}, u32[]{:S(2)}, u32[]{:S(2)}) collective-permute-start(f32[4,1,256]{2,1,0:T(1,128)S(1)} %collective-permute-done.25.refs_12_), channel_id=1, source_target_pairs={{0,8},{8,0},{16,24},{24,16},{1,9},{9,1},{17,25},{25,17},{2,10},{10... | collective-permute-start | bytes 12296 | tf_op jit(solution)/shard_map/ppermute | solution.py:432
  445.9 64.2 %collective-permute-start.37 = (bf16[1024,1408]{1,0:T(8,128)(2,1)}, bf16[1024,1408]{1,0:T(8,128)(2,1)}, u32[]{:S(2)}, u32[]{:S(2)}) collective-permute-start(bf16[1024,1408]{1,0:T(8,128)(2,1)} %convolution_convert_fusion.6), channel_id=1, source_target_pairs={{0,1},{1,0},{2,3},{3,2},{4,5},{5,4},{6,7},{7,6},{8,9},{9,8},{10,11... | collective-permute-start | bytes 8650760 | tf_op jit(solution)/shard_map/ppermute | solution.py:723
  448.7 18.8 %collective-permute-start.29 = (bf16[1024,512]{1,0:T(8,128)(2,1)}, bf16[1024,512]{1,0:T(8,128)(2,1)S(1)}, u32[]{:S(2)}, u32[]{:S(2)}) collective-permute-start(bf16[1024,512]{1,0:T(8,128)(2,1)} %get-tuple-element.229), channel_id=1, source_target_pairs={{0,8},{8,0},{16,24},{24,16},{1,9},{9,1},{17,25},{25,17},{2,10},{10... | collective-permute-start | bytes 3145736 | tf_op jit(solution)/shard_map/ppermute | solution.py:432
  450.5 24.5 %collective-permute-start.30 = (bf16[1024,512]{1,0:T(8,128)(2,1)S(1)}, bf16[1024,512]{1,0:T(8,128)(2,1)S(1)}, u32[]{:S(2)}, u32[]{:S(2)}) collective-permute-start(bf16[1024,512]{1,0:T(8,128)(2,1)S(1)} %add_convert_fusion.9), channel_id=1, source_target_pairs={{0,16},{8,24},{16,0},{24,8},{1,17},{9,25},{17,1},{25,9},{2,18},{10... | collective-permute-start | bytes 3145736 | tf_op jit(solution)/shard_map/ppermute | solution.py:432
  485.1 7.8 collective-permute-start.31
  514.2 254.7 %reduce-scatter.11.cloned.1.call-start = ((), (), s32[]{:S(2)}) async-start(), calls=%async_computation.10 | async-start | bytes 3604480 | tf_op jit(solution)/shard_map/reduce_scatter | solution.py:478
  514.7 63.2 %collective-permute-start.49 = (bf16[1024,1408]{1,0:T(8,128)(2,1)}, bf16[1024,1408]{1,0:T(8,128)(2,1)S(1)}, u32[]{:S(2)}, u32[]{:S(2)}) collective-permute-start(bf16[1024,1408]{1,0:T(8,128)(2,1)} %convolution_convert_fusion.5), channel_id=1, source_target_pairs={{0,1},{1,0},{2,3},{3,2},{4,5},{5,4},{6,7},{7,6},{8,9},{9,8},{10,11... | collective-permute-start | bytes 8650760 | tf_op jit(solution)/shard_map/ppermute | solution.py:723
  515.0 8.9 collective-permute-start.32
  516.4 25.1 %collective-permute-start.34 = (bf16[1024,512]{1,0:T(8,128)(2,1)}, bf16[1024,512]{1,0:T(8,128)(2,1)S(1)}, u32[]{:S(2)}, u32[]{:S(2)}) collective-permute-start(bf16[1024,512]{1,0:T(8,128)(2,1)} %add_convert_fusion.8), channel_id=1, source_target_pairs={{0,16},{8,24},{16,0},{24,8},{1,17},{9,25},{17,1},{25,9},{2,18},{10... | collective-permute-start | bytes 3145736 | tf_op jit(solution)/shard_map/ppermute | solution.py:432
  580.3 250.1 %reduce-scatter.13.cloned.1.call-start = ((), (), s32[]{:S(2)}) async-start(), calls=%async_computation.11 | async-start | bytes 3604480 | tf_op jit(solution)/shard_map/reduce_scatter | solution.py:478
  580.6 5.7 collective-permute-start.33
  585.9 64.1 %collective-permute-start.54 = (bf16[704,2048]{1,0:T(8,128)(2,1)S(1)}, bf16[704,2048]{1,0:T(8,128)(2,1)S(1)}, u32[]{:S(2)}, u32[]{:S(2)}) collective-permute-start(bf16[704,2048]{1,0:T(8,128)(2,1)S(1)} %bitcast.95), channel_id=1, source_target_pairs={{0,1},{1,0},{2,3},{3,2},{4,5},{5,4},{6,7},{7,6},{8,9},{9,8},{10,11... | collective-permute-start | bytes 8650760 | tf_op jit(solution)/shard_map/ppermute | solution.py:723
  588.4 24.8 %collective-permute-start.35 = (bf16[256,2048]{1,0:T(8,128)(2,1)S(1)}, bf16[256,2048]{1,0:T(8,128)(2,1)S(1)}, u32[]{:S(2)}, u32[]{:S(2)}) collective-permute-start(bf16[256,2048]{1,0:T(8,128)(2,1)S(1)} %add_convert_fusion.7), channel_id=1, source_target_pairs={{0,16},{8,24},{16,0},{24,8},{1,17},{9,25},{17,1},{25,9},{2,18},{10... | collective-permute-start | bytes 3145736 | tf_op jit(solution)/shard_map/ppermute | solution.py:432
  652.9 209.1 %reduce-scatter.15.cloned.1.call-start = ((), (), s32[]{:S(2)}) async-start(), calls=%async_computation.12 | async-start | bytes 1310720 | tf_op jit(solution)/shard_map/reduce_scatter | solution.py:478
  653.0 11.1 %collective-permute-start.41 = (bf16[256,2048]{1,0:T(8,128)(2,1)}, bf16[256,2048]{1,0:T(8,128)(2,1)S(1)}, u32[]{:S(2)}, u32[]{:S(2)}) collective-permute-start(bf16[256,2048]{1,0:T(8,128)(2,1)} %get-tuple-element.282), channel_id=1, source_target_pairs={{0,8},{8,0},{16,24},{24,16},{1,9},{9,1},{17,25},{25,17},{2,10},{10... | collective-permute-start | bytes 3145736 | tf_op jit(solution)/shard_map/ppermute | solution.py:432
  654.2 7.2 collective-permute-start.38
  661.3 9.9 %collective-permute-start.39 = (bf16[256,512]{1,0:T(8,128)(2,1)S(1)}, bf16[256,512]{1,0:T(8,128)(2,1)S(1)}, u32[]{:S(2)}, u32[]{:S(2)}) collective-permute-start(bf16[256,512]{1,0:T(8,128)(2,1)S(1)} %get-tuple-element.280), channel_id=1, source_target_pairs={{0,24},{8,16},{16,8},{24,0},{1,25},{9,17},{17,9},{25,1},{2,26},{10... | collective-permute-start | bytes 786440 | tf_op jit(solution)/shard_map/ppermute | solution.py:432
  664.0 8.0 collective-permute-start.42
  672.0 17.8 %collective-permute-start.40 = (bf16[256,1408]{1,0:T(8,128)(2,1)}, bf16[256,1408]{1,0:T(8,128)(2,1)S(1)}, u32[]{:S(2)}, u32[]{:S(2)}) collective-permute-start(bf16[256,1408]{1,0:T(8,128)(2,1)} %reduce-scatter.7.cloned.1.call-done.refs_0_), channel_id=1, source_target_pairs={{0,16},{8,24},{16,0},{24,8},{1,17},{9,25},{17,1},{25,9},{2,18},{10... | collective-permute-start | bytes 2162696 | tf_op jit(solution)/shard_map/ppermute | solution.py:432
  672.0 17.7 %collective-permute-start.43 = (bf16[256,1408]{1,0:T(8,128)(2,1)}, bf16[256,1408]{1,0:T(8,128)(2,1)}, u32[]{:S(2)}, u32[]{:S(2)}) collective-permute-start(bf16[256,1408]{1,0:T(8,128)(2,1)} %reduce-scatter.7.cloned.1.call-done.refs_0_), channel_id=1, source_target_pairs={{0,8},{8,0},{16,24},{24,16},{1,9},{9,1},{17,25},{25,17},{2,10},{10... | collective-permute-start | bytes 2162696 | tf_op jit(solution)/shard_map/ppermute | solution.py:432
  689.7 24.0 %collective-permute-start.44 = (bf16[256,1408]{1,0:T(8,128)(2,1)S(1)}, bf16[256,1408]{1,0:T(8,128)(2,1)S(1)}, u32[]{:S(2)}, u32[]{:S(2)}) collective-permute-start(bf16[256,1408]{1,0:T(8,128)(2,1)S(1)} %collective-permute-done.40.refs_2_), channel_id=1, source_target_pairs={{0,8},{8,0},{16,24},{24,16},{1,9},{9,1},{17,25},{25,17},{2,10},{10... | collective-permute-start | bytes 2162696 | tf_op jit(solution)/shard_map/ppermute | solution.py:432
  694.6 24.8 %collective-permute-start.36 = (bf16[1024,512]{1,0:T(8,128)(2,1)}, bf16[1024,512]{1,0:T(8,128)(2,1)S(1)}, u32[]{:S(2)}, u32[]{:S(2)}) collective-permute-start(bf16[1024,512]{1,0:T(8,128)(2,1)} %convolution_convert_fusion.9), channel_id=1, source_target_pairs={{0,1},{1,0},{2,3},{3,2},{4,5},{5,4},{6,7},{7,6},{8,9},{9,8},{10,11... | collective-permute-start | bytes 3145736 | tf_op jit(solution)/shard_map/ppermute | solution.py:723
  713.8 6.9 collective-permute-start.45
  714.3 50.0 %collective-permute-start.47 = (bf16[1024,1024]{1,0:T(8,128)(2,1)}, bf16[1024,1024]{1,0:T(8,128)(2,1)S(1)}, u32[]{:S(2)}, u32[]{:S(2)}) collective-permute-start(bf16[1024,1024]{1,0:T(8,128)(2,1)} %convolution_convert_fusion.7), channel_id=1, source_target_pairs={{0,1},{1,0},{2,3},{3,2},{4,5},{5,4},{6,7},{7,6},{8,9},{9,8},{10,11... | collective-permute-start | bytes 6291464 | tf_op jit(solution)/shard_map/ppermute | solution.py:723
  720.7 153.3 %reduce-scatter.17.cloned.1.call-start = ((), (), s32[]{:S(2)}) async-start(), calls=%async_computation.13 | async-start | bytes 2621440 | tf_op jit(solution)/shard_map/reduce_scatter | solution.py:478
  722.5 23.1 %collective-permute-start.46 = (bf16[256,2048]{1,0:T(8,128)(2,1)S(1)}, bf16[256,2048]{1,0:T(8,128)(2,1)S(1)}, u32[]{:S(2)}, u32[]{:S(2)}) collective-permute-start(bf16[256,2048]{1,0:T(8,128)(2,1)S(1)} %add_convert_fusion.5), channel_id=1, source_target_pairs={{0,16},{8,24},{16,0},{24,8},{1,17},{9,25},{17,1},{25,9},{2,18},{10... | collective-permute-start | bytes 3145736 | tf_op jit(solution)/shard_map/ppermute | solution.py:432
  766.6 136.7 %reduce-scatter.9.cloned.1.call-start = ((), (), s32[]{:S(2)}) async-start(), calls=%async_computation.9 | async-start | bytes 2949120 | tf_op jit(solution)/shard_map/reduce_scatter | solution.py:478
  766.9 52.0 %collective-permute-start.48 = (bf16[1024,1152]{1,0:T(8,128)(2,1)}, bf16[1024,1152]{1,0:T(8,128)(2,1)}, u32[]{:S(2)}, u32[]{:S(2)}) collective-permute-start(bf16[1024,1152]{1,0:T(8,128)(2,1)} %convolution_convert_fusion.1), channel_id=1, source_target_pairs={{0,1},{1,0},{2,3},{3,2},{4,5},{5,4},{6,7},{7,6},{8,9},{9,8},{10,11... | collective-permute-start | bytes 7077896 | tf_op jit(solution)/shard_map/ppermute | solution.py:723
  771.2 5.6 collective-permute-start.51
  771.6 17.9 %collective-permute-start.52 = (bf16[256,1408]{1,0:T(8,128)(2,1)}, bf16[256,1408]{1,0:T(8,128)(2,1)}, u32[]{:S(2)}, u32[]{:S(2)}) collective-permute-start(bf16[256,1408]{1,0:T(8,128)(2,1)} %reduce-scatter.11.cloned.1.call-done.refs_0_), channel_id=1, source_target_pairs={{0,16},{8,24},{16,0},{24,8},{1,17},{9,25},{17,1},{25,9},{2,18},{10... | collective-permute-start | bytes 2162696 | tf_op jit(solution)/shard_map/ppermute | solution.py:432
  789.5 41.0 %collective-permute-start.53 = (bf16[256,1408]{1,0:T(8,128)(2,1)}, bf16[256,1408]{1,0:T(8,128)(2,1)}, u32[]{:S(2)}, u32[]{:S(2)}) collective-permute-start(bf16[256,1408]{1,0:T(8,128)(2,1)} %collective-permute-done.52.refs_2_), channel_id=1, source_target_pairs={{0,8},{8,0},{16,24},{24,16},{1,9},{9,1},{17,25},{25,17},{2,10},{10... | collective-permute-start | bytes 2162696 | tf_op jit(solution)/shard_map/ppermute | solution.py:432
  830.4 15.9 %collective-permute-start.55 = (bf16[176,2048]{1,0:T(8,128)(2,1)}, bf16[176,2048]{1,0:T(8,128)(2,1)}, u32[]{:S(2)}, u32[]{:S(2)}) collective-permute-start(bf16[176,2048]{1,0:T(8,128)(2,1)} %reduce-scatter.13.cloned.1.call-done), channel_id=1, source_target_pairs={{0,16},{8,24},{16,0},{24,8},{1,17},{9,25},{17,1},{25,9},{2,18},{10... | collective-permute-start | bytes 2162696 | tf_op jit(solution)/shard_map/ppermute | solution.py:432
  830.5 15.9 %collective-permute-start.56 = (bf16[176,2048]{1,0:T(8,128)(2,1)}, bf16[176,2048]{1,0:T(8,128)(2,1)}, u32[]{:S(2)}, u32[]{:S(2)}) collective-permute-start(bf16[176,2048]{1,0:T(8,128)(2,1)} %reduce-scatter.13.cloned.1.call-done), channel_id=1, source_target_pairs={{0,8},{8,0},{16,24},{24,16},{1,9},{9,1},{17,25},{25,17},{2,10},{10... | collective-permute-start | bytes 2162696 | tf_op jit(solution)/shard_map/ppermute | solution.py:432
  846.4 17.1 %collective-permute-start.57 = (bf16[176,2048]{1,0:T(8,128)(2,1)}, bf16[176,2048]{1,0:T(8,128)(2,1)}, u32[]{:S(2)}, u32[]{:S(2)}) collective-permute-start(bf16[176,2048]{1,0:T(8,128)(2,1)} %collective-permute-done.55), channel_id=1, source_target_pairs={{0,8},{8,0},{16,24},{24,16},{1,9},{9,1},{17,25},{25,17},{2,10},{10... | collective-permute-start | bytes 2162696 | tf_op jit(solution)/shard_map/ppermute | solution.py:432
  854.9 20.6 %collective-permute-start.62 = (f32[232,128]{1,0:T(8,128)}, f32[232,128]{1,0:T(8,128)}, u32[]{:S(2)}, u32[]{:S(2)}) collective-permute-start(f32[232,128]{1,0:T(8,128)} %fusion.23), channel_id=1, source_target_pairs={{0,16},{8,24},{16,0},{24,8},{1,17},{9,25},{17,1},{25,9},{2,18},{10... | collective-permute-start | bytes 356360 | tf_op jit(solution)/shard_map/ppermute | solution.py:897
  862.0 7.8 collective-permute-start.59
  863.5 6.3 collective-permute-start.58
  874.0 12.3 %collective-permute-start.66 = (bf16[256,1024]{1,0:T(8,128)(2,1)}, bf16[256,1024]{1,0:T(8,128)(2,1)}, u32[]{:S(2)}, u32[]{:S(2)}) collective-permute-start(bf16[256,1024]{1,0:T(8,128)(2,1)} %reduce-scatter.17.cloned.1.call-done.refs_0_), channel_id=1, source_target_pairs={{0,8},{8,0},{16,24},{24,16},{1,9},{9,1},{17,25},{25,17},{2,10},{10... | collective-permute-start | bytes 1572872 | tf_op jit(solution)/shard_map/ppermute | solution.py:432
  874.1 13.4 %collective-permute-start.67 = (bf16[256,1024]{1,0:T(8,128)(2,1)}, bf16[256,1024]{1,0:T(8,128)(2,1)}, u32[]{:S(2)}, u32[]{:S(2)}) collective-permute-start(bf16[256,1024]{1,0:T(8,128)(2,1)} %reduce-scatter.17.cloned.1.call-done.refs_0_), channel_id=1, source_target_pairs={{0,16},{8,24},{16,0},{24,8},{1,17},{9,25},{17,1},{25,9},{2,18},{10... | collective-permute-start | bytes 1572872 | tf_op jit(solution)/shard_map/ppermute | solution.py:432
  884.9 7.8 collective-permute-start.65
  887.5 10.8 %collective-permute-start.68 = (bf16[256,1024]{1,0:T(8,128)(2,1)}, bf16[256,1024]{1,0:T(8,128)(2,1)}, u32[]{:S(2)}, u32[]{:S(2)}) collective-permute-start(bf16[256,1024]{1,0:T(8,128)(2,1)} %collective-permute-done.67.refs_2_), channel_id=1, source_target_pairs={{0,8},{8,0},{16,24},{24,16},{1,9},{9,1},{17,25},{25,17},{2,10},{10... | collective-permute-start | bytes 1572872 | tf_op jit(solution)/shard_map/ppermute | solution.py:432
  904.5 15.2 %collective-permute-start.70 = (bf16[256,1152]{1,0:T(8,128)(2,1)}, bf16[256,1152]{1,0:T(8,128)(2,1)}, u32[]{:S(2)}, u32[]{:S(2)}) collective-permute-start(bf16[256,1152]{1,0:T(8,128)(2,1)} %reduce-scatter.9.cloned.1.call-done.refs_0_), channel_id=1, source_target_pairs={{0,16},{8,24},{16,0},{24,8},{1,17},{9,25},{17,1},{25,9},{2,18},{10... | collective-permute-start | bytes 1769480 | tf_op jit(solution)/shard_map/ppermute | solution.py:432
  (78 other events, 1231.4 us)
Sparse Core Ops, SparseCore 0:
  20.3 193.8 all-gather.2
  216.9 160.7 all-gather.4
  514.3 54.5 reduce-scatter.6
  580.4 55.4 reduce-scatter.10
  653.0 54.3 reduce-scatter.12
  720.8 25.3 reduce-scatter.14
  766.7 41.3 reduce-scatter.16
  822.7 46.4 reduce-scatter.8
